TPU v7x, 512 devices: a whole 4x8x8 slice. The times are simulated.
512 devices in a mesh: group: 16 (over y, core), ctx: 32 (over z, x).
Axes of the slice: x: 4, y: 8, z: 8, core: 2. Of those that a mesh axis runs over, the one named last changes fastest.
Arguments:
- queries: bfloat16 [65536, 1024], P(('group', 'ctx')), may hold values from -8 to 8
- keys: bfloat16 [65536, 1024], P(('group', 'ctx')), may hold values from -6 to 6
- values: bfloat16 [65536, 1024], P(('group', 'ctx')), may hold values from -6 to 6
- cotangent: bfloat16 [65536, 1024], P(('group', 'ctx')), may hold values from -192 to 192
Outputs:
- output: bfloat16 [65536, 1024], P(('group', 'ctx'))
- grad_queries: bfloat16 [65536, 1024], P(('group', 'ctx'))
- grad_keys: bfloat16 [65536, 1024], P(('group', 'ctx'))
- grad_values: bfloat16 [65536, 1024], P(('group', 'ctx'))
All inputs are finite; a program needn't handle non-finite values.
Results may differ from a plain program's by a relative error of at most 0.0096.
Values may be sent and summed in bfloat16 or wider, within the bound.
No kernel may reach another device: no remote copies, remote signals or barrier semaphores. Data moves between devices by JAX's collectives and lax.ppermute only.
A program may use at most 128 MiB of HBM per device.

v0:
```python
import math

import jax
import jax.numpy as jnp
from jax import lax
from jax.sharding import PartitionSpec as P

HEADS = 8
HEAD_DIM = 128
BLOCK = 128
COARSE_ONE = 16
COARSE_TWO = 16


def from_behind(value, axis, steps):
    count = lax.axis_size(axis)
    first, last = (max(0, -steps), min(count, count - steps))
    return lax.ppermute(value, axis, [(source, source + steps) for source in range(first, last)])


def attend(queries, cotangent, key_rows, value_rows, allowed):
    row_count = queries.shape[0]
    key_count = key_rows.shape[0]
    factor = HEAD_DIM ** (-0.5)
    query_h = queries.reshape(row_count, HEADS, HEAD_DIM)
    cot_h = cotangent.reshape(row_count, HEADS, HEAD_DIM)
    key_h = key_rows.reshape(key_count, HEADS, HEAD_DIM)
    value_h = value_rows.reshape(key_count, HEADS, HEAD_DIM)
    shutout = jnp.where(allowed, 0.0, -jnp.inf).astype(jnp.float32)
    scores = (
        jnp.einsum("rhd,nhd->hrn", query_h, key_h, preferred_element_type=jnp.float32) * factor
        + shutout[None]
    )
    highest = jnp.max(scores, axis=2, keepdims=True)
    weights = jnp.exp(scores - highest)
    chance = weights * (1.0 / jnp.sum(weights, axis=2, keepdims=True))
    chance_low = chance.astype(jnp.bfloat16)
    blended = jnp.einsum("hrn,nhd->rhd", chance_low, value_h, preferred_element_type=jnp.float32)
    output = blended.reshape(row_count, -1).astype(jnp.bfloat16)
    slopes = jnp.einsum("rhd,nhd->hrn", cot_h, value_h, preferred_element_type=jnp.float32)
    centre = jnp.sum(chance * slopes, axis=2, keepdims=True)
    dscore = (chance * (slopes - centre) * factor).astype(jnp.bfloat16)
    grad_q = jnp.einsum("hrn,nhd->rhd", dscore, key_h, preferred_element_type=jnp.float32)
    grad_q = grad_q.reshape(row_count, -1).astype(jnp.bfloat16)
    grad_k = jnp.einsum(
        "hrn,rhd->nhd", dscore, query_h, preferred_element_type=jnp.float32
    ).reshape(key_count, -1)
    grad_v = jnp.einsum(
        "hrn,rhd->nhd", chance_low, cot_h, preferred_element_type=jnp.float32
    ).reshape(key_count, -1)
    return (output, grad_q, grad_k, grad_v)


def key_mask(device, group_index, tok_rows, group_rows, level_rows, seq_total):
    query_pos = device * tok_rows + jnp.arange(tok_rows, dtype=jnp.int32)
    query_block = query_pos // BLOCK
    window_pos = device * tok_rows - BLOCK + jnp.arange(tok_rows + 2 * BLOCK, dtype=jnp.int32)
    inside = (window_pos >= 0) & (window_pos < seq_total)
    near_field = inside[None, :] & (
        jnp.abs(window_pos[None, :] // BLOCK - query_block[:, None]) <= 1
    )
    coarse_pos = group_index * group_rows + jnp.arange(group_rows, dtype=jnp.int32)
    coarse_block = coarse_pos * COARSE_ONE // BLOCK
    first_level = jnp.abs(coarse_block[None, :] - query_block[:, None]) > 1
    level_group = jnp.arange(level_rows, dtype=jnp.int32) // (group_rows // COARSE_TWO)
    second_level = jnp.broadcast_to((level_group != group_index)[None, :], (tok_rows, level_rows))
    return jnp.concatenate([near_field, first_level, second_level], axis=1)


def local(queries, keys, values, cotangent):
    tok_rows, features = queries.shape
    ctx_count = lax.axis_size("ctx")
    group_count = lax.axis_size("group")
    group_index = lax.axis_index("group")
    ctx_index = lax.axis_index("ctx")
    device = group_index * ctx_count + ctx_index
    key_value = jnp.stack([keys, values])
    below_rim = from_behind(key_value, ("group", "ctx"), 1)
    above_rim = from_behind(key_value, ("group", "ctx"), -1)
    window = jnp.concatenate([below_rim, key_value, above_rim], axis=1)
    own_one = jnp.sum(
        key_value.reshape(2, tok_rows // COARSE_ONE, COARSE_ONE, features),
        axis=2,
        dtype=jnp.float32,
    )
    own_one = (own_one / math.sqrt(COARSE_ONE)).astype(jnp.bfloat16)
    level_one = lax.all_gather(own_one, "ctx", axis=1, tiled=True)
    group_rows = level_one.shape[1]
    own_two = jnp.sum(
        level_one.reshape(2, group_rows // COARSE_TWO, COARSE_TWO, features),
        axis=2,
        dtype=jnp.float32,
    )
    own_two = (own_two / math.sqrt(COARSE_TWO)).astype(jnp.bfloat16)
    level_two = lax.all_gather(own_two, "group", axis=1, tiled=True)
    level_rows = level_two.shape[1]
    allkeys = jnp.concatenate([window, level_one, level_two], axis=1)
    allowed = key_mask(
        device, group_index, tok_rows, group_rows, level_rows, tok_rows * group_count * ctx_count
    )
    output, grad_q, grad_k, grad_v = attend(queries, cotangent, allkeys[0], allkeys[1], allowed)
    grads = jnp.stack([grad_k, grad_v])
    width = tok_rows + 2 * BLOCK
    fine_grad = grads[:, BLOCK : BLOCK + tok_rows]
    from_above = from_behind(grads[:, :BLOCK], ("group", "ctx"), -1)
    from_below = from_behind(grads[:, BLOCK + tok_rows : width], ("group", "ctx"), 1)
    fine_grad = fine_grad.at[:, tok_rows - BLOCK :].add(from_above)
    fine_grad = fine_grad.at[:, :BLOCK].add(from_below)
    part_one = grads[:, width : width + group_rows]
    part_two = grads[:, width + group_rows :]
    owned_rows = group_rows // ctx_count
    total_one = lax.psum(part_one, "ctx")
    total_two = lax.psum(part_two, ("group", "ctx"))
    rows_two = level_rows // group_count
    group_two = lax.dynamic_slice_in_dim(total_two, group_index * rows_two, rows_two, 1)
    carried = total_one + jnp.repeat(group_two, COARSE_TWO, axis=1) / math.sqrt(COARSE_TWO)
    owned = lax.dynamic_slice_in_dim(carried, ctx_index * owned_rows, owned_rows, 1)
    gradient = fine_grad + jnp.repeat(owned, COARSE_ONE, axis=1) / math.sqrt(COARSE_ONE)
    return (output, grad_q, gradient[0].astype(jnp.bfloat16), gradient[1].astype(jnp.bfloat16))


def solution(mesh):
    placed = (
        P(("group", "ctx"), None),
        P(("group", "ctx"), None),
        P(("group", "ctx"), None),
        P(("group", "ctx"), None),
    )
    return jax.shard_map(
        local,
        mesh=mesh,
        in_specs=placed,
        out_specs=(
            P(("group", "ctx"), None),
            P(("group", "ctx"), None),
            P(("group", "ctx"), None),
            P(("group", "ctx"), None),
        ),
        check_vma=False,
    )
```

profile of v0, /device:TPU:1, one launch (start us, length us, event | category | flops | bytes accessed | tf_op | source)
XLA Modules:
  0.0 654.9 jit_solution(7216936391135050496)
XLA Ops:
  7.2 1.3 convert_reduce_fusion.1
  8.5 0.6 multiply_convert_fusion.4
  9.2 0.0 all-gather.5.cloned.1.call-start
  9.2 85.8 %all-gather.3.cloned.1.call-done = bf16[2,256,1024]{2,1,0:T(8,128)(2,1)} async-done(((bf16[2,8,1024]{2,1,0:T(8,128)(2,1)}), bf16[2,256,1024]{2,1,0:T(8,128)(2,1)}) %all-gather.3.cloned.1.call-update) | async-done | bytes 1048592 | tf_op jit(solution)/shard_map/all_gather | solution.py:87
  95.1 1.7 convert_reduce_fusion
  96.8 0.6 multiply_convert_fusion.3
  97.5 1.1 pad_maximum_fusion.4
  98.6 2.2 collective-permute-start
  100.8 9.0 %collective-permute-start.1 = (bf16[2,128,1024]{2,1,0:T(8,128)(2,1)S(1)}, bf16[2,128,1024]{2,1,0:T(8,128)(2,1)S(1)}, u32[]{:S(2)}, u32[]{:S(2)}) collective-permute-start(bf16[2,128,1024]{2,1,0:T(8,128)(2,1)S(1)} %pad_maximum_fusion.4), channel_id=1, source_target_pairs={{1,0},{2,1},{3,2},{4,3},{5,4},{6,5},{7,6},{8,7},{9,8},{10,9},{11,1... | collective-permute-start | bytes 1572872 | tf_op jit(solution)/shard_map/ppermute | solution.py:18
  109.9 0.2 fusion.18
  110.1 0.1 abs_compare_fusion.1
  110.2 1.1 copy.61
  111.4 0.2 copy.62
  111.6 1.0 add_select_fusion
  112.5 2.4 collective-permute-done
  114.9 1.9 constant_dynamic-update-slice_fusion.4
  116.8 0.9 constant_dynamic-update-slice_fusion.3
  117.6 1.3 collective-permute-done.1
  118.9 0.8 constant_dynamic-update-slice_fusion.2
  119.8 1.1 constant_dynamic-update-slice_fusion.1
  120.9 20.0 %all-gather.5.cloned.1.call-done = bf16[2,256,1024]{2,1,0:T(8,128)(2,1)} async-done(((bf16[2,16,1024]{2,1,0:T(8,128)(2,1)}), bf16[2,256,1024]{2,1,0:T(8,128)(2,1)}) %all-gather.5.cloned.1.call-update) | async-done | bytes 1048592 | tf_op jit(solution)/shard_map/all_gather | solution.py:95
  140.9 2.3 constant_dynamic-update-slice_fusion
  143.2 3.7 fusion.38
  146.9 3.8 copy.39
  150.7 2.5 copy.40
  153.1 4.3 fusion.40
  157.4 3.3 fusion.39
  160.7 4.0 fusion.41
  164.8 6.6 %fusion.15 = f32[8,896,128]{1,2,0:T(8,128)} fusion(bf16[128,8,128]{0,2,1:T(8,128)(2,1)S(1)} %bitcast.111, f32[8,128]{1,0:T(8,128)S(1)} %broadcast_divide_fusion, f32[8,896,128]{2,1,0:T(8,128)} %fusion.40, f32[128,896]{0,1:T(8,128)S(1)} %copy-done.4), kind=kOutput, calls=%fused_computation.28 | convolution fusion | flops 241305472 | bytes 8065024 | tf_op jit(solution)/shard_map/hrn,rhd->nhd/dot_general | solution.py:48
  171.4 5.0 copy.52
  176.4 8.6 %fusion.7 = f32[8,896,128]{1,2,0:T(8,128)} fusion(bf16[128,8,128]{0,2,1:T(8,128)(2,1)S(1)} %bitcast.109, f32[8,896,128]{2,1,0:T(8,128)} %fusion.41, f32[8,128,896]{1,2,0:T(8,128)} %get-tuple-element.65, f32[8,128]{1,0:T(8,128)S(1)} %broadcast_divide_fusion), kind=kOutput, calls=%fused_computation.15 | convolution fusion | flops 241305472 | bytes 11276288 | tf_op jit(solution)/shard_map/hrn,rhd->nhd/dot_general | solution.py:45
  185.0 5.0 copy.51
  190.1 4.7 pad_maximum_fusion.1
  194.9 0.5 all-reduce.3.cloned.1.call-update
  195.4 3.1 pad_maximum_fusion.3
  198.5 3.1 collective-permute-start.3
  201.6 6.8 %collective-permute-start.2 = (f32[2,128,1024]{2,1,0:T(8,128)}, f32[2,128,1024]{2,1,0:T(8,128)}, u32[]{:S(2)}, u32[]{:S(2)}) collective-permute-start(f32[2,128,1024]{2,1,0:T(8,128)} %get-tuple-element.58), channel_id=1, source_target_pairs={{1,0},{2,1},{3,2},{4,3},{5,4},{6,5},{7,6},{8,7},{9,8},{10,9},{11,1... | collective-permute-start | bytes 3145736 | tf_op jit(solution)/shard_map/ppermute | solution.py:18
  208.4 6.2 convolution_convert_fusion
  214.6 1.8 copy.53
  216.4 6.8 %fusion.11 = bf16[8,128,128]{2,1,0:T(8,128)(2,1)S(1)} fusion(bf16[896,8,128]{0,2,1:T(8,128)(2,1)S(1)} %bitcast.95, f32[8,896,128]{2,1,0:T(8,128)} %fusion.41, f32[8,128,896]{1,2,0:T(8,128)} %get-tuple-element.65, f32[8,128]{1,0:T(8,128)S(1)} %broadcast_divide_fusion), kind=kOutput, calls=%fused_computation.20 | convolution fusion | flops 241436544 | bytes 9441280 | tf_op jit(solution)/shard_map/hrn,nhd->rhd/dot_general | solution.py:43
  223.1 0.9 copy.54
  224.0 258.9 %all-reduce.5.cloned.1.call-done = f32[2,256,1024]{2,1,0:T(8,128)} async-done(((f32[2,256,1024]{2,1,0:T(8,128)}), f32[2,256,1024]{2,1,0:T(8,128)}) %all-reduce.5.cloned.1.call-update) | async-done | bytes 2097168 | tf_op jit(solution)/shard_map/psum | solution.py:113
  482.9 0.9 dynamic-slice_multiply_fusion
  483.9 160.7 %all-reduce.3.cloned.1.call-done = f32[2,256,1024]{2,1,0:T(8,128)} async-done(((f32[2,256,1024]{2,1,0:T(8,128)}), f32[2,256,1024]{2,1,0:T(8,128)}) %all-reduce.3.cloned.1.call-update) | async-done | bytes 2097168 | tf_op jit(solution)/shard_map/psum | solution.py:112
  644.6 0.2 broadcast_in_dim.17
  644.9 0.9 fusion.19
  645.7 1.8 fusion.14
  647.6 0.8 slice_bitcast_fusion
  (27 shorter events, 0.3 us)
Async XLA Ops:
  7.2 109.6 %copy-start.2 = (bf16[128,1024]{1,0:T(8,128)(2,1)S(1)}, bf16[128,1024]{1,0:T(8,128)(2,1)}, u32[]{:S(2)}) copy-start(bf16[128,1024]{1,0:T(8,128)(2,1)} %param.14) | copy-start | bytes 786436
  7.2 109.6 %copy-start.3 = (bf16[128,1024]{1,0:T(8,128)(2,1)S(1)}, bf16[128,1024]{1,0:T(8,128)(2,1)}, u32[]{:S(2)}) copy-start(bf16[128,1024]{1,0:T(8,128)(2,1)} %param.13) | copy-start | bytes 786436
  7.2 104.2 %copy-start.5 = (bf16[128,1024]{1,0:T(8,128)(2,1)S(1)}, bf16[128,1024]{1,0:T(8,128)(2,1)}, u32[]{:S(2)}) copy-start(bf16[128,1024]{1,0:T(8,128)(2,1)} %param.15) | copy-start | bytes 786436
  7.2 87.9 %all-gather.3.cloned.1.call-start = ((), (), s32[]{:S(2)}) async-start(), calls=%async_computation | async-start | bytes 1081344 | tf_op jit(solution)/shard_map/all_gather | solution.py:87
  9.2 131.7 %all-gather.5.cloned.1.call-start = ((), (), s32[]{:S(2)}) async-start(), calls=%async_computation.1 | async-start | bytes 1114112 | tf_op jit(solution)/shard_map/all_gather | solution.py:95
  95.1 24.7 %copy-start.1 = (bf16[2,256,1024]{2,1,0:T(8,128)(2,1)S(1)}, bf16[2,256,1024]{2,1,0:T(8,128)(2,1)}, u32[]{:S(2)}) copy-start(bf16[2,256,1024]{2,1,0:T(8,128)(2,1)} %all-gather.3.cloned.1.call-done) | copy-start | bytes 3145732
  97.5 385.5 %all-reduce.5.cloned.1.call-start = ((), (), s32[]{:S(2)}) async-start(), calls=%async_computation.3 | async-start | bytes 4194304 | tf_op jit(solution)/shard_map/psum | solution.py:113
  98.6 16.3 %collective-permute-start = (bf16[2,128,1024]{2,1,0:T(8,128)(2,1)S(1)}, bf16[2,128,1024]{2,1,0:T(8,128)(2,1)}, u32[]{:S(2)}, u32[]{:S(2)}) collective-permute-start(bf16[2,128,1024]{2,1,0:T(8,128)(2,1)S(1)} %pad_maximum_fusion.4), channel_id=1, source_target_pairs={{0,1},{1,2},{2,3},{3,4},{4,5},{5,6},{6,7},{7,8},{8,9},{9,10},{10,1... | collective-permute-start | bytes 1572872 | tf_op jit(solution)/shard_map/ppermute | solution.py:18
  100.8 18.1 %collective-permute-start.1 = (bf16[2,128,1024]{2,1,0:T(8,128)(2,1)S(1)}, bf16[2,128,1024]{2,1,0:T(8,128)(2,1)S(1)}, u32[]{:S(2)}, u32[]{:S(2)}) collective-permute-start(bf16[2,128,1024]{2,1,0:T(8,128)(2,1)S(1)} %pad_maximum_fusion.4), channel_id=1, source_target_pairs={{1,0},{2,1},{3,2},{4,3},{5,4},{6,5},{7,6},{8,7},{9,8},{10,9},{11,1... | collective-permute-start | bytes 1572872 | tf_op jit(solution)/shard_map/ppermute | solution.py:18
  153.1 4.3 copy-start
  153.1 4.3 copy-start.4
  194.8 449.8 %all-reduce.3.cloned.1.call-start = ((), (), s32[]{:S(2)}) async-start(), calls=%async_computation.2 | async-start | bytes 4194304 | tf_op jit(solution)/shard_map/psum | solution.py:112
  198.5 447.2 %collective-permute-start.3 = (f32[2,128,1024]{2,1,0:T(8,128)}, f32[2,128,1024]{2,1,0:T(8,128)S(1)}, u32[]{:S(2)}, u32[]{:S(2)}) collective-permute-start(f32[2,128,1024]{2,1,0:T(8,128)} %get-tuple-element.59), channel_id=1, source_target_pairs={{0,1},{1,2},{2,3},{3,4},{4,5},{5,6},{6,7},{7,8},{8,9},{9,10},{10,1... | collective-permute-start | bytes 3145736 | tf_op jit(solution)/shard_map/ppermute | solution.py:18
  201.6 444.2 %collective-permute-start.2 = (f32[2,128,1024]{2,1,0:T(8,128)}, f32[2,128,1024]{2,1,0:T(8,128)}, u32[]{:S(2)}, u32[]{:S(2)}) collective-permute-start(f32[2,128,1024]{2,1,0:T(8,128)} %get-tuple-element.58), channel_id=1, source_target_pairs={{1,0},{2,1},{3,2},{4,3},{5,4},{6,5},{7,6},{8,7},{9,8},{10,9},{11,1... | collective-permute-start | bytes 3145736 | tf_op jit(solution)/shard_map/ppermute | solution.py:18
Sparse Core Ops, SparseCore 0:
  11.8 83.2 all-gather.2
  97.8 43.0 all-gather.4
  194.9 287.9 all-reduce.4
  486.7 157.8 all-reduce.2
where the time goes:
time: 659 us; the launch traced here: 655 us
  waiting for transfers between devices  530 us (80%)
  matrix products  39.8 us (6%)
  local copies, waits for them, and re-layouts  31.2 us (5%)
  starting transfers between devices  21.3 us (3%)
  other arithmetic  18.9 us (3%)
  between operations  14 us (2%)
    psum x1, waiting for transfers between devices, local(): total_two = lax.psum(part_two, ('group', 'ctx'))  259 us
    psum x1, waiting for transfers between devices, local(): total_one = lax.psum(part_one, 'ctx')  161 us
    all_gather x1, waiting for transfers between devices, local(): level_one = lax.all_gather(own_one, 'ctx', axis=1, tiled=True)  85.8 us
    ppermute x4, starting transfers between devices, from_behind(): lax.ppermute(value, axis, [(source, source + steps) for source in range(f...  21.1 us
    all_gather x1, waiting for transfers between devices, local(): level_two = lax.all_gather(own_two, 'group', axis=1, tiled=True)  20 us
  transfers between devices with their start and end apart: 8, of which 6 were waited for; matrix products, arithmetic and copies ran while one was open for 4% of the time, Pallas kernels for 0%

commit v1 on v0

v1 whole, which is shorter than its diff:
```python
import jax
import jax.numpy as jnp
from jax import lax
from jax.experimental import pallas as pl
from jax.experimental.pallas import tpu as pltpu
from jax.sharding import PartitionSpec as P

HEADS = 8
HEAD_DIM = 128
BLOCK = 128
COARSE = 16
ONE_ROWS = BLOCK // COARSE
N_CTX = 32
N_GROUP = 16
GROUP_ROWS = N_CTX * ONE_ROWS
TWO_ROWS = GROUP_ROWS // COARSE
LEVEL_TWO = N_GROUP * TWO_ROWS
FEATURES = HEADS * HEAD_DIM
FACTOR = HEAD_DIM ** (-0.5)
SHUT = -1e30
F32 = jnp.float32
BF16 = jnp.bfloat16
VMEM = pl.BlockSpec(memory_space=pltpu.VMEM)
SMEM = pl.BlockSpec(memory_space=pltpu.SMEM)


def shifted(value, steps):
    count = N_CTX * N_GROUP
    first, last = (max(0, -steps), min(count, count - steps))
    return lax.ppermute(value, ("group", "ctx"), [(s, s + steps) for s in range(first, last)])


def dot_nt(left, right):
    return lax.dot_general(left, right, (((1,), (1,)), ((), ())), preferred_element_type=F32)


def dot_nn(left, right):
    return lax.dot_general(left, right, (((1,), (0,)), ((), ())), preferred_element_type=F32)


def dot_tn(left, right):
    return lax.dot_general(left, right, (((0,), (0,)), ((), ())), preferred_element_type=F32)


def rows_of(shape, dim):
    return lax.broadcasted_iota(jnp.int32, shape, dim)


def coarsen_one_kernel(keys, values, spread):
    row, token = rows_of((2 * ONE_ROWS, BLOCK), 0), rows_of((2 * ONE_ROWS, BLOCK), 1)
    pick_k = jnp.where(row == token // COARSE, 1.0, 0.0).astype(BF16)
    pick_v = jnp.where(row - ONE_ROWS == token // COARSE, 1.0, 0.0).astype(BF16)
    own = (dot_nn(pick_k, keys[...]) + dot_nn(pick_v, values[...])) * 0.25
    own = own.astype(BF16)
    for copy in range(N_CTX):
        spread[copy] = own


def coarsen_two_kernel(level_one, spread):
    total = N_CTX * 2 * ONE_ROWS
    row, source = rows_of((2 * TWO_ROWS, total), 0), rows_of((2 * TWO_ROWS, total), 1)
    kind = (source % (2 * ONE_ROWS)) // ONE_ROWS
    pick = jnp.where(row == kind * TWO_ROWS + source // (4 * ONE_ROWS), 1.0, 0.0).astype(BF16)
    own = (dot_nn(pick, level_one[...].reshape(total, FEATURES)) * 0.25).astype(BF16)
    for copy in range(N_GROUP):
        spread[copy] = own


def split_one(block):
    wide = block.astype(F32)
    key = wide[:, :ONE_ROWS].reshape(GROUP_ROWS, HEAD_DIM).astype(BF16)
    value = wide[:, ONE_ROWS:].reshape(GROUP_ROWS, HEAD_DIM).astype(BF16)
    return key, value


def near_bias(place):
    group, ctx = place[0], place[1]
    device = group * N_CTX + ctx
    low = jnp.where(device == 0, SHUT, 0.0).astype(F32)
    high = jnp.where(device == N_CTX * N_GROUP - 1, SHUT, 0.0).astype(F32)
    shape = (BLOCK, HEAD_DIM)
    row = rows_of((GROUP_ROWS, HEAD_DIM), 0) // ONE_ROWS
    one = jnp.where(jnp.abs(row - ctx) <= 1, SHUT, 0.0).astype(F32)
    return [jnp.full(shape, low), jnp.zeros(shape, F32), jnp.full(shape, high), one]


def two_bias(place):
    row = rows_of((LEVEL_TWO, HEAD_DIM), 0) // TWO_ROWS
    return jnp.where(row == place[0], SHUT, 0.0).astype(F32)


def stats_kernel(place, queries, cotangent, keys, values, below, above, level_one, stats, bias):
    @pl.when(pl.program_id(0) == 0)
    def _():
        bias[...] = jnp.concatenate(near_bias(place), axis=0)

    one_k, one_v = split_one(level_one[...])
    all_k = jnp.concatenate([below[:BLOCK], keys[...], above[:BLOCK], one_k], axis=0)
    all_v = jnp.concatenate([below[BLOCK:], values[...], above[BLOCK:], one_v], axis=0)
    scores = dot_nt(all_k, queries[...]) * FACTOR + bias[...]
    highest = jnp.max(scores, axis=0, keepdims=True)
    weights = jnp.exp(scores - highest)
    slopes = dot_nt(all_v, cotangent[...])
    total = jnp.sum(weights, axis=0, keepdims=True)
    centre = jnp.sum(weights * slopes, axis=0, keepdims=True)
    stats[0, 0:1] = highest
    stats[0, 1:2] = total
    stats[0, 2:3] = centre


def two_kernel(place, queries, cotangent, level_two, near, stats, part_two):
    bias = two_bias(place)
    for head in range(HEADS):
        lanes = slice(head * HEAD_DIM, (head + 1) * HEAD_DIM)
        query, cot = queries[:, lanes], cotangent[:, lanes]
        key = level_two[:, :TWO_ROWS, lanes].reshape(LEVEL_TWO, HEAD_DIM)
        value = level_two[:, TWO_ROWS:, lanes].reshape(LEVEL_TWO, HEAD_DIM)
        scores = dot_nt(key, query) * FACTOR + bias
        slopes = dot_nt(value, cot)
        near_highest = near[head, 0:1]
        highest = jnp.maximum(near_highest, jnp.max(scores, axis=0, keepdims=True))
        scale = jnp.exp(near_highest - highest)
        weights = jnp.exp(scores - highest)
        total = near[head, 1:2] * scale + jnp.sum(weights, axis=0, keepdims=True)
        inverse = 1.0 / total
        centre = near[head, 2:3] * scale + jnp.sum(weights * slopes, axis=0, keepdims=True)
        centre = centre * inverse
        stats[head, 0:1] = highest
        stats[head, 1:2] = inverse
        stats[head, 2:3] = centre
        chance = weights * inverse
        dscore = (chance * (slopes - centre) * FACTOR).astype(BF16)
        grad_k = dot_nn(dscore, query).reshape(N_GROUP, TWO_ROWS, HEAD_DIM)
        grad_v = dot_nn(chance.astype(BF16), cot).reshape(N_GROUP, TWO_ROWS, HEAD_DIM)
        part_two[:, :, lanes] = jnp.concatenate([grad_k, grad_v], axis=1).astype(BF16)


def attend_kernel(
    place, queries, cotangent, keys, values, below, above, level_one, level_two, stats,
    output, grad_q, fine, grad_below, grad_above, part_one, bias,
):
    @pl.when(pl.program_id(0) == 0)
    def _():
        bias[...] = jnp.concatenate(near_bias(place) + [two_bias(place)], axis=0)

    query, cot = queries[...], cotangent[...]
    one_k, one_v = split_one(level_one[...])
    two_k = level_two[:, :TWO_ROWS].reshape(LEVEL_TWO, HEAD_DIM)
    two_v = level_two[:, TWO_ROWS:].reshape(LEVEL_TWO, HEAD_DIM)
    all_k = jnp.concatenate([below[:BLOCK], keys[...], above[:BLOCK], one_k, two_k], axis=0)
    all_v = jnp.concatenate([below[BLOCK:], values[...], above[BLOCK:], one_v, two_v], axis=0)
    scores = dot_nt(all_k, query) * FACTOR + bias[...]
    chance = jnp.exp(scores - stats[0, 0:1]) * stats[0, 1:2]
    slopes = dot_nt(all_v, cot)
    dscore = (chance * (slopes - stats[0, 2:3]) * FACTOR).astype(BF16)
    chance = chance.astype(BF16)
    output[...] = dot_tn(chance, all_v).astype(BF16)
    grad_q[...] = dot_tn(dscore, all_k).astype(BF16)
    seen = 3 * BLOCK + GROUP_ROWS
    grad_k = dot_nn(dscore[:seen], query)
    grad_v = dot_nn(chance[:seen], cot)
    grad_below[:BLOCK] = grad_k[:BLOCK].astype(BF16)
    grad_below[BLOCK:] = grad_v[:BLOCK].astype(BF16)
    fine[:BLOCK] = grad_k[BLOCK : 2 * BLOCK]
    fine[BLOCK:] = grad_v[BLOCK : 2 * BLOCK]
    grad_above[:BLOCK] = grad_k[2 * BLOCK : 3 * BLOCK].astype(BF16)
    grad_above[BLOCK:] = grad_v[2 * BLOCK : 3 * BLOCK].astype(BF16)
    one_k = grad_k[3 * BLOCK :].reshape(N_CTX, ONE_ROWS, HEAD_DIM)
    one_v = grad_v[3 * BLOCK :].reshape(N_CTX, ONE_ROWS, HEAD_DIM)
    part_one[...] = jnp.concatenate([one_k, one_v], axis=1)


def merge_kernel(part_one, arrived, merged):
    for head in range(HEADS):
        lanes = slice(head * HEAD_DIM, (head + 1) * HEAD_DIM)
        two = jnp.sum(arrived[:, :, lanes].astype(F32), axis=0) * 0.25
        for ctx in range(N_CTX):
            low, high = ctx // 2, TWO_ROWS + ctx // 2
            carried = jnp.concatenate(
                [
                    jnp.broadcast_to(two[low : low + 1], (ONE_ROWS, HEAD_DIM)),
                    jnp.broadcast_to(two[high : high + 1], (ONE_ROWS, HEAD_DIM)),
                ],
                axis=0,
            )
            merged[ctx, :, lanes] = (part_one[ctx, :, lanes] + carried).astype(BF16)


def finish_kernel(fine, from_below, from_above, arrived, grad_keys, grad_values):
    for head in range(HEADS):
        lanes = slice(head * HEAD_DIM, (head + 1) * HEAD_DIM)
        owned = jnp.sum(arrived[:, :, lanes].astype(F32), axis=0) * 0.25
        for first, out in ((0, grad_keys), (1, grad_values)):
            rows = slice(first * BLOCK, (first + 1) * BLOCK)
            total = fine[rows, lanes] + from_below[rows, lanes].astype(F32)
            total = total + from_above[rows, lanes].astype(F32)
            carried = owned[first * ONE_ROWS : (first + 1) * ONE_ROWS].reshape(ONE_ROWS, 1, HEAD_DIM)
            total = total.reshape(ONE_ROWS, COARSE, HEAD_DIM) + carried
            out[:, lanes] = total.reshape(BLOCK, HEAD_DIM).astype(BF16)


def shape_of(shape, dtype):
    return jax.ShapeDtypeStruct(shape, dtype)


def per_head(*shape):
    block = shape + (HEAD_DIM,)
    lead = (0,) * len(shape)
    return pl.BlockSpec(block, lambda head: lead + (head,))


def local(queries, keys, values, cotangent):
    group_index = lax.axis_index("group")
    ctx_index = lax.axis_index("ctx")
    place = jnp.stack([group_index, ctx_index]).astype(jnp.int32)
    one_shape = (N_CTX, 2 * ONE_ROWS, FEATURES)
    two_shape = (N_GROUP, 2 * TWO_ROWS, FEATURES)

    spread_one = pl.pallas_call(
        coarsen_one_kernel,
        out_shape=shape_of(one_shape, BF16),
        in_specs=[VMEM] * 2,
        out_specs=VMEM,
        name="coarsen_one",
    )(keys, values)
    level_one = lax.all_to_all(spread_one, "ctx", 0, 0, tiled=True)
    pair = jnp.concatenate([keys, values], axis=0)
    below = shifted(pair, 1)
    above = shifted(pair, -1)
    spread_two = pl.pallas_call(
        coarsen_two_kernel,
        out_shape=shape_of(two_shape, BF16),
        in_specs=[VMEM],
        out_specs=VMEM,
        name="coarsen_two",
    )(level_one)
    level_two = lax.all_to_all(spread_two, "group", 0, 0, tiled=True)

    stats_shape = shape_of((HEADS, 8, HEAD_DIM), F32)
    stats_spec = pl.BlockSpec((1, 8, HEAD_DIM), lambda head: (head, 0, 0))
    tok, both = per_head(BLOCK), per_head(2 * BLOCK)
    near = pl.pallas_call(
        stats_kernel,
        grid=(HEADS,),
        out_shape=stats_shape,
        in_specs=[SMEM, tok, tok, tok, tok, both, both, per_head(*one_shape[:2])],
        out_specs=stats_spec,
        scratch_shapes=[pltpu.VMEM((3 * BLOCK + GROUP_ROWS, HEAD_DIM), F32)],
        cost_estimate=pl.CostEstimate(
            flops=4 * BLOCK * 640 * FEATURES, bytes_accessed=4 << 20, transcendentals=640 * 1024
        ),
        name="near_stats",
    )(place, queries, cotangent, keys, values, below, above, level_one)

    stats, part_two = pl.pallas_call(
        two_kernel,
        out_shape=(stats_shape, shape_of(two_shape, BF16)),
        in_specs=[SMEM] + [VMEM] * 4,
        out_specs=(VMEM, VMEM),
        name="level_two",
    )(place, queries, cotangent, level_two, near)
    arrived_two = lax.all_to_all(part_two, "group", 0, 0, tiled=True)

    output, grad_q, fine, grad_below, grad_above, part_one = pl.pallas_call(
        attend_kernel,
        grid=(HEADS,),
        out_shape=(
            shape_of((BLOCK, FEATURES), BF16),
            shape_of((BLOCK, FEATURES), BF16),
            shape_of((2 * BLOCK, FEATURES), F32),
            shape_of((2 * BLOCK, FEATURES), BF16),
            shape_of((2 * BLOCK, FEATURES), BF16),
            shape_of(one_shape, F32),
        ),
        in_specs=[SMEM, tok, tok, tok, tok, both, both, per_head(*one_shape[:2])]
        + [per_head(*two_shape[:2]), stats_spec],
        out_specs=(tok, tok, both, both, both, per_head(*one_shape[:2])),
        scratch_shapes=[pltpu.VMEM((3 * BLOCK + GROUP_ROWS + LEVEL_TWO, HEAD_DIM), F32)],
        cost_estimate=pl.CostEstimate(
            flops=12 * BLOCK * 896 * FEATURES, bytes_accessed=10 << 20, transcendentals=896 * 1024
        ),
        name="attend",
    )(place, queries, cotangent, keys, values, below, above, level_one, level_two, stats)

    from_above = shifted(grad_below, -1)
    from_below = shifted(grad_above, 1)
    merged = pl.pallas_call(
        merge_kernel,
        out_shape=shape_of(one_shape, BF16),
        in_specs=[VMEM] * 2,
        out_specs=VMEM,
        name="merge",
    )(part_one, arrived_two)
    arrived_one = lax.all_to_all(merged, "ctx", 0, 0, tiled=True)
    grad_keys, grad_values = pl.pallas_call(
        finish_kernel,
        out_shape=(shape_of((BLOCK, FEATURES), BF16),) * 2,
        in_specs=[VMEM] * 4,
        out_specs=(VMEM, VMEM),
        name="finish",
    )(fine, from_below, from_above, arrived_one)
    return (output, grad_q, grad_keys, grad_values)


def solution(mesh):
    placed = P(("group", "ctx"), None)
    return jax.shard_map(
        local,
        mesh=mesh,
        in_specs=(placed,) * 4,
        out_specs=(placed,) * 4,
        check_vma=False,
    )
```

time: 659 us -> 187 us (0.28)
  the two profiles are of different devices: /device:TPU:1 before, /device:TPU:25 now
where the time goes in v1:
time: 187 us; the launch traced here: 186 us
  waiting for transfers between devices  59.4 us (32%)
  starting transfers between devices  49.7 us (27%)
  blocking collectives  39.2 us (21%)
  Pallas kernels  32.5 us (17%)
  local copies, waits for them, and re-layouts  4.12 us (2%)
    ppermute x4, waiting for transfers between devices, shifted(): lax.ppermute(value, ('group', 'ctx'), [(s, s + steps) for s in range(firs...  41.4 us
    all_to_all x1, blocking collectives, local(): level_one = lax.all_to_all(spread_one, 'ctx', 0, 0, tiled=True)  39.2 us
    all_to_all x1, starting transfers between devices, local(): arrived_two = lax.all_to_all(part_two, 'group', 0, 0, tiled=True)  19.4 us
    all_to_all x1, waiting for transfers between devices, local(): arrived_two = lax.all_to_all(part_two, 'group', 0, 0, tiled=True)  16.9 us
    ppermute x4, starting transfers between devices, shifted(): lax.ppermute(value, ('group', 'ctx'), [(s, s + steps) for s in range(firs...  14.6 us
    all_to_all x1, starting transfers between devices, local(): level_two = lax.all_to_all(spread_two, 'group', 0, 0, tiled=True)  9.81 us
    pallas_call x1, Pallas kernels, local(): pl.pallas_call(attend_kernel, grid=(HEADS,), out_shape=(shape_of((BLOCK,...  9.28 us
    pallas_call x1, Pallas kernels, local(): pl.pallas_call(stats_kernel, grid=(HEADS,), out_shape=stats_shape, in_spe...  7.07 us
  transfers between devices with their start and end apart: 7, of which 5 were waited for; matrix products, arithmetic and copies ran while one was open for 0% of the time, Pallas kernels for 9%

profile of v1, /device:TPU:25, one launch (start us, length us, event | category | flops | bytes accessed | tf_op | source)
XLA Modules:
  0.0 186.2 jit_solution(4738875437536308620)
XLA Ops:
  0.6 2.3 %coarsen_one.1 = bf16[32,16,1024]{2,1,0:T(8,128)(2,1)} custom-call(bf16[128,1024]{1,0:T(8,128)(2,1)} %keys.5, bf16[128,1024]{1,0:T(8,128)(2,1)} %values.5), custom_call_target="tpu_custom_call" | custom-call | tf_op jit(solution)/shard_map/coarsen_one/pallas_call | solution.py:219
  2.9 39.2 %all_to_all.20.level_one = bf16[32,16,1024]{2,1,0:T(8,128)(2,1)} all-to-all(bf16[32,16,1024]{2,1,0:T(8,128)(2,1)} %coarsen_one.1), channel_id=1, replica_groups=mesh['group'=16,'ctx'=32] {'ctx'}, dimensions={0} | all-to-all | bytes 2097152 | tf_op jit(solution)/shard_map/all_to_all | solution.py:226
  42.1 0.0 copy-start.3
  42.1 0.0 copy-start.4
  42.1 2.6 %coarsen_two.1 = bf16[16,32,1024]{2,1,0:T(8,128)(2,1)} custom-call(bf16[32,16,1024]{2,1,0:T(8,128)(2,1)} %all_to_all.20.level_one), custom_call_target="tpu_custom_call" | custom-call | tf_op jit(solution)/shard_map/coarsen_two/pallas_call | solution.py:230
  44.8 9.8 %all-to-all-start.1 = ((bf16[16,32,1024]{2,1,0:T(8,128)(2,1)}), bf16[16,32,1024]{2,1,0:T(8,128)(2,1)S(1)}, u32[]{:S(2)}, u32[]{:S(2)}) async-start(bf16[16,32,1024]{2,1,0:T(8,128)(2,1)} %coarsen_two.1), calls=%async_computation.1 | async-start | bytes 2097152 | tf_op jit(solution)/shard_map/all_to_all | solution.py:237
  54.6 0.0 copy-done.3
  54.6 0.0 copy-done.4
  54.6 3.2 %collective-permute-start.1 = (bf16[256,1024]{1,0:T(8,128)(2,1)S(1)}, bf16[256,1024]{1,0:T(8,128)(2,1)S(1)}, u32[]{:S(2)}, u32[]{:S(2)}) collective-permute-start(bf16[256,1024]{1,0:T(8,128)(2,1)S(1)} %constant_dynamic-update-slice_fusion), channel_id=1, source_target_pairs={{1,0},{2,1},{3,2},{4,3},{5,4},{6,5},{7,6},{8,7},{9,8},{10,9},{11,1... | collective-permute-start | bytes 1572872 | tf_op jit(solution)/shard_map/ppermute | solution.py:30
  57.8 2.1 %collective-permute-start = (bf16[256,1024]{1,0:T(8,128)(2,1)S(1)}, bf16[256,1024]{1,0:T(8,128)(2,1)S(1)}, u32[]{:S(2)}, u32[]{:S(2)}) collective-permute-start(bf16[256,1024]{1,0:T(8,128)(2,1)S(1)} %constant_dynamic-update-slice_fusion), channel_id=1, source_target_pairs={{0,1},{1,2},{2,3},{3,4},{4,5},{5,6},{6,7},{7,8},{8,9},{9,10},{10,1... | collective-permute-start | bytes 1572872 | tf_op jit(solution)/shard_map/ppermute | solution.py:30
  60.0 0.6 pad_add_fusion.place
  60.6 9.2 %collective-permute-done.1.above = bf16[256,1024]{1,0:T(8,128)(2,1)S(1)} collective-permute-done((bf16[256,1024]{1,0:T(8,128)(2,1)S(1)}, bf16[256,1024]{1,0:T(8,128)(2,1)S(1)}, u32[]{:S(2)}, u32[]{:S(2)}) %collective-permute-start.1) | collective-permute-done | bytes 524320 | tf_op jit(solution)/shard_map/ppermute | solution.py:30
  69.8 0.0 copy-start.5
  69.8 2.2 %collective-permute-done.below = bf16[256,1024]{1,0:T(8,128)(2,1)S(1)} collective-permute-done((bf16[256,1024]{1,0:T(8,128)(2,1)S(1)}, bf16[256,1024]{1,0:T(8,128)(2,1)S(1)}, u32[]{:S(2)}, u32[]{:S(2)}) %collective-permute-start) | collective-permute-done | bytes 524320 | tf_op jit(solution)/shard_map/ppermute | solution.py:30
  72.0 0.0 copy-done.5
  72.0 0.0 copy-start.6
  72.0 0.8 copy-done.6
  72.8 7.1 %near_stats.1.near = f32[8,8,128]{2,1,0:T(8,128)} custom-call(s32[2]{0:T(128)} %pad_add_fusion.place, bf16[128,1024]{1,0:T(8,128)(2,1)} %queries.5, bf16[128,1024]{1,0:T(8,128)(2,1)} %cotangent.5, bf16[128,1024]{1,0:T(8,128)(2,1)} %keys.5, bf16[128,1024]{1,0:T(8,128)(2,1)} %values.5, bf16[256,1024]{1,0:T(8,128)(2,1)} %copy-done.6, ...), custom_call_target="tpu_custom_call" | custom-call | flops 335544320 | bytes 4194304 | tf_op jit(solution)/shard_map/near_stats/pallas_call | solution.py:242
  79.8 1.1 all-to-all-done.1.level_two
  80.9 0.0 copy-start.1
  80.9 1.0 copy-done.1
  81.9 4.8 %level_two.1 = (f32[8,8,128]{2,1,0:T(8,128)}, bf16[16,32,1024]{2,1,0:T(8,128)(2,1)}) custom-call(s32[2]{0:T(128)} %pad_add_fusion.place, bf16[128,1024]{1,0:T(8,128)(2,1)} %queries.5, bf16[128,1024]{1,0:T(8,128)(2,1)} %cotangent.5, bf16[16,32,1024]{2,1,0:T(8,128)(2,1)} %copy-done.1, f32[8,8,128]{2,1,0:T(8,128)} %near_stats.1.near), custom_call_target="tpu_custom_call" | custom-call | tf_op jit(solution)/shard_map/level_two/pallas_call | solution.py:255
  86.7 19.4 %all-to-all-start.2 = ((bf16[16,32,1024]{2,1,0:T(8,128)(2,1)}), bf16[16,32,1024]{2,1,0:T(8,128)(2,1)S(1)}, u32[]{:S(2)}, u32[]{:S(2)}) async-start(bf16[16,32,1024]{2,1,0:T(8,128)(2,1)} %get-tuple-element.21), calls=%async_computation.2 | async-start | bytes 2097152 | tf_op jit(solution)/shard_map/all_to_all | solution.py:262
  106.1 9.3 %attend.1 = (bf16[128,1024]{1,0:T(8,128)(2,1)}, bf16[128,1024]{1,0:T(8,128)(2,1)}, f32[256,1024]{1,0:T(8,128)}, bf16[256,1024]{1,0:T(8,128)(2,1)}, bf16[256,1024]{1,0:T(8,128)(2,1)}, /*index=5*/f32[32,16,1024]{2,1,0:T(8,128)}) custom-call(s32[2]{0:T(128)} %pad_add_fusion.place, bf16[128,1024]{1,0:T(8,128)(2,1)} %queries.5, bf16[128,1024]{1,0:T(8,128)(2,1)} %cotangent.5, ...), custom_call_target="tpu_custom_call" | custom-call | flops 1409286144 | bytes 10485760 | tf_op jit(solution)/shard_map/attend/pallas_call | solution.py:264
  115.3 16.9 %all-to-all-done.2.arrived = bf16[16,32,1024]{2,1,0:T(8,128)(2,1)S(1)} async-done(((bf16[16,32,1024]{2,1,0:T(8,128)(2,1)}), bf16[16,32,1024]{2,1,0:T(8,128)(2,1)S(1)}, u32[]{:S(2)}, u32[]{:S(2)}) %all-to-all-start.2) | async-done | bytes 1048608 | tf_op jit(solution)/shard_map/all_to_all | solution.py:262
  132.3 0.0 copy-start.2
  132.3 1.0 copy-done.2
  133.3 3.3 %merge.1 = bf16[32,16,1024]{2,1,0:T(8,128)(2,1)} custom-call(f32[32,16,1024]{2,1,0:T(8,128)} %get-tuple-element.20.part_one, bf16[16,32,1024]{2,1,0:T(8,128)(2,1)} %copy-done.2), custom_call_target="tpu_custom_call" | custom-call | tf_op jit(solution)/shard_map/merge/pallas_call | solution.py:287
  136.5 0.0 copy-start.10
  136.5 0.0 copy-start.9
  136.5 5.8 %all-to-all-start.3 = ((bf16[32,16,1024]{2,1,0:T(8,128)(2,1)}), bf16[32,16,1024]{2,1,0:T(8,128)(2,1)S(1)}, u32[]{:S(2)}, u32[]{:S(2)}) async-start(bf16[32,16,1024]{2,1,0:T(8,128)(2,1)} %merge.1), calls=%async_computation.3 | async-start | bytes 2097152 | tf_op jit(solution)/shard_map/all_to_all | solution.py:294
  142.4 0.0 copy-done.10
  142.4 3.1 %collective-permute-start.2 = (bf16[256,1024]{1,0:T(8,128)(2,1)S(1)}, bf16[256,1024]{1,0:T(8,128)(2,1)S(1)}, u32[]{:S(2)}, u32[]{:S(2)}) collective-permute-start(bf16[256,1024]{1,0:T(8,128)(2,1)S(1)} %copy-done.10), channel_id=1, source_target_pairs={{0,1},{1,2},{2,3},{3,4},{4,5},{5,6},{6,7},{7,8},{8,9},{9,10},{10,1... | collective-permute-start | bytes 1572872 | tf_op jit(solution)/shard_map/ppermute | solution.py:30
  145.5 0.0 copy-done.9
  145.5 6.2 %collective-permute-start.3 = (bf16[256,1024]{1,0:T(8,128)(2,1)S(1)}, bf16[256,1024]{1,0:T(8,128)(2,1)S(1)}, u32[]{:S(2)}, u32[]{:S(2)}) collective-permute-start(bf16[256,1024]{1,0:T(8,128)(2,1)S(1)} %copy-done.9), channel_id=1, source_target_pairs={{1,0},{2,1},{3,2},{4,3},{5,4},{6,5},{7,6},{8,7},{9,8},{10,9},{11,1... | collective-permute-start | bytes 1572872 | tf_op jit(solution)/shard_map/ppermute | solution.py:30
  151.7 30.0 %collective-permute-done.2.from_below = bf16[256,1024]{1,0:T(8,128)(2,1)S(1)} collective-permute-done((bf16[256,1024]{1,0:T(8,128)(2,1)S(1)}, bf16[256,1024]{1,0:T(8,128)(2,1)S(1)}, u32[]{:S(2)}, u32[]{:S(2)}) %collective-permute-start.2) | collective-permute-done | bytes 524320 | tf_op jit(solution)/shard_map/ppermute | solution.py:30
  181.8 0.0 copy-start.7
  181.8 0.0 collective-permute-done.3.from_above
  181.8 0.0 copy-start.8
  181.8 0.0 all-to-all-done.3.arrived
  181.8 0.0 copy-start
  181.8 0.8 copy-done.7
  182.6 0.2 copy-done.8
  182.7 0.4 copy-done
  183.1 3.1 %finish.1 = (bf16[128,1024]{1,0:T(8,128)(2,1)}, bf16[128,1024]{1,0:T(8,128)(2,1)}) custom-call(f32[256,1024]{1,0:T(8,128)} %get-tuple-element.17.fine, bf16[256,1024]{1,0:T(8,128)(2,1)} %copy-done.7, bf16[256,1024]{1,0:T(8,128)(2,1)} %copy-done.8, bf16[32,16,1024]{2,1,0:T(8,128)(2,1)} %copy-done), custom_call_target="tpu_custom_call" | custom-call | tf_op jit(solution)/shard_map/finish/pallas_call | solution.py:295
  (2 shorter events, 0.0 us)
Async XLA Ops:
  42.1 12.4 %copy-start.3 = (bf16[128,1024]{1,0:T(8,128)(2,1)S(1)}, bf16[128,1024]{1,0:T(8,128)(2,1)}, u32[]{:S(2)}) copy-start(bf16[128,1024]{1,0:T(8,128)(2,1)} %keys.5) | copy-start | bytes 786436
  42.1 12.5 %copy-start.4 = (bf16[128,1024]{1,0:T(8,128)(2,1)S(1)}, bf16[128,1024]{1,0:T(8,128)(2,1)}, u32[]{:S(2)}) copy-start(bf16[128,1024]{1,0:T(8,128)(2,1)} %values.5) | copy-start | bytes 786436
  44.8 36.1 %all-to-all-start.1 = ((bf16[16,32,1024]{2,1,0:T(8,128)(2,1)}), bf16[16,32,1024]{2,1,0:T(8,128)(2,1)S(1)}, u32[]{:S(2)}, u32[]{:S(2)}) async-start(bf16[16,32,1024]{2,1,0:T(8,128)(2,1)} %coarsen_two.1), calls=%async_computation.1 | async-start | bytes 2097152 | tf_op jit(solution)/shard_map/all_to_all | solution.py:237
  54.6 15.1 %collective-permute-start.1 = (bf16[256,1024]{1,0:T(8,128)(2,1)S(1)}, bf16[256,1024]{1,0:T(8,128)(2,1)S(1)}, u32[]{:S(2)}, u32[]{:S(2)}) collective-permute-start(bf16[256,1024]{1,0:T(8,128)(2,1)S(1)} %constant_dynamic-update-slice_fusion), channel_id=1, source_target_pairs={{1,0},{2,1},{3,2},{4,3},{5,4},{6,5},{7,6},{8,7},{9,8},{10,9},{11,1... | collective-permute-start | bytes 1572872 | tf_op jit(solution)/shard_map/ppermute | solution.py:30
  57.8 14.1 %collective-permute-start = (bf16[256,1024]{1,0:T(8,128)(2,1)S(1)}, bf16[256,1024]{1,0:T(8,128)(2,1)S(1)}, u32[]{:S(2)}, u32[]{:S(2)}) collective-permute-start(bf16[256,1024]{1,0:T(8,128)(2,1)S(1)} %constant_dynamic-update-slice_fusion), channel_id=1, source_target_pairs={{0,1},{1,2},{2,3},{3,4},{4,5},{5,6},{6,7},{7,8},{8,9},{9,10},{10,1... | collective-permute-start | bytes 1572872 | tf_op jit(solution)/shard_map/ppermute | solution.py:30
  69.8 2.2 %copy-start.5 = (bf16[256,1024]{1,0:T(8,128)(2,1)}, bf16[256,1024]{1,0:T(8,128)(2,1)S(1)}, u32[]{:S(2)}) copy-start(bf16[256,1024]{1,0:T(8,128)(2,1)S(1)} %collective-permute-done.1.above) | copy-start | bytes 1572868
  72.0 0.8 copy-start.6
  80.9 1.0 copy-start.1
  86.7 45.6 %all-to-all-start.2 = ((bf16[16,32,1024]{2,1,0:T(8,128)(2,1)}), bf16[16,32,1024]{2,1,0:T(8,128)(2,1)S(1)}, u32[]{:S(2)}, u32[]{:S(2)}) async-start(bf16[16,32,1024]{2,1,0:T(8,128)(2,1)} %get-tuple-element.21), calls=%async_computation.2 | async-start | bytes 2097152 | tf_op jit(solution)/shard_map/all_to_all | solution.py:262
  132.3 1.0 copy-start.2
  136.5 5.8 %copy-start.10 = (bf16[256,1024]{1,0:T(8,128)(2,1)S(1)}, bf16[256,1024]{1,0:T(8,128)(2,1)}, u32[]{:S(2)}) copy-start(bf16[256,1024]{1,0:T(8,128)(2,1)} %get-tuple-element.18) | copy-start | bytes 1572868
  136.5 9.0 %copy-start.9 = (bf16[256,1024]{1,0:T(8,128)(2,1)S(1)}, bf16[256,1024]{1,0:T(8,128)(2,1)}, u32[]{:S(2)}) copy-start(bf16[256,1024]{1,0:T(8,128)(2,1)} %get-tuple-element.19) | copy-start | bytes 1572868
  136.5 45.2 %all-to-all-start.3 = ((bf16[32,16,1024]{2,1,0:T(8,128)(2,1)}), bf16[32,16,1024]{2,1,0:T(8,128)(2,1)S(1)}, u32[]{:S(2)}, u32[]{:S(2)}) async-start(bf16[32,16,1024]{2,1,0:T(8,128)(2,1)} %merge.1), calls=%async_computation.3 | async-start | bytes 2097152 | tf_op jit(solution)/shard_map/all_to_all | solution.py:294
  142.4 39.4 %collective-permute-start.2 = (bf16[256,1024]{1,0:T(8,128)(2,1)S(1)}, bf16[256,1024]{1,0:T(8,128)(2,1)S(1)}, u32[]{:S(2)}, u32[]{:S(2)}) collective-permute-start(bf16[256,1024]{1,0:T(8,128)(2,1)S(1)} %copy-done.10), channel_id=1, source_target_pairs={{0,1},{1,2},{2,3},{3,4},{4,5},{5,6},{6,7},{7,8},{8,9},{9,10},{10,1... | collective-permute-start | bytes 1572872 | tf_op jit(solution)/shard_map/ppermute | solution.py:30
  145.5 36.2 %collective-permute-start.3 = (bf16[256,1024]{1,0:T(8,128)(2,1)S(1)}, bf16[256,1024]{1,0:T(8,128)(2,1)S(1)}, u32[]{:S(2)}, u32[]{:S(2)}) collective-permute-start(bf16[256,1024]{1,0:T(8,128)(2,1)S(1)} %copy-done.9), channel_id=1, source_target_pairs={{1,0},{2,1},{3,2},{4,3},{5,4},{6,5},{7,6},{8,7},{9,8},{10,9},{11,1... | collective-permute-start | bytes 1572872 | tf_op jit(solution)/shard_map/ppermute | solution.py:30
  181.8 0.8 copy-start.7
  181.8 1.0 copy-start.8
  181.8 1.3 copy-start

commit v2 on v0

v2 whole, which is shorter than its diff:
```python
import jax
import jax.numpy as jnp
from jax import lax
from jax.experimental import pallas as pl
from jax.experimental.pallas import tpu as pltpu
from jax.sharding import Mesh
from jax.sharding import PartitionSpec as P

HEADS = 8
HEAD_DIM = 128
BLOCK = 128
COARSE = 16
ONE_ROWS = BLOCK // COARSE
N_Y, N_CORE, N_Z, N_X = 8, 2, 8, 4
AXES = ("y", "core", "z", "x")
ROW = ("core", "x")
N_BLOCK = N_CORE * N_X
N_CTX = N_Z * N_X
N_GROUP = N_Y * N_CORE
GROUP_ROWS = N_CTX * ONE_ROWS
TWO_ROWS = GROUP_ROWS // COARSE
LEVEL_TWO = N_GROUP * TWO_ROWS
FEATURES = HEADS * HEAD_DIM
FACTOR = HEAD_DIM ** (-0.5)
SHUT = -1e30
F32 = jnp.float32
BF16 = jnp.bfloat16
VMEM = pl.BlockSpec(memory_space=pltpu.VMEM)
SMEM = pl.BlockSpec(memory_space=pltpu.SMEM)
QUERY, KEY, VALUE, COT = (slice(i * BLOCK, (i + 1) * BLOCK) for i in range(4))
PAIR = slice(BLOCK, 3 * BLOCK)


def dot_nt(left, right):
    return lax.dot_general(left, right, (((1,), (1,)), ((), ())), preferred_element_type=F32)


def dot_nn(left, right):
    return lax.dot_general(left, right, (((1,), (0,)), ((), ())), preferred_element_type=F32)


def dot_tn(left, right):
    return lax.dot_general(left, right, (((0,), (0,)), ((), ())), preferred_element_type=F32)


def iota(shape, dim):
    return lax.broadcasted_iota(jnp.int32, shape, dim)


def lanes_of(head):
    return slice(head * HEAD_DIM, (head + 1) * HEAD_DIM)


def pack_kernel(queries, keys, values, cotangent, packed):
    for head in range(HEADS):
        for rows, source in ((QUERY, queries), (KEY, keys), (VALUE, values), (COT, cotangent)):
            packed[head, rows] = source[:, lanes_of(head)]


def coarsen_one_kernel(held, spread):
    row, token = iota((2 * ONE_ROWS, BLOCK), 0), iota((2 * ONE_ROWS, BLOCK), 1)
    pick_k = jnp.where(row == token // COARSE, 1.0, 0.0).astype(BF16)
    pick_v = jnp.where(row - ONE_ROWS == token // COARSE, 1.0, 0.0).astype(BF16)
    pick = jnp.concatenate([pick_k, pick_v], axis=1)
    for block in range(N_BLOCK):
        own = (dot_nn(pick, held[block, PAIR]) * 0.25).astype(BF16)
        rows = slice(block * 2 * ONE_ROWS, (block + 1) * 2 * ONE_ROWS)
        for copy in range(N_Z):
            spread[copy, rows] = own


def coarsen_two_kernel(level_one, spread):
    width = N_BLOCK * 2 * ONE_ROWS
    shape = (N_CORE * 2 * TWO_ROWS, N_Z * width)
    row, source = iota(shape, 0), iota(shape, 1)
    z, rest = source // width, source % width
    group, rest = rest // (width // 2), rest % (width // 2)
    x, kind = rest // (2 * ONE_ROWS), (rest % (2 * ONE_ROWS)) // ONE_ROWS
    target = (group * 2 + kind) * TWO_ROWS + (z * N_X + x) // 2
    pick = jnp.where(row == target, 1.0, 0.0).astype(BF16)
    own = dot_nn(pick, level_one[...].reshape(N_Z * width, HEAD_DIM))
    own = (own * 0.25).astype(BF16)
    for copy in range(N_Y):
        spread[copy] = own


def split_one(level_one, group):
    half = N_X * 2 * ONE_ROWS
    wide = level_one[:, group * half : (group + 1) * half].astype(F32)
    wide = wide.reshape(N_CTX, 2 * ONE_ROWS, HEAD_DIM)
    key = wide[:, :ONE_ROWS].reshape(GROUP_ROWS, HEAD_DIM).astype(BF16)
    value = wide[:, ONE_ROWS:].reshape(GROUP_ROWS, HEAD_DIM).astype(BF16)
    return key, value


def near_bias(place, block):
    y, z = place[0], place[1]
    group, x = block // N_X, block % N_X
    shape = (BLOCK, HEAD_DIM)
    low, high = jnp.zeros(shape, F32), jnp.zeros(shape, F32)
    if block == 0:
        low = jnp.full(shape, jnp.where((y == 0) & (z == 0), SHUT, 0.0).astype(F32))
    if block == N_BLOCK - 1:
        high = jnp.full(shape, jnp.where((y == N_Y - 1) & (z == N_Z - 1), SHUT, 0.0).astype(F32))
    row = iota((GROUP_ROWS, HEAD_DIM), 0) // ONE_ROWS
    one = jnp.where(jnp.abs(row - (z * N_X + x)) <= 1, SHUT, 0.0).astype(F32)
    return [low, jnp.zeros(shape, F32), high, one]


def two_bias(place, group):
    row = iota((LEVEL_TWO, HEAD_DIM), 0) // TWO_ROWS
    return jnp.where(row == place[0] * N_CORE + group, SHUT, 0.0).astype(F32)


def near_window(held, below, above, block, first):
    group, x = block // N_X, block % N_X
    rows = slice(BLOCK + first * BLOCK, BLOCK + (first + 1) * BLOCK)
    halo = slice(first * BLOCK, (first + 1) * BLOCK)
    low = below[group, halo] if x == 0 else held[block - 1, rows]
    high = above[group, halo] if x == N_X - 1 else held[block + 1, rows]
    return [low, held[block, rows], high]


def near_kernel(place, held, below, above, level_one, stats):
    for group in range(N_CORE):
        one_k, one_v = split_one(level_one, group)
        for block in range(group * N_X, (group + 1) * N_X):
            all_k = jnp.concatenate(near_window(held, below, above, block, 0) + [one_k], axis=0)
            all_v = jnp.concatenate(near_window(held, below, above, block, 1) + [one_v], axis=0)
            bias = jnp.concatenate(near_bias(place, block), axis=0)
            scores = dot_nt(all_k, held[block, QUERY]) * FACTOR + bias
            highest = jnp.max(scores, axis=0, keepdims=True)
            weights = jnp.exp(scores - highest)
            slopes = dot_nt(all_v, held[block, COT])
            stats[block, 0:1] = highest
            stats[block, 1:2] = jnp.sum(weights, axis=0, keepdims=True)
            stats[block, 2:3] = jnp.sum(weights * slopes, axis=0, keepdims=True)


def two_kernel(place, held, level_two, near, stats, part_two, chances, dscores):
    key = level_two[:, :TWO_ROWS].reshape(LEVEL_TWO, HEAD_DIM)
    value = level_two[:, TWO_ROWS:].reshape(LEVEL_TWO, HEAD_DIM)
    for group in range(N_CORE):
        bias = two_bias(place, group)
        for block in range(group * N_X, (group + 1) * N_X):
            scores = dot_nt(key, held[block, QUERY]) * FACTOR + bias
            slopes = dot_nt(value, held[block, COT])
            near_highest = near[block, 0:1]
            highest = jnp.maximum(near_highest, jnp.max(scores, axis=0, keepdims=True))
            scale = jnp.exp(near_highest - highest)
            weights = jnp.exp(scores - highest)
            total = near[block, 1:2] * scale + jnp.sum(weights, axis=0, keepdims=True)
            inverse = 1.0 / total
            centre = near[block, 2:3] * scale + jnp.sum(weights * slopes, axis=0, keepdims=True)
            centre = centre * inverse
            stats[block, 0:1] = highest
            stats[block, 1:2] = inverse
            stats[block, 2:3] = centre
            chance = weights * inverse
            dscores[:, lanes_of(block)] = (chance * (slopes - centre) * FACTOR).astype(BF16)
            chances[:, lanes_of(block)] = chance.astype(BF16)
    tokens = N_BLOCK * BLOCK
    grad_k = dot_nn(dscores[...], held[:, QUERY].reshape(tokens, HEAD_DIM))
    grad_v = dot_nn(chances[...], held[:, COT].reshape(tokens, HEAD_DIM))
    grad_k = grad_k.reshape(N_GROUP, TWO_ROWS, HEAD_DIM)
    grad_v = grad_v.reshape(N_GROUP, TWO_ROWS, HEAD_DIM)
    part_two[...] = jnp.concatenate([grad_k, grad_v], axis=1).astype(BF16)


def attend_kernel(
    place, held, below, above, level_one, level_two, stats,
    answer, fine, grad_below, grad_above, part_one, window, ones,
):
    two_k = level_two[:, :TWO_ROWS].reshape(LEVEL_TWO, HEAD_DIM)
    two_v = level_two[:, TWO_ROWS:].reshape(LEVEL_TWO, HEAD_DIM)
    near = 3 * BLOCK
    seen = near + GROUP_ROWS
    for group in range(N_CORE):
        one_k, one_v = split_one(level_one, group)
        shut = two_bias(place, group)
        window[...] = jnp.zeros_like(window)
        for block in range(group * N_X, (group + 1) * N_X):
            x = block % N_X
            query, cot = held[block, QUERY], held[block, COT]
            near_k = near_window(held, below, above, block, 0)
            near_v = near_window(held, below, above, block, 1)
            all_k = jnp.concatenate(near_k + [one_k, two_k], axis=0)
            all_v = jnp.concatenate(near_v + [one_v, two_v], axis=0)
            bias = jnp.concatenate(near_bias(place, block) + [shut], axis=0)
            scores = dot_nt(all_k, query) * FACTOR + bias
            chance = jnp.exp(scores - stats[block, 0:1]) * stats[block, 1:2]
            slopes = dot_nt(all_v, cot)
            dscore = (chance * (slopes - stats[block, 2:3]) * FACTOR).astype(BF16)
            chance = chance.astype(BF16)
            answer[block, :BLOCK] = dot_tn(chance, all_v).astype(BF16)
            answer[block, BLOCK:] = dot_tn(dscore, all_k).astype(BF16)
            for kind, (left, right) in enumerate(((dscore, query), (chance, cot))):
                grad = dot_nn(left[:seen], right)
                window[kind, x * BLOCK : (x + 3) * BLOCK] += grad[:near]
                ones[kind] = grad[near:] if x == 0 else ones[kind] + grad[near:]
        for kind in range(2):
            rows = slice(kind * BLOCK, (kind + 1) * BLOCK)
            grad_below[group, rows] = window[kind, :BLOCK].astype(BF16)
            grad_above[group, rows] = window[kind, (N_X + 1) * BLOCK :].astype(BF16)
            for x in range(N_X):
                fine[group * N_X + x, rows] = window[kind, (x + 1) * BLOCK : (x + 2) * BLOCK]
        both = [ones[kind].reshape(N_CTX, ONE_ROWS, HEAD_DIM) for kind in range(2)]
        both = jnp.concatenate(both, axis=1).reshape(N_Z, N_X * 2 * ONE_ROWS, HEAD_DIM)
        half = N_X * 2 * ONE_ROWS
        part_one[:, group * half : (group + 1) * half] = both


def merge_kernel(part_one, arrived, merged):
    two = jnp.sum(arrived[...].astype(F32), axis=0) * 0.25
    for group in range(N_CORE):
        for ctx in range(N_CTX):
            z, x = ctx // N_X, ctx % N_X
            low = group * 2 * TWO_ROWS + ctx // 2
            high = low + TWO_ROWS
            first = (group * N_X + x) * 2 * ONE_ROWS
            rows = slice(first, first + 2 * ONE_ROWS)
            carried = jnp.concatenate(
                [
                    jnp.broadcast_to(two[low : low + 1], (ONE_ROWS, HEAD_DIM)),
                    jnp.broadcast_to(two[high : high + 1], (ONE_ROWS, HEAD_DIM)),
                ],
                axis=0,
            )
            merged[z, rows] = (part_one[z, rows] + carried).astype(BF16)


def finish_kernel(answer, fine, from_below, from_above, arrived, result):
    owned = jnp.sum(arrived[...].astype(F32), axis=0) * 0.25
    for block in range(N_BLOCK):
        group, x = block // N_X, block % N_X
        result[block, : 2 * BLOCK] = answer[block]
        for kind in range(2):
            rows = slice(kind * BLOCK, (kind + 1) * BLOCK)
            total = fine[block, rows]
            if x == 0:
                total = total + from_below[group, rows].astype(F32)
            if x == N_X - 1:
                total = total + from_above[group, rows].astype(F32)
            first = (2 * block + kind) * ONE_ROWS
            carried = owned[first : first + ONE_ROWS].reshape(ONE_ROWS, 1, HEAD_DIM)
            total = total.reshape(ONE_ROWS, COARSE, HEAD_DIM) + carried
            out = slice((2 + kind) * BLOCK, (3 + kind) * BLOCK)
            result[block, out] = total.reshape(BLOCK, HEAD_DIM).astype(BF16)


def unpack_kernel(packed, output, grad_q, grad_k, grad_v):
    for head in range(HEADS):
        for place, out in enumerate((output, grad_q, grad_k, grad_v)):
            out[:, lanes_of(head)] = packed[head, place * BLOCK : (place + 1) * BLOCK]


def shape_of(shape, dtype):
    return jax.ShapeDtypeStruct(shape, dtype)


def run(kernel, name, out_shape, *args, scratch=(), place=False, cost=None):
    several = isinstance(out_shape, tuple)
    specs = [SMEM if place and i == 0 else VMEM for i in range(len(args))]
    return pl.pallas_call(
        kernel,
        out_shape=out_shape,
        in_specs=specs,
        out_specs=(VMEM,) * len(out_shape) if several else VMEM,
        scratch_shapes=list(scratch),
        cost_estimate=cost,
        name=name,
    )(*args)


def at(y, z):
    return y * N_Z + z


SPOTS = [(y, z) for y in range(N_Y) for z in range(N_Z)]
RISE = (
    [(at(y, z), at(y, (z + 1) % N_Z)) for y, z in SPOTS],
    [(at(y, z), at(y, z) + 1) for y, z in SPOTS if at(y, z) + 1 < N_Y * N_Z],
)
FALL = (
    [(at(y, z), at(y, z) - 1) for y, z in SPOTS if at(y, z) > 0],
    [(at(y, z), at(y, (z - 1) % N_Z)) for y, z in SPOTS],
)


def exchange(parts, routes, swap):
    first, second = (lax.ppermute(v, ("y", "z"), r) for v, r in zip(parts, routes))
    return jnp.where(swap, jnp.stack([second, first]), jnp.stack([first, second]))


def local(queries, keys, values, cotangent):
    y, z = lax.axis_index("y"), lax.axis_index("z")
    place = jnp.stack([y, z]).astype(jnp.int32)
    wide = (HEADS, 4 * BLOCK, HEAD_DIM)
    one = (N_Z, N_BLOCK * 2 * ONE_ROWS, HEAD_DIM)
    two = (N_GROUP, 2 * TWO_ROWS, HEAD_DIM)
    halo = (N_CORE, 2 * BLOCK, HEAD_DIM)
    tokens = N_BLOCK * BLOCK

    packed = run(pack_kernel, "pack", shape_of(wide, BF16), queries, keys, values, cotangent)
    held = lax.all_to_all(packed, ROW, 0, 0, tiled=True)

    spread = run(coarsen_one_kernel, "coarsen_one", shape_of(one, BF16), held)
    level_one = lax.all_to_all(spread, "z", 0, 0, tiled=True)
    below = exchange([held[N_X - 1, PAIR], held[N_BLOCK - 1, PAIR]], RISE, z == 0)
    above = exchange([held[0, PAIR], held[N_X, PAIR]], FALL, z == N_Z - 1)

    spread = run(coarsen_two_kernel, "coarsen_two", shape_of((N_Y, 4 * TWO_ROWS, HEAD_DIM), BF16), level_one)
    level_two = lax.all_to_all(spread, "y", 0, 0, tiled=True).reshape(two)

    stats_shape = shape_of((N_BLOCK, 8, HEAD_DIM), F32)
    near = run(
        near_kernel, "near_stats", stats_shape, place, held, below, above, level_one, place=True,
        cost=pl.CostEstimate(
            flops=4 * tokens * 640 * HEAD_DIM, bytes_accessed=2 << 20, transcendentals=640 * tokens
        ),
    )
    stats, part_two = run(
        two_kernel, "level_two", (stats_shape, shape_of(two, BF16)),
        place, held, level_two, near, place=True,
        scratch=[pltpu.VMEM((LEVEL_TWO, tokens), BF16)] * 2,
    )
    part_two = part_two.reshape(N_Y, 4 * TWO_ROWS, HEAD_DIM)
    arrived_two = lax.all_to_all(part_two, "y", 0, 0, tiled=True)

    answer, fine, grad_below, grad_above, part_one = run(
        attend_kernel, "attend",
        (
            shape_of((N_BLOCK, 2 * BLOCK, HEAD_DIM), BF16),
            shape_of((N_BLOCK, 2 * BLOCK, HEAD_DIM), F32),
            shape_of(halo, BF16),
            shape_of(halo, BF16),
            shape_of(one, F32),
        ),
        place, held, below, above, level_one, level_two, stats, place=True,
        scratch=[
            pltpu.VMEM((2, (N_X + 2) * BLOCK, HEAD_DIM), F32),
            pltpu.VMEM((2, GROUP_ROWS, HEAD_DIM), F32),
        ],
        cost=pl.CostEstimate(
            flops=12 * tokens * 896 * HEAD_DIM, bytes_accessed=4 << 20, transcendentals=896 * tokens
        ),
    )
    from_below = exchange([grad_above[0], grad_above[1]], RISE, z == 0)
    from_above = exchange([grad_below[0], grad_below[1]], FALL, z == N_Z - 1)

    merged = run(merge_kernel, "merge", shape_of(one, BF16), part_one, arrived_two)
    arrived_one = lax.all_to_all(merged, "z", 0, 0, tiled=True)
    result = run(
        finish_kernel, "finish", shape_of(wide, BF16), answer, fine, from_below, from_above, arrived_one
    )
    arrived = lax.all_to_all(result, ROW, 0, 0, tiled=True)
    return run(unpack_kernel, "unpack", (shape_of((BLOCK, FEATURES), BF16),) * 4, arrived)


def solution(mesh):
    rows = Mesh(mesh.devices.reshape(N_Y, N_CORE, N_Z, N_X), AXES)
    placed = P(AXES, None)
    return jax.shard_map(
        local,
        mesh=rows,
        in_specs=(placed,) * 4,
        out_specs=(placed,) * 4,
        check_vma=False,
    )
```

time: 659 us -> 138 us (0.21)
  waiting for transfers between devices: 530 us -> 8.54 us
  blocking collectives: 0 us -> 48.7 us
  matrix products: 39.8 us -> 0 us
  Pallas kernels: 0 us -> 26.7 us
  local copies, waits for them, and re-layouts: 31.2 us -> 4.55 us
  starting transfers between devices: 21.3 us -> 44 us
  other arithmetic: 18.9 us -> 3.27 us
  between operations: 14 us -> 0.79 us
    psum x2 -> x0, waiting for transfers between devices: 420 us -> none  [the longest x1 259 us: local(): total_two = lax.psum(part_two, ('group', 'ctx'))]
    all_gather x2 -> x0, waiting for transfers between devices: 106 us -> none  [the longest x1 85.8 us: local(): level_one = lax.all_gather(own_one, 'ctx', axis=1, tiled=True)]
    all_to_all x0 -> x2, blocking collectives: none -> 48.7 us  [the longest x1 26.1 us: local(): held = lax.all_to_all(packed, ROW, 0, 0, tiled=True)]
    dot_general x6 -> x0, matrix products: 36.5 us -> none  [the longest x1 8.6 us: attend(): jnp.einsum('hrn,rhd->nhd', dscore, query_h, preferred_element_type=jnp.fl...]
    pallas_call x0 -> x9, Pallas kernels: none -> 26.7 us  [run(): pl.pallas_call(kernel, out_shape=out_shape, in_specs=specs, out_specs=(VM...]
    all_to_all x0 -> x4, starting transfers between devices: none -> 19.9 us  [the longest x1 6.83 us: local(): level_two = lax.all_to_all(spread, 'y', 0, 0, tiled=True).reshape(two)]
    another operation x2 -> x0, local copies, waits for them, and re-layouts: 10.1 us -> none  [local(): grads = jnp.stack([grad_k, grad_v])]
    slice x3 -> x0, local copies, waits for them, and re-layouts: 9.96 us -> none  [the longest x2 6.16 us: local(): allkeys[0]]
  transfers between devices with their start and end apart: 8 -> 12, of which waited for: 6 -> 2; matrix products, arithmetic and copies ran while one was open for 4% -> 4% of each run, Pallas kernels for 0% -> 10%
where the time goes in v2:
time: 138 us; the launch traced here: 137 us
  blocking collectives  48.7 us (35%)
  starting transfers between devices  44 us (32%)
  Pallas kernels  26.7 us (19%)
  waiting for transfers between devices  8.54 us (6%)
  local copies, waits for them, and re-layouts  4.55 us (3%)
  other arithmetic  3.27 us (2%)
    pallas_call x9, Pallas kernels, run(): pl.pallas_call(kernel, out_shape=out_shape, in_specs=specs, out_specs=(VM...  26.7 us
    all_to_all x1, blocking collectives, local(): held = lax.all_to_all(packed, ROW, 0, 0, tiled=True)  26.1 us
    ppermute x8, starting transfers between devices, exchange(): lax.ppermute(v, ('y', 'z'), r)  24.1 us
    all_to_all x1, blocking collectives, local(): arrived = lax.all_to_all(result, ROW, 0, 0, tiled=True)  22.7 us
    all_to_all x1, starting transfers between devices, local(): level_two = lax.all_to_all(spread, 'y', 0, 0, tiled=True).reshape(two)  6.83 us
    ppermute x8, waiting for transfers between devices, exchange(): lax.ppermute(v, ('y', 'z'), r)  5.38 us
    all_to_all x1, starting transfers between devices, local(): level_one = lax.all_to_all(spread, 'z', 0, 0, tiled=True)  4.86 us
    all_to_all x1, starting transfers between devices, local(): arrived_one = lax.all_to_all(merged, 'z', 0, 0, tiled=True)  4.71 us
  transfers between devices with their start and end apart: 12, of which 2 were waited for; matrix products, arithmetic and copies ran while one was open for 4% of the time, Pallas kernels for 10%

profile of v2, /device:TPU:1, one launch (start us, length us, event | category | flops | bytes accessed | tf_op | source)
XLA Modules:
  0.0 136.6 jit_solution(9216851070715383084)
XLA Ops:
  0.6 2.3 %pack.1 = bf16[8,512,128]{2,1,0:T(8,128)(2,1)} custom-call(bf16[128,1024]{1,0:T(8,128)(2,1)} %queries.1, bf16[128,1024]{1,0:T(8,128)(2,1)} %keys.1, bf16[128,1024]{1,0:T(8,128)(2,1)} %values.1, bf16[128,1024]{1,0:T(8,128)(2,1)} %cotangent.1), custom_call_target="tpu_custom_call" | custom-call | tf_op jit(solution)/shard_map/pack/pallas_call | solution.py:264
  3.0 26.1 %all_to_all.30.held = bf16[8,512,128]{2,1,0:T(8,128)(2,1)} all-to-all(bf16[8,512,128]{2,1,0:T(8,128)(2,1)} %pack.1), channel_id=1, replica_groups=mesh['y'=8,'core'=2,'z'=8,'x'=4] {'core','x'}, dimensions={0} | all-to-all | bytes 2097152 | tf_op jit(solution)/shard_map/all_to_all | solution.py:305
  29.0 2.1 %coarsen_one.1 = bf16[8,128,128]{2,1,0:T(8,128)(2,1)} custom-call(bf16[8,512,128]{2,1,0:T(8,128)(2,1)} %all_to_all.30.held), custom_call_target="tpu_custom_call" | custom-call | tf_op jit(solution)/shard_map/coarsen_one/pallas_call | solution.py:264
  31.2 4.9 %all-to-all-start.1 = ((bf16[8,128,128]{2,1,0:T(8,128)(2,1)}), bf16[8,128,128]{2,1,0:T(8,128)(2,1)S(1)}, u32[]{:S(2)}, u32[]{:S(2)}) async-start(bf16[8,128,128]{2,1,0:T(8,128)(2,1)} %coarsen_one.1), calls=%async_computation.1 | async-start | bytes 524288 | tf_op jit(solution)/shard_map/all_to_all | solution.py:308
  36.0 1.0 slice_bitcast_fusion.1
  37.0 4.6 %collective-permute-start.2 = (bf16[256,128]{1,0:T(8,128)(2,1)S(1)}, bf16[256,128]{1,0:T(8,128)(2,1)S(1)}, u32[]{:S(2)}, u32[]{:S(2)}) collective-permute-start(bf16[256,128]{1,0:T(8,128)(2,1)S(1)} %get-tuple-element.18), channel_id=1, source_target_pairs={{0,28},{4,0},{8,4},{12,8},{16,12},{20,16},{24,20},{28,24},{64,92},... | collective-permute-start | bytes 196616 | tf_op jit(solution)/shard_map/ppermute | solution.py:291
  41.6 1.3 collective-permute-start.3
  42.9 0.6 pad_add_fusion.place
  43.5 4.0 %collective-permute-start.1 = (bf16[256,128]{1,0:T(8,128)(2,1)S(1)}, bf16[256,128]{1,0:T(8,128)(2,1)S(1)}, u32[]{:S(2)}, u32[]{:S(2)}) collective-permute-start(bf16[256,128]{1,0:T(8,128)(2,1)S(1)} %get-tuple-element.20), channel_id=1, source_target_pairs={{0,4},{4,8},{8,12},{12,16},{16,20},{20,24},{24,28},{28,0},{64,68},... | collective-permute-start | bytes 196616 | tf_op jit(solution)/shard_map/ppermute | solution.py:291
  47.4 1.9 %collective-permute-start = (bf16[256,128]{1,0:T(8,128)(2,1)S(1)}, bf16[256,128]{1,0:T(8,128)(2,1)S(1)}, u32[]{:S(2)}, u32[]{:S(2)}) collective-permute-start(bf16[256,128]{1,0:T(8,128)(2,1)S(1)} %get-tuple-element.21), channel_id=1, source_target_pairs={{0,4},{4,8},{8,12},{12,16},{16,20},{20,24},{24,28},{28,64},{64,68}... | collective-permute-start | bytes 196616 | tf_op jit(solution)/shard_map/ppermute | solution.py:291
  49.4 0.0 all-to-all-done.1.level_one
  49.4 0.0 copy-start
  49.4 0.7 copy-done
  50.1 1.8 %coarsen_two.1 = bf16[8,64,128]{2,1,0:T(8,128)(2,1)} custom-call(bf16[8,128,128]{2,1,0:T(8,128)(2,1)} %copy-done), custom_call_target="tpu_custom_call" | custom-call | tf_op jit(solution)/shard_map/coarsen_two/pallas_call | solution.py:264
  51.9 6.8 %all-to-all-start.2 = ((bf16[8,64,128]{2,1,0:T(8,128)(2,1)}), bf16[8,64,128]{2,1,0:T(8,128)(2,1)S(1)}, u32[]{:S(2)}, u32[]{:S(2)}) async-start(bf16[8,64,128]{2,1,0:T(8,128)(2,1)} %coarsen_two.1), calls=%async_computation.2 | async-start | bytes 262144 | tf_op jit(solution)/shard_map/all_to_all | solution.py:313
  58.7 0.0 collective-permute-done.2
  58.7 0.0 collective-permute-done.3
  58.8 0.7 maximum_select_fusion.1.above
  59.4 0.0 collective-permute-done.1
  59.4 0.0 collective-permute-done
  59.4 0.7 maximum_select_fusion.below
  60.1 3.5 %near_stats.1.near = f32[8,8,128]{2,1,0:T(8,128)} custom-call(s32[2]{0:T(128)} %pad_add_fusion.place, bf16[8,512,128]{2,1,0:T(8,128)(2,1)} %all_to_all.30.held, bf16[2,256,128]{2,1,0:T(8,128)(2,1)} %maximum_select_fusion.below, bf16[2,256,128]{2,1,0:T(8,128)(2,1)} %maximum_select_fusion.1.above, bf16[8,128,128]{2,1,0:T(8,128)(2,1)} %copy-done), custom_call_target="tpu_custom_call" | custom-call | flops 335544320 | bytes 2097152 | tf_op jit(solution)/shard_map/near_stats/pallas_call | solution.py:264
  63.6 3.2 %all-to-all-done.2 = bf16[8,64,128]{2,1,0:T(8,128)(2,1)S(1)} async-done(((bf16[8,64,128]{2,1,0:T(8,128)(2,1)}), bf16[8,64,128]{2,1,0:T(8,128)(2,1)S(1)}, u32[]{:S(2)}, u32[]{:S(2)}) %all-to-all-start.2) | async-done | bytes 131104 | tf_op jit(solution)/shard_map/all_to_all | solution.py:313
  66.8 0.7 copy-done.2
  67.4 3.3 %level_two.1 = (f32[8,8,128]{2,1,0:T(8,128)}, bf16[16,32,128]{2,1,0:T(8,128)(2,1)}) custom-call(s32[2]{0:T(128)} %pad_add_fusion.place, bf16[8,512,128]{2,1,0:T(8,128)(2,1)} %all_to_all.30.held, bf16[16,32,128]{2,1,0:T(8,128)(2,1)} %bitcast.28, f32[8,8,128]{2,1,0:T(8,128)} %near_stats.1.near), custom_call_target="tpu_custom_call" | custom-call | tf_op jit(solution)/shard_map/level_two/pallas_call | solution.py:264
  70.7 3.5 %all-to-all-start.3 = ((bf16[8,64,128]{2,1,0:T(8,128)(2,1)}), bf16[8,64,128]{2,1,0:T(8,128)(2,1)S(1)}, u32[]{:S(2)}, u32[]{:S(2)}) async-start(bf16[8,64,128]{2,1,0:T(8,128)(2,1)} %bitcast.30), calls=%async_computation.3 | async-start | bytes 262144 | tf_op jit(solution)/shard_map/all_to_all | solution.py:328
  74.2 6.7 %attend.1 = (bf16[8,256,128]{2,1,0:T(8,128)(2,1)}, f32[8,256,128]{2,1,0:T(8,128)}, bf16[2,256,128]{2,1,0:T(8,128)(2,1)}, bf16[2,256,128]{2,1,0:T(8,128)(2,1)}, f32[8,128,128]{2,1,0:T(8,128)}) custom-call(s32[2]{0:T(128)} %pad_add_fusion.place, bf16[8,512,128]{2,1,0:T(8,128)(2,1)} %all_to_all.30.held, bf16[2,256,128]{2,1,0:T(8,128)(2,1)} %maximum_select_fusion.below, ...), custom_call_target="tpu_custom_call" | custom-call | flops 1409286144 | bytes 4194304 | tf_op jit(solution)/shard_map/attend/pallas_call | solution.py:264
  80.9 0.9 slice_bitcast_fusion.7
  81.8 2.1 %collective-permute-start.4 = (bf16[256,128]{1,0:T(8,128)(2,1)S(1)}, bf16[256,128]{1,0:T(8,128)(2,1)S(1)}, u32[]{:S(2)}, u32[]{:S(2)}) collective-permute-start(bf16[256,128]{1,0:T(8,128)(2,1)S(1)} %get-tuple-element.24), channel_id=1, source_target_pairs={{0,4},{4,8},{8,12},{12,16},{16,20},{20,24},{24,28},{28,64},{64,68}... | collective-permute-start | bytes 196616 | tf_op jit(solution)/shard_map/ppermute | solution.py:291
  83.9 4.3 %collective-permute-start.5 = (bf16[256,128]{1,0:T(8,128)(2,1)S(1)}, bf16[256,128]{1,0:T(8,128)(2,1)S(1)}, u32[]{:S(2)}, u32[]{:S(2)}) collective-permute-start(bf16[256,128]{1,0:T(8,128)(2,1)S(1)} %get-tuple-element.25), channel_id=1, source_target_pairs={{0,4},{4,8},{8,12},{12,16},{16,20},{20,24},{24,28},{28,0},{64,68},... | collective-permute-start | bytes 196616 | tf_op jit(solution)/shard_map/ppermute | solution.py:291
  88.2 0.0 all-to-all-done.3.arrived
  88.2 0.0 copy-start.3
  88.3 0.6 copy-done.3
  88.9 1.8 %merge.1 = bf16[8,128,128]{2,1,0:T(8,128)(2,1)} custom-call(f32[8,128,128]{2,1,0:T(8,128)} %get-tuple-element.16.part_one, bf16[8,64,128]{2,1,0:T(8,128)(2,1)} %copy-done.3), custom_call_target="tpu_custom_call" | custom-call | tf_op jit(solution)/shard_map/merge/pallas_call | solution.py:264
  90.7 4.7 %all-to-all-start.4 = ((bf16[8,128,128]{2,1,0:T(8,128)(2,1)}), bf16[8,128,128]{2,1,0:T(8,128)(2,1)S(1)}, u32[]{:S(2)}, u32[]{:S(2)}) async-start(bf16[8,128,128]{2,1,0:T(8,128)(2,1)} %merge.1), calls=%async_computation.4 | async-start | bytes 524288 | tf_op jit(solution)/shard_map/all_to_all | solution.py:352
  95.5 4.6 %collective-permute-start.6 = (bf16[256,128]{1,0:T(8,128)(2,1)S(1)}, bf16[256,128]{1,0:T(8,128)(2,1)S(1)}, u32[]{:S(2)}, u32[]{:S(2)}) collective-permute-start(bf16[256,128]{1,0:T(8,128)(2,1)S(1)} %get-tuple-element.22), channel_id=1, source_target_pairs={{0,28},{4,0},{8,4},{12,8},{16,12},{20,16},{24,20},{28,24},{64,92},... | collective-permute-start | bytes 196616 | tf_op jit(solution)/shard_map/ppermute | solution.py:291
  100.0 1.3 collective-permute-start.7
  101.3 0.0 collective-permute-done.4
  101.3 0.0 collective-permute-done.5
  101.4 0.7 maximum_select_fusion.2.from_below
  102.0 0.0 collective-permute-done.6
  102.0 5.4 %collective-permute-done.7 = bf16[256,128]{1,0:T(8,128)(2,1)S(1)} collective-permute-done((bf16[256,128]{1,0:T(8,128)(2,1)S(1)}, bf16[256,128]{1,0:T(8,128)(2,1)S(1)}, u32[]{:S(2)}, u32[]{:S(2)}) %collective-permute-start.7) | collective-permute-done | bytes 65568 | tf_op jit(solution)/shard_map/ppermute | solution.py:291
  107.4 0.7 maximum_select_fusion.3.from_above
  108.1 0.0 all-to-all-done.4.arrived
  108.1 0.7 copy-done.1
  108.8 2.7 %finish.1 = bf16[8,512,128]{2,1,0:T(8,128)(2,1)} custom-call(bf16[8,256,128]{2,1,0:T(8,128)(2,1)} %get-tuple-element.12.answer, f32[8,256,128]{2,1,0:T(8,128)} %get-tuple-element.13.fine, bf16[2,256,128]{2,1,0:T(8,128)(2,1)} %maximum_select_fusion.2.from_below, bf16[2,256,128]{2,1,0:T(8,128)(2,1)} %maximum_select_fusion.3.from_above, ...), custom_call_target="tpu_custom_call" | custom-call | tf_op jit(solution)/shard_map/finish/pallas_call | solution.py:264
  111.5 22.7 %all_to_all.31.packed = bf16[8,512,128]{2,1,0:T(8,128)(2,1)} all-to-all(bf16[8,512,128]{2,1,0:T(8,128)(2,1)} %finish.1), channel_id=1, replica_groups=mesh['y'=8,'core'=2,'z'=8,'x'=4] {'core','x'}, dimensions={0} | all-to-all | bytes 2097152 | tf_op jit(solution)/shard_map/all_to_all | solution.py:356
  134.1 2.5 %unpack.1 = (bf16[128,1024]{1,0:T(8,128)(2,1)}, bf16[128,1024]{1,0:T(8,128)(2,1)}, bf16[128,1024]{1,0:T(8,128)(2,1)}, bf16[128,1024]{1,0:T(8,128)(2,1)}) custom-call(bf16[8,512,128]{2,1,0:T(8,128)(2,1)} %all_to_all.31.packed), custom_call_target="tpu_custom_call" | custom-call | tf_op jit(solution)/shard_map/unpack/pallas_call | solution.py:264
  (5 shorter events, 0.0 us)
Async XLA Ops:
  31.2 18.2 %all-to-all-start.1 = ((bf16[8,128,128]{2,1,0:T(8,128)(2,1)}), bf16[8,128,128]{2,1,0:T(8,128)(2,1)S(1)}, u32[]{:S(2)}, u32[]{:S(2)}) async-start(bf16[8,128,128]{2,1,0:T(8,128)(2,1)} %coarsen_one.1), calls=%async_computation.1 | async-start | bytes 524288 | tf_op jit(solution)/shard_map/all_to_all | solution.py:308
  37.0 21.8 %collective-permute-start.2 = (bf16[256,128]{1,0:T(8,128)(2,1)S(1)}, bf16[256,128]{1,0:T(8,128)(2,1)S(1)}, u32[]{:S(2)}, u32[]{:S(2)}) collective-permute-start(bf16[256,128]{1,0:T(8,128)(2,1)S(1)} %get-tuple-element.18), channel_id=1, source_target_pairs={{0,28},{4,0},{8,4},{12,8},{16,12},{20,16},{24,20},{28,24},{64,92},... | collective-permute-start | bytes 196616 | tf_op jit(solution)/shard_map/ppermute | solution.py:291
  41.6 17.2 %collective-permute-start.3 = (bf16[256,128]{1,0:T(8,128)(2,1)S(1)}, bf16[256,128]{1,0:T(8,128)(2,1)S(1)}, u32[]{:S(2)}, u32[]{:S(2)}) collective-permute-start(bf16[256,128]{1,0:T(8,128)(2,1)S(1)} %get-tuple-element.19), channel_id=1, source_target_pairs={{4,0},{8,4},{12,8},{16,12},{20,16},{24,20},{28,24},{64,28},{68,64}... | collective-permute-start | bytes 196616 | tf_op jit(solution)/shard_map/ppermute | solution.py:291
  43.5 16.0 %collective-permute-start.1 = (bf16[256,128]{1,0:T(8,128)(2,1)S(1)}, bf16[256,128]{1,0:T(8,128)(2,1)S(1)}, u32[]{:S(2)}, u32[]{:S(2)}) collective-permute-start(bf16[256,128]{1,0:T(8,128)(2,1)S(1)} %get-tuple-element.20), channel_id=1, source_target_pairs={{0,4},{4,8},{8,12},{12,16},{16,20},{20,24},{24,28},{28,0},{64,68},... | collective-permute-start | bytes 196616 | tf_op jit(solution)/shard_map/ppermute | solution.py:291
  47.4 12.0 %collective-permute-start = (bf16[256,128]{1,0:T(8,128)(2,1)S(1)}, bf16[256,128]{1,0:T(8,128)(2,1)S(1)}, u32[]{:S(2)}, u32[]{:S(2)}) collective-permute-start(bf16[256,128]{1,0:T(8,128)(2,1)S(1)} %get-tuple-element.21), channel_id=1, source_target_pairs={{0,4},{4,8},{8,12},{12,16},{16,20},{20,24},{24,28},{28,64},{64,68}... | collective-permute-start | bytes 196616 | tf_op jit(solution)/shard_map/ppermute | solution.py:291
  49.4 0.7 copy-start
  51.9 14.9 %all-to-all-start.2 = ((bf16[8,64,128]{2,1,0:T(8,128)(2,1)}), bf16[8,64,128]{2,1,0:T(8,128)(2,1)S(1)}, u32[]{:S(2)}, u32[]{:S(2)}) async-start(bf16[8,64,128]{2,1,0:T(8,128)(2,1)} %coarsen_two.1), calls=%async_computation.2 | async-start | bytes 262144 | tf_op jit(solution)/shard_map/all_to_all | solution.py:313
  66.8 0.7 copy-start.2
  70.7 17.5 %all-to-all-start.3 = ((bf16[8,64,128]{2,1,0:T(8,128)(2,1)}), bf16[8,64,128]{2,1,0:T(8,128)(2,1)S(1)}, u32[]{:S(2)}, u32[]{:S(2)}) async-start(bf16[8,64,128]{2,1,0:T(8,128)(2,1)} %bitcast.30), calls=%async_computation.3 | async-start | bytes 262144 | tf_op jit(solution)/shard_map/all_to_all | solution.py:328
  81.8 19.6 %collective-permute-start.4 = (bf16[256,128]{1,0:T(8,128)(2,1)S(1)}, bf16[256,128]{1,0:T(8,128)(2,1)S(1)}, u32[]{:S(2)}, u32[]{:S(2)}) collective-permute-start(bf16[256,128]{1,0:T(8,128)(2,1)S(1)} %get-tuple-element.24), channel_id=1, source_target_pairs={{0,4},{4,8},{8,12},{12,16},{16,20},{20,24},{24,28},{28,64},{64,68}... | collective-permute-start | bytes 196616 | tf_op jit(solution)/shard_map/ppermute | solution.py:291
  83.9 17.4 %collective-permute-start.5 = (bf16[256,128]{1,0:T(8,128)(2,1)S(1)}, bf16[256,128]{1,0:T(8,128)(2,1)S(1)}, u32[]{:S(2)}, u32[]{:S(2)}) collective-permute-start(bf16[256,128]{1,0:T(8,128)(2,1)S(1)} %get-tuple-element.25), channel_id=1, source_target_pairs={{0,4},{4,8},{8,12},{12,16},{16,20},{20,24},{24,28},{28,0},{64,68},... | collective-permute-start | bytes 196616 | tf_op jit(solution)/shard_map/ppermute | solution.py:291
  88.2 0.7 copy-start.3
  90.7 4.7 %copy-start.4 = (bf16[2,256,128]{2,1,0:T(8,128)(2,1)S(1)}, bf16[2,256,128]{2,1,0:T(8,128)(2,1)}, u32[]{:S(2)}) copy-start(bf16[2,256,128]{2,1,0:T(8,128)(2,1)} %get-tuple-element.15) | copy-start | bytes 393220
  90.7 17.4 %all-to-all-start.4 = ((bf16[8,128,128]{2,1,0:T(8,128)(2,1)}), bf16[8,128,128]{2,1,0:T(8,128)(2,1)S(1)}, u32[]{:S(2)}, u32[]{:S(2)}) async-start(bf16[8,128,128]{2,1,0:T(8,128)(2,1)} %merge.1), calls=%async_computation.4 | async-start | bytes 524288 | tf_op jit(solution)/shard_map/all_to_all | solution.py:352
  95.5 6.6 %collective-permute-start.6 = (bf16[256,128]{1,0:T(8,128)(2,1)S(1)}, bf16[256,128]{1,0:T(8,128)(2,1)S(1)}, u32[]{:S(2)}, u32[]{:S(2)}) collective-permute-start(bf16[256,128]{1,0:T(8,128)(2,1)S(1)} %get-tuple-element.22), channel_id=1, source_target_pairs={{0,28},{4,0},{8,4},{12,8},{16,12},{20,16},{24,20},{28,24},{64,92},... | collective-permute-start | bytes 196616 | tf_op jit(solution)/shard_map/ppermute | solution.py:291
  100.0 7.4 %collective-permute-start.7 = (bf16[256,128]{1,0:T(8,128)(2,1)S(1)}, bf16[256,128]{1,0:T(8,128)(2,1)S(1)}, u32[]{:S(2)}, u32[]{:S(2)}) collective-permute-start(bf16[256,128]{1,0:T(8,128)(2,1)S(1)} %get-tuple-element.23), channel_id=1, source_target_pairs={{4,0},{8,4},{12,8},{16,12},{20,16},{24,20},{28,24},{64,28},{68,64}... | collective-permute-start | bytes 196616 | tf_op jit(solution)/shard_map/ppermute | solution.py:291
  108.1 0.7 copy-start.1

commit v3 on v2

v3 whole, which is shorter than its diff:
```python
import jax
import jax.numpy as jnp
from jax import lax
from jax.experimental import pallas as pl
from jax.experimental.pallas import tpu as pltpu
from jax.sharding import Mesh
from jax.sharding import PartitionSpec as P

HEADS = 8
HEAD_DIM = 128
BLOCK = 128
COARSE = 16
ONE_ROWS = BLOCK // COARSE
N_Y, N_CORE, N_Z, N_X = 8, 2, 8, 4
AXES = ("y", "core", "z", "x")
GROUP = ("y", "core")
LINE = ("y", "core", "z")
N_HEAD = HEADS // N_X
N_UNIT = N_X * N_HEAD
N_CTX = N_Z * N_X
N_GROUP = N_Y * N_CORE
GROUP_ROWS = N_CTX * ONE_ROWS
TWO_ROWS = GROUP_ROWS // COARSE
LEVEL_TWO = N_GROUP * TWO_ROWS
FEATURES = HEADS * HEAD_DIM
FACTOR = HEAD_DIM ** (-0.5)
SHUT = -1e30
LIMIT = 24 << 20
F32 = jnp.float32
BF16 = jnp.bfloat16
VMEM = pl.BlockSpec(memory_space=pltpu.VMEM)
SMEM = pl.BlockSpec(memory_space=pltpu.SMEM)
QUERY, KEY, VALUE, COT = (slice(i * BLOCK, (i + 1) * BLOCK) for i in range(4))
PAIR = slice(BLOCK, 3 * BLOCK)


def dot_nt(left, right):
    return lax.dot_general(left, right, (((1,), (1,)), ((), ())), preferred_element_type=F32)


def dot_nn(left, right):
    return lax.dot_general(left, right, (((1,), (0,)), ((), ())), preferred_element_type=F32)


def dot_tn(left, right):
    return lax.dot_general(left, right, (((0,), (0,)), ((), ())), preferred_element_type=F32)


def iota(shape, dim):
    return lax.broadcasted_iota(jnp.int32, shape, dim)


def lanes_of(head):
    return slice(head * HEAD_DIM, (head + 1) * HEAD_DIM)


def pack_kernel(queries, keys, values, cotangent, packed):
    for head in range(HEADS):
        for rows, source in ((QUERY, queries), (KEY, keys), (VALUE, values), (COT, cotangent)):
            packed[head, rows] = source[:, lanes_of(head)]


def coarsen_one_kernel(held, spread):
    row, token = iota((2 * ONE_ROWS, BLOCK), 0), iota((2 * ONE_ROWS, BLOCK), 1)
    pick_k = jnp.where(row == token // COARSE, 1.0, 0.0).astype(BF16)
    pick_v = jnp.where(row - ONE_ROWS == token // COARSE, 1.0, 0.0).astype(BF16)
    pick = jnp.concatenate([pick_k, pick_v], axis=1)
    for unit in range(N_UNIT):
        own = (dot_nn(pick, held[unit, PAIR]) * 0.25).astype(BF16)
        rows = slice(unit * 2 * ONE_ROWS, (unit + 1) * 2 * ONE_ROWS)
        for copy in range(N_Z):
            spread[copy, rows] = own


def coarsen_two_kernel(level_one, spread):
    width = N_UNIT * 2 * ONE_ROWS
    shape = (N_HEAD * 2 * TWO_ROWS, N_Z * width)
    row, source = iota(shape, 0), iota(shape, 1)
    z, rest = source // width, source % width
    unit, kind = rest // (2 * ONE_ROWS), (rest % (2 * ONE_ROWS)) // ONE_ROWS
    x, head = unit // N_HEAD, unit % N_HEAD
    target = (head * 2 + kind) * TWO_ROWS + (z * N_X + x) // 2
    pick = jnp.where(row == target, 1.0, 0.0).astype(BF16)
    own = dot_nn(pick, level_one[...].reshape(N_Z * width, HEAD_DIM))
    own = (own * 0.25).astype(BF16)
    for copy in range(N_GROUP):
        spread[copy] = own


def split_one(level_one, head):
    wide = level_one[...].reshape(N_CTX, N_HEAD, 2 * ONE_ROWS, HEAD_DIM)[:, head].astype(F32)
    key = wide[:, :ONE_ROWS].reshape(GROUP_ROWS, HEAD_DIM).astype(BF16)
    value = wide[:, ONE_ROWS:].reshape(GROUP_ROWS, HEAD_DIM).astype(BF16)
    return key, value


def split_two(level_two, head):
    first = head * 2 * TWO_ROWS
    key = level_two[:, first : first + TWO_ROWS].reshape(LEVEL_TWO, HEAD_DIM)
    value = level_two[:, first + TWO_ROWS : first + 2 * TWO_ROWS].reshape(LEVEL_TWO, HEAD_DIM)
    return key, value


def near_bias(place, x):
    group, z = place[0], place[1]
    shape = (BLOCK, HEAD_DIM)
    low, high = jnp.zeros(shape, F32), jnp.zeros(shape, F32)
    if x == 0:
        low = jnp.full(shape, jnp.where((group == 0) & (z == 0), SHUT, 0.0).astype(F32))
    if x == N_X - 1:
        last = (group == N_GROUP - 1) & (z == N_Z - 1)
        high = jnp.full(shape, jnp.where(last, SHUT, 0.0).astype(F32))
    row = iota((GROUP_ROWS, HEAD_DIM), 0) // ONE_ROWS
    one = jnp.where(jnp.abs(row - (z * N_X + x)) <= 1, SHUT, 0.0).astype(F32)
    return [low, jnp.zeros(shape, F32), high, one]


def two_bias(place):
    row = iota((LEVEL_TWO, HEAD_DIM), 0) // TWO_ROWS
    return jnp.where(row == place[0], SHUT, 0.0).astype(F32)


def near_window(held, below, above, x, head, kind):
    rows = slice((1 + kind) * BLOCK, (2 + kind) * BLOCK)
    halo = slice(kind * BLOCK, (kind + 1) * BLOCK)
    unit = x * N_HEAD + head
    low = below[head, halo] if x == 0 else held[unit - N_HEAD, rows]
    high = above[head, halo] if x == N_X - 1 else held[unit + N_HEAD, rows]
    return [low, held[unit, rows], high]


def near_kernel(place, held, below, above, level_one, stats):
    for head in range(N_HEAD):
        one_k, one_v = split_one(level_one, head)
        for x in range(N_X):
            unit = x * N_HEAD + head
            all_k = jnp.concatenate(near_window(held, below, above, x, head, 0) + [one_k], axis=0)
            all_v = jnp.concatenate(near_window(held, below, above, x, head, 1) + [one_v], axis=0)
            bias = jnp.concatenate(near_bias(place, x), axis=0)
            scores = dot_nt(all_k, held[unit, QUERY]) * FACTOR + bias
            highest = jnp.max(scores, axis=0, keepdims=True)
            weights = jnp.exp(scores - highest)
            slopes = dot_nt(all_v, held[unit, COT])
            stats[unit, 0:1] = highest
            stats[unit, 1:2] = jnp.sum(weights, axis=0, keepdims=True)
            stats[unit, 2:3] = jnp.sum(weights * slopes, axis=0, keepdims=True)


def two_kernel(place, held, level_two, near, stats, part_two, chances, dscores):
    bias = two_bias(place)
    tokens = N_X * BLOCK
    for head in range(N_HEAD):
        key, value = split_two(level_two, head)
        for x in range(N_X):
            unit = x * N_HEAD + head
            scores = dot_nt(key, held[unit, QUERY]) * FACTOR + bias
            slopes = dot_nt(value, held[unit, COT])
            near_highest = near[unit, 0:1]
            highest = jnp.maximum(near_highest, jnp.max(scores, axis=0, keepdims=True))
            scale = jnp.exp(near_highest - highest)
            weights = jnp.exp(scores - highest)
            total = near[unit, 1:2] * scale + jnp.sum(weights, axis=0, keepdims=True)
            inverse = 1.0 / total
            centre = near[unit, 2:3] * scale + jnp.sum(weights * slopes, axis=0, keepdims=True)
            centre = centre * inverse
            stats[unit, 0:1] = highest
            stats[unit, 1:2] = inverse
            stats[unit, 2:3] = centre
            chance = weights * inverse
            dscores[head, :, lanes_of(x)] = (chance * (slopes - centre) * FACTOR).astype(BF16)
            chances[head, :, lanes_of(x)] = chance.astype(BF16)
        queries = jnp.concatenate([held[x * N_HEAD + head, QUERY] for x in range(N_X)], axis=0)
        cots = jnp.concatenate([held[x * N_HEAD + head, COT] for x in range(N_X)], axis=0)
        grad_k = dot_nn(dscores[head], queries).reshape(N_GROUP, TWO_ROWS, HEAD_DIM)
        grad_v = dot_nn(chances[head], cots).reshape(N_GROUP, TWO_ROWS, HEAD_DIM)
        rows = slice(head * 2 * TWO_ROWS, (head + 1) * 2 * TWO_ROWS)
        part_two[:, rows] = jnp.concatenate([grad_k, grad_v], axis=1).astype(BF16)


def attend_kernel(
    place, held, below, above, level_one, level_two, stats,
    answer, fine, grad_below, grad_above, part_one, window, ones,
):
    near = 3 * BLOCK
    seen = near + GROUP_ROWS
    shut = two_bias(place)
    for head in range(N_HEAD):
        one_k, one_v = split_one(level_one, head)
        two_k, two_v = split_two(level_two, head)
        window[head] = jnp.zeros_like(window[head])
        for x in range(N_X):
            unit = x * N_HEAD + head
            query, cot = held[unit, QUERY], held[unit, COT]
            near_k = near_window(held, below, above, x, head, 0)
            near_v = near_window(held, below, above, x, head, 1)
            all_k = jnp.concatenate(near_k + [one_k, two_k], axis=0)
            all_v = jnp.concatenate(near_v + [one_v, two_v], axis=0)
            bias = jnp.concatenate(near_bias(place, x) + [shut], axis=0)
            scores = dot_nt(all_k, query) * FACTOR + bias
            chance = jnp.exp(scores - stats[unit, 0:1]) * stats[unit, 1:2]
            slopes = dot_nt(all_v, cot)
            dscore = (chance * (slopes - stats[unit, 2:3]) * FACTOR).astype(BF16)
            chance = chance.astype(BF16)
            answer[unit, :BLOCK] = dot_tn(chance, all_v).astype(BF16)
            answer[unit, BLOCK:] = dot_tn(dscore, all_k).astype(BF16)
            for kind, (left, right) in enumerate(((dscore, query), (chance, cot))):
                grad = dot_nn(left[:seen], right)
                window[head, kind, x * BLOCK : (x + 3) * BLOCK] += grad[:near]
                ones[head, kind] = grad[near:] if x == 0 else ones[head, kind] + grad[near:]
        for kind in range(2):
            rows = slice(kind * BLOCK, (kind + 1) * BLOCK)
            grad_below[head, rows] = window[head, kind, :BLOCK].astype(BF16)
            grad_above[head, rows] = window[head, kind, (N_X + 1) * BLOCK :].astype(BF16)
            for x in range(N_X):
                fine[x * N_HEAD + head, rows] = window[head, kind, (x + 1) * BLOCK : (x + 2) * BLOCK]
        both = [ones[head, kind].reshape(N_CTX, ONE_ROWS, HEAD_DIM) for kind in range(2)]
        both = jnp.concatenate(both, axis=1)
        for ctx in range(N_CTX):
            first = ((ctx % N_X) * N_HEAD + head) * 2 * ONE_ROWS
            part_one[ctx // N_X, first : first + 2 * ONE_ROWS] = both[ctx]


def merge_kernel(part_one, arrived, merged):
    two = jnp.sum(arrived[...].astype(F32), axis=0) * 0.25
    for ctx in range(N_CTX):
        z, x = ctx // N_X, ctx % N_X
        for head in range(N_HEAD):
            low = head * 2 * TWO_ROWS + ctx // 2
            high = low + TWO_ROWS
            first = (x * N_HEAD + head) * 2 * ONE_ROWS
            rows = slice(first, first + 2 * ONE_ROWS)
            carried = jnp.concatenate(
                [
                    jnp.broadcast_to(two[low : low + 1], (ONE_ROWS, HEAD_DIM)),
                    jnp.broadcast_to(two[high : high + 1], (ONE_ROWS, HEAD_DIM)),
                ],
                axis=0,
            )
            merged[z, rows] = (part_one[z, rows] + carried).astype(BF16)


def finish_kernel(answer, fine, from_below, from_above, arrived, result):
    owned = jnp.sum(arrived[...].astype(F32), axis=0) * 0.25
    for unit in range(N_UNIT):
        x, head = unit // N_HEAD, unit % N_HEAD
        result[unit, : 2 * BLOCK] = answer[unit]
        for kind in range(2):
            rows = slice(kind * BLOCK, (kind + 1) * BLOCK)
            total = fine[unit, rows]
            if x == 0:
                total = total + from_below[head, rows].astype(F32)
            if x == N_X - 1:
                total = total + from_above[head, rows].astype(F32)
            first = (2 * unit + kind) * ONE_ROWS
            carried = owned[first : first + ONE_ROWS].reshape(ONE_ROWS, 1, HEAD_DIM)
            total = total.reshape(ONE_ROWS, COARSE, HEAD_DIM) + carried
            out = slice((2 + kind) * BLOCK, (3 + kind) * BLOCK)
            result[unit, out] = total.reshape(BLOCK, HEAD_DIM).astype(BF16)


def unpack_kernel(packed, output, grad_q, grad_k, grad_v):
    for head in range(HEADS):
        for place, out in enumerate((output, grad_q, grad_k, grad_v)):
            out[:, lanes_of(head)] = packed[head, place * BLOCK : (place + 1) * BLOCK]


def shape_of(shape, dtype):
    return jax.ShapeDtypeStruct(shape, dtype)


def run(kernel, name, out_shape, *args, scratch=(), place=False, cost=None):
    several = isinstance(out_shape, tuple)
    specs = [SMEM if place and i == 0 else VMEM for i in range(len(args))]
    return pl.pallas_call(
        kernel,
        out_shape=out_shape,
        in_specs=specs,
        out_specs=(VMEM,) * len(out_shape) if several else VMEM,
        scratch_shapes=list(scratch),
        compiler_params=pltpu.CompilerParams(vmem_limit_bytes=LIMIT),
        cost_estimate=cost,
        name=name,
    )(*args)


def shifted(value, steps):
    count = N_GROUP * N_Z
    first, last = max(0, -steps), min(count, count - steps)
    return lax.ppermute(value, LINE, [(s, s + steps) for s in range(first, last)])


def local(queries, keys, values, cotangent):
    group, z = lax.axis_index(GROUP), lax.axis_index("z")
    place = jnp.stack([group, z]).astype(jnp.int32)
    wide = (HEADS, 4 * BLOCK, HEAD_DIM)
    one = (N_Z, N_UNIT * 2 * ONE_ROWS, HEAD_DIM)
    two = (N_GROUP, N_HEAD * 2 * TWO_ROWS, HEAD_DIM)
    halo = (N_HEAD, 2 * BLOCK, HEAD_DIM)
    tokens = N_UNIT * BLOCK

    packed = run(pack_kernel, "pack", shape_of(wide, BF16), queries, keys, values, cotangent)
    held = lax.all_to_all(packed, "x", 0, 0, tiled=True)

    spread = run(coarsen_one_kernel, "coarsen_one", shape_of(one, BF16), held)
    level_one = lax.all_to_all(spread, "z", 0, 0, tiled=True)
    below = shifted(held[-N_HEAD:, PAIR], 1)
    above = shifted(held[:N_HEAD, PAIR], -1)

    spread = run(coarsen_two_kernel, "coarsen_two", shape_of(two, BF16), level_one)
    level_two = lax.all_to_all(spread, GROUP, 0, 0, tiled=True)

    stats_shape = shape_of((N_UNIT, 8, HEAD_DIM), F32)
    near = run(
        near_kernel, "near_stats", stats_shape, place, held, below, above, level_one, place=True,
        cost=pl.CostEstimate(
            flops=4 * tokens * 640 * HEAD_DIM, bytes_accessed=2 << 20, transcendentals=640 * tokens
        ),
    )
    stats, part_two = run(
        two_kernel, "level_two", (stats_shape, shape_of(two, BF16)),
        place, held, level_two, near, place=True,
        scratch=[pltpu.VMEM((N_HEAD, LEVEL_TWO, N_X * BLOCK), BF16)] * 2,
    )
    arrived_two = lax.all_to_all(part_two, GROUP, 0, 0, tiled=True)

    answer, fine, grad_below, grad_above, part_one = run(
        attend_kernel, "attend",
        (
            shape_of((N_UNIT, 2 * BLOCK, HEAD_DIM), BF16),
            shape_of((N_UNIT, 2 * BLOCK, HEAD_DIM), F32),
            shape_of(halo, BF16),
            shape_of(halo, BF16),
            shape_of(one, F32),
        ),
        place, held, below, above, level_one, level_two, stats, place=True,
        scratch=[
            pltpu.VMEM((N_HEAD, 2, (N_X + 2) * BLOCK, HEAD_DIM), F32),
            pltpu.VMEM((N_HEAD, 2, GROUP_ROWS, HEAD_DIM), F32),
        ],
        cost=pl.CostEstimate(
            flops=12 * tokens * 896 * HEAD_DIM, bytes_accessed=4 << 20, transcendentals=896 * tokens
        ),
    )
    merged = run(merge_kernel, "merge", shape_of(one, BF16), part_one, arrived_two)
    merged, grad_below, grad_above = lax.optimization_barrier((merged, grad_below, grad_above))
    arrived_one = lax.all_to_all(merged, "z", 0, 0, tiled=True)
    from_below = shifted(grad_above, 1)
    from_above = shifted(grad_below, -1)
    result = run(
        finish_kernel, "finish", shape_of(wide, BF16), answer, fine, from_below, from_above, arrived_one
    )
    arrived = lax.all_to_all(result, "x", 0, 0, tiled=True)
    return run(unpack_kernel, "unpack", (shape_of((BLOCK, FEATURES), BF16),) * 4, arrived)


def solution(mesh):
    rows = Mesh(mesh.devices.reshape(N_Y, N_CORE, N_Z, N_X), AXES)
    placed = P(AXES, None)
    return jax.shard_map(
        local,
        mesh=rows,
        in_specs=(placed,) * 4,
        out_specs=(placed,) * 4,
        check_vma=False,
    )
```

time: 138 us -> 126 us (0.913)
  Pallas kernels: 26.7 us -> 12.5 us
  starting transfers between devices: 44 us -> 35.3 us
  blocking collectives: 48.7 us -> 55 us
  waiting for transfers between devices: 8.54 us -> 13.5 us
  local copies, waits for them, and re-layouts: 4.55 us -> 8.2 us
  other arithmetic: 3.27 us -> 0.08 us
    pallas_call x9, Pallas kernels: 26.7 us -> 12.5 us  [run(): pl.pallas_call(kernel, out_shape=out_shape, in_specs=specs, out_specs=(VM...]
    ppermute x8 -> x4, starting transfers between devices: 24.1 us -> 12.1 us  [shifted(): lax.ppermute(value, LINE, [(s, s + steps) for s in range(first, last)])]
    all_to_all x2 -> x3, blocking collectives: 48.7 us -> 55 us  [the longest x1 22.9 us: local(): level_one = lax.all_to_all(spread, 'z', 0, 0, tiled=True)]
    unnamed x10 -> x28, local copies, waits for them, and re-layouts: 2.71 us -> 8.18 us
    all_to_all x3 -> x2, starting transfers between devices: 15.2 us -> 19.7 us  [the longest x1 10.6 us: local(): level_two = lax.all_to_all(spread, GROUP, 0, 0, tiled=True)]
    ppermute x8 -> x4, waiting for transfers between devices: 5.38 us -> 8.85 us  [shifted(): lax.ppermute(value, LINE, [(s, s + steps) for s in range(first, last)])]
    select_n x4 -> x0, other arithmetic: 2.68 us -> none  [exchange(): jnp.where(swap, jnp.stack([second, first]), jnp.stack([first, second]))]
    squeeze x3 -> x0, local copies, waits for them, and re-layouts: 1.84 us -> none  [the longest x1 0.95 us: local(): above = exchange([held[0, PAIR], held[N_X, PAIR]], FALL, z == N_Z - 1)]
  transfers between devices with their start and end apart: 12 -> 7, of which waited for: 2 -> 6; matrix products, arithmetic and copies ran while one was open for 4% -> 0% of each run, Pallas kernels for 10% -> 5%
where the time goes in v3:
time: 126 us; the launch traced here: 125 us
  blocking collectives  55 us (44%)
  starting transfers between devices  35.3 us (28%)
  waiting for transfers between devices  13.5 us (11%)
  Pallas kernels  12.5 us (10%)
  local copies, waits for them, and re-layouts  8.2 us (7%)
    all_to_all x1, blocking collectives, local(): level_one = lax.all_to_all(spread, 'z', 0, 0, tiled=True)  22.9 us
    all_to_all x1, blocking collectives, local(): arrived = lax.all_to_all(result, 'x', 0, 0, tiled=True)  17.1 us
    all_to_all x1, blocking collectives, local(): held = lax.all_to_all(packed, 'x', 0, 0, tiled=True)  15.1 us
    pallas_call x9, Pallas kernels, run(): pl.pallas_call(kernel, out_shape=out_shape, in_specs=specs, out_specs=(VM...  12.5 us
    ppermute x4, starting transfers between devices, shifted(): lax.ppermute(value, LINE, [(s, s + steps) for s in range(first, last)])  12.1 us
    all_to_all x1, starting transfers between devices, local(): level_two = lax.all_to_all(spread, GROUP, 0, 0, tiled=True)  10.6 us
    all_to_all x1, starting transfers between devices, local(): arrived_two = lax.all_to_all(part_two, GROUP, 0, 0, tiled=True)  9.08 us
    ppermute x4, waiting for transfers between devices, shifted(): lax.ppermute(value, LINE, [(s, s + steps) for s in range(first, last)])  8.85 us
  transfers between devices with their start and end apart: 7, of which 6 were waited for; matrix products, arithmetic and copies ran while one was open for 0% of the time, Pallas kernels for 5%

profile of v3, /device:TPU:1, one launch (start us, length us, event | category | flops | bytes accessed | tf_op | source)
XLA Modules:
  0.0 125.4 jit_solution(8358572248851503824)
XLA Ops:
  0.6 0.0 copy-start.2
  0.6 0.9 copy-done.2
  1.6 0.0 copy-start.3
  1.6 0.9 copy-done.3
  2.5 0.0 copy-start.4
  2.5 0.9 copy-done.4
  3.5 0.0 copy-start.5
  3.5 0.9 copy-done.5
  4.4 0.2 pack.1
  4.6 15.1 %all_to_all.30.held = bf16[8,512,128]{2,1,0:T(8,128)(2,1)S(1)} all-to-all(bf16[8,512,128]{2,1,0:T(8,128)(2,1)S(1)} %pack.1), channel_id=1, replica_groups=mesh['y'=8,'core'=2,'z'=8,'x'=4] {'x'}, dimensions={0} | all-to-all | bytes 2097152 | tf_op jit(solution)/shard_map/all_to_all | solution.py:302
  19.7 0.2 coarsen_one.1
  19.9 22.9 %all_to_all.31.level_one = bf16[8,128,128]{2,1,0:T(8,128)(2,1)S(1)} all-to-all(bf16[8,128,128]{2,1,0:T(8,128)(2,1)S(1)} %coarsen_one.1), channel_id=1, replica_groups=mesh['y'=8,'core'=2,'z'=8,'x'=4] {'z'}, dimensions={0} | all-to-all | bytes 524288 | tf_op jit(solution)/shard_map/all_to_all | solution.py:305
  42.8 0.9 coarsen_two.1
  43.7 10.6 %all-to-all-start.2 = ((bf16[16,64,128]{2,1,0:T(8,128)(2,1)}), bf16[16,64,128]{2,1,0:T(8,128)(2,1)S(1)}, u32[]{:S(2)}, u32[]{:S(2)}) async-start(bf16[16,64,128]{2,1,0:T(8,128)(2,1)} %coarsen_two.1), calls=%async_computation.2 | async-start | bytes 524288 | tf_op jit(solution)/shard_map/all_to_all | solution.py:310
  54.4 2.2 %collective-permute-start.1 = (bf16[2,256,128]{2,1,0:T(8,128)(2,1)S(1)}, bf16[2,256,128]{2,1,0:T(8,128)(2,1)S(1)}, u32[]{:S(2)}, u32[]{:S(2)}) collective-permute-start(bf16[2,256,128]{2,1,0:T(8,128)(2,1)S(1)} %get-tuple-element.24), channel_id=1, source_target_pairs={{4,0},{8,4},{12,8},{16,12},{20,16},{24,20},{28,24},{32,28},{36,32}... | collective-permute-start | bytes 393224 | tf_op jit(solution)/shard_map/ppermute | solution.py:289
  56.6 3.1 %collective-permute-start = (bf16[2,256,128]{2,1,0:T(8,128)(2,1)S(1)}, bf16[2,256,128]{2,1,0:T(8,128)(2,1)S(1)}, u32[]{:S(2)}, u32[]{:S(2)}) collective-permute-start(bf16[2,256,128]{2,1,0:T(8,128)(2,1)S(1)} %get-tuple-element.25), channel_id=1, source_target_pairs={{0,4},{4,8},{8,12},{12,16},{16,20},{20,24},{24,28},{28,32},{32,36}... | collective-permute-start | bytes 393224 | tf_op jit(solution)/shard_map/ppermute | solution.py:289
  59.7 0.1 pad_add_fusion.place
  59.8 1.6 %collective-permute-done.1.above = bf16[2,256,128]{2,1,0:T(8,128)(2,1)S(1)} collective-permute-done((bf16[2,256,128]{2,1,0:T(8,128)(2,1)S(1)}, bf16[2,256,128]{2,1,0:T(8,128)(2,1)S(1)}, u32[]{:S(2)}, u32[]{:S(2)}) %collective-permute-start.1) | collective-permute-done | bytes 131104 | tf_op jit(solution)/shard_map/ppermute | solution.py:289
  61.3 3.0 %collective-permute-done.below = bf16[2,256,128]{2,1,0:T(8,128)(2,1)S(1)} collective-permute-done((bf16[2,256,128]{2,1,0:T(8,128)(2,1)S(1)}, bf16[2,256,128]{2,1,0:T(8,128)(2,1)S(1)}, u32[]{:S(2)}, u32[]{:S(2)}) %collective-permute-start) | collective-permute-done | bytes 131104 | tf_op jit(solution)/shard_map/ppermute | solution.py:289
  64.3 0.0 copy-start.6
  64.3 1.9 %near_stats.1.near = f32[8,8,128]{2,1,0:T(8,128)S(1)} custom-call(s32[2]{0:T(128)S(1)} %pad_add_fusion.place, bf16[8,512,128]{2,1,0:T(8,128)(2,1)S(1)} %all_to_all.30.held, bf16[2,256,128]{2,1,0:T(8,128)(2,1)S(1)} %collective-permute-done.below, bf16[2,256,128]{2,1,0:T(8,128)(2,1)S(1)} %collective-permute-done.1.above, ...), custom_call_target="tpu_custom_call" | custom-call | flops 335544320 | bytes 2097152 | tf_op jit(solution)/shard_map/near_stats/pallas_call | solution.py:274
  66.3 0.0 copy-done.6
  66.3 0.0 all-to-all-done.2.level_two
  66.3 2.6 %level_two.1 = (f32[8,8,128]{2,1,0:T(8,128)S(1)}, bf16[16,64,128]{2,1,0:T(8,128)(2,1)}) custom-call(s32[2]{0:T(128)S(1)} %pad_add_fusion.place, bf16[8,512,128]{2,1,0:T(8,128)(2,1)S(1)} %all_to_all.30.held, bf16[16,64,128]{2,1,0:T(8,128)(2,1)S(1)} %all-to-all-done.2.level_two, f32[8,8,128]{2,1,0:T(8,128)S(1)} %near_stats.1.near), custom_call_target="tpu_custom_call" | custom-call | tf_op jit(solution)/shard_map/level_two/pallas_call | solution.py:274
  68.9 0.0 copy-start.12
  68.9 0.6 copy-done.12
  69.5 9.1 %all-to-all-start.3 = ((bf16[16,64,128]{2,1,0:T(8,128)(2,1)}), bf16[16,64,128]{2,1,0:T(8,128)(2,1)S(1)}, u32[]{:S(2)}, u32[]{:S(2)}) async-start(bf16[16,64,128]{2,1,0:T(8,128)(2,1)} %get-tuple-element.18), calls=%async_computation.3 | async-start | bytes 524288 | tf_op jit(solution)/shard_map/all_to_all | solution.py:324
  78.6 0.9 copy-done.7
  79.5 0.8 copy-done.13
  80.2 4.5 %attend.1 = (bf16[8,256,128]{2,1,0:T(8,128)(2,1)S(1)}, f32[8,256,128]{2,1,0:T(8,128)S(1)}, bf16[2,256,128]{2,1,0:T(8,128)(2,1)S(1)}, bf16[2,256,128]{2,1,0:T(8,128)(2,1)S(1)}, f32[8,128,128]{2,1,0:T(8,128)S(1)}) custom-call(s32[2]{0:T(128)S(1)} %pad_add_fusion.place, bf16[8,512,128]{2,1,0:T(8,128)(2,1)S(1)} %all_to_all.30.held, ...), custom_call_target="tpu_custom_call" | custom-call | flops 1409286144 | bytes 4194304 | tf_op jit(solution)/shard_map/attend/pallas_call | solution.py:274
  84.7 0.0 copy-start
  84.7 0.8 copy-done
  85.5 0.7 copy-done.8
  86.2 0.7 copy-done.10
  86.8 3.5 %all-to-all-done.3.arrived = bf16[16,64,128]{2,1,0:T(8,128)(2,1)S(1)} async-done(((bf16[16,64,128]{2,1,0:T(8,128)(2,1)}), bf16[16,64,128]{2,1,0:T(8,128)(2,1)S(1)}, u32[]{:S(2)}, u32[]{:S(2)}) %all-to-all-start.3) | async-done | bytes 262176 | tf_op jit(solution)/shard_map/all_to_all | solution.py:324
  90.3 0.8 merge.1
  91.1 3.5 %all-to-all-start.4 = ((bf16[8,128,128]{2,1,0:T(8,128)(2,1)}), bf16[8,128,128]{2,1,0:T(8,128)(2,1)S(1)}, u32[]{:S(2)}, u32[]{:S(2)}) async-start(bf16[8,128,128]{2,1,0:T(8,128)(2,1)} %merge.1), calls=%async_computation.4 | async-start | bytes 524288 | tf_op jit(solution)/shard_map/all_to_all | solution.py:346
  94.6 0.0 copy-done.11
  94.6 3.2 %collective-permute-start.2 = (bf16[2,256,128]{2,1,0:T(8,128)(2,1)S(1)}, bf16[2,256,128]{2,1,0:T(8,128)(2,1)S(1)}, u32[]{:S(2)}, u32[]{:S(2)}) collective-permute-start(bf16[2,256,128]{2,1,0:T(8,128)(2,1)S(1)} %copy-done.11), channel_id=1, source_target_pairs={{0,4},{4,8},{8,12},{12,16},{16,20},{20,24},{24,28},{28,32},{32,36}... | collective-permute-start | bytes 393224 | tf_op jit(solution)/shard_map/ppermute | solution.py:289
  97.9 0.0 copy-done.9
  97.9 3.5 %collective-permute-start.3 = (bf16[2,256,128]{2,1,0:T(8,128)(2,1)S(1)}, bf16[2,256,128]{2,1,0:T(8,128)(2,1)S(1)}, u32[]{:S(2)}, u32[]{:S(2)}) collective-permute-start(bf16[2,256,128]{2,1,0:T(8,128)(2,1)S(1)} %copy-done.9), channel_id=1, source_target_pairs={{4,0},{8,4},{12,8},{16,12},{20,16},{24,20},{28,24},{32,28},{36,32}... | collective-permute-start | bytes 393224 | tf_op jit(solution)/shard_map/ppermute | solution.py:289
  101.4 3.3 %collective-permute-done.2.from_below = bf16[2,256,128]{2,1,0:T(8,128)(2,1)S(1)} collective-permute-done((bf16[2,256,128]{2,1,0:T(8,128)(2,1)S(1)}, bf16[2,256,128]{2,1,0:T(8,128)(2,1)S(1)}, u32[]{:S(2)}, u32[]{:S(2)}) %collective-permute-start.2) | collective-permute-done | bytes 131104 | tf_op jit(solution)/shard_map/ppermute | solution.py:289
  104.7 1.0 collective-permute-done.3.from_above
  105.7 1.2 all-to-all-done.4.arrived
  106.9 0.0 copy-done.1
  106.9 0.2 finish.1
  107.1 17.1 %all_to_all.32.packed = bf16[8,512,128]{2,1,0:T(8,128)(2,1)S(1)} all-to-all(bf16[8,512,128]{2,1,0:T(8,128)(2,1)S(1)} %finish.1), channel_id=1, replica_groups=mesh['y'=8,'core'=2,'z'=8,'x'=4] {'x'}, dimensions={0} | all-to-all | bytes 2097152 | tf_op jit(solution)/shard_map/all_to_all | solution.py:352
  124.2 1.3 unpack.1
  (8 shorter events, 0.0 us)
Async XLA Ops:
  0.6 1.0 copy-start.2
  1.6 0.9 copy-start.3
  2.5 0.9 copy-start.4
  3.5 0.9 copy-start.5
  43.7 22.5 %all-to-all-start.2 = ((bf16[16,64,128]{2,1,0:T(8,128)(2,1)}), bf16[16,64,128]{2,1,0:T(8,128)(2,1)S(1)}, u32[]{:S(2)}, u32[]{:S(2)}) async-start(bf16[16,64,128]{2,1,0:T(8,128)(2,1)} %coarsen_two.1), calls=%async_computation.2 | async-start | bytes 524288 | tf_op jit(solution)/shard_map/all_to_all | solution.py:310
  54.4 7.0 %collective-permute-start.1 = (bf16[2,256,128]{2,1,0:T(8,128)(2,1)S(1)}, bf16[2,256,128]{2,1,0:T(8,128)(2,1)S(1)}, u32[]{:S(2)}, u32[]{:S(2)}) collective-permute-start(bf16[2,256,128]{2,1,0:T(8,128)(2,1)S(1)} %get-tuple-element.24), channel_id=1, source_target_pairs={{4,0},{8,4},{12,8},{16,12},{20,16},{24,20},{28,24},{32,28},{36,32}... | collective-permute-start | bytes 393224 | tf_op jit(solution)/shard_map/ppermute | solution.py:289
  56.6 7.8 %collective-permute-start = (bf16[2,256,128]{2,1,0:T(8,128)(2,1)S(1)}, bf16[2,256,128]{2,1,0:T(8,128)(2,1)S(1)}, u32[]{:S(2)}, u32[]{:S(2)}) collective-permute-start(bf16[2,256,128]{2,1,0:T(8,128)(2,1)S(1)} %get-tuple-element.25), channel_id=1, source_target_pairs={{0,4},{4,8},{8,12},{12,16},{16,20},{20,24},{24,28},{28,32},{32,36}... | collective-permute-start | bytes 393224 | tf_op jit(solution)/shard_map/ppermute | solution.py:289
  64.3 1.9 %copy-start.6 = (bf16[2,256,128]{2,1,0:T(8,128)(2,1)}, bf16[2,256,128]{2,1,0:T(8,128)(2,1)S(1)}, u32[]{:S(2)}) copy-start(bf16[2,256,128]{2,1,0:T(8,128)(2,1)S(1)} %collective-permute-done.below) | copy-start | bytes 393220
  68.9 0.6 copy-start.12
  69.5 20.8 %all-to-all-start.3 = ((bf16[16,64,128]{2,1,0:T(8,128)(2,1)}), bf16[16,64,128]{2,1,0:T(8,128)(2,1)S(1)}, u32[]{:S(2)}, u32[]{:S(2)}) async-start(bf16[16,64,128]{2,1,0:T(8,128)(2,1)} %get-tuple-element.18), calls=%async_computation.3 | async-start | bytes 524288 | tf_op jit(solution)/shard_map/all_to_all | solution.py:324
  78.6 0.9 copy-start.7
  79.5 0.8 copy-start.13
  84.7 0.8 copy-start
  85.5 0.7 copy-start.8
  86.2 0.7 copy-start.10
  90.3 4.3 %copy-start.11 = (bf16[2,256,128]{2,1,0:T(8,128)(2,1)S(1)}, bf16[2,256,128]{2,1,0:T(8,128)(2,1)}, u32[]{:S(2)}) copy-start(bf16[2,256,128]{2,1,0:T(8,128)(2,1)} %copy-done.10) | copy-start | bytes 393220
  90.3 7.6 %copy-start.9 = (bf16[2,256,128]{2,1,0:T(8,128)(2,1)S(1)}, bf16[2,256,128]{2,1,0:T(8,128)(2,1)}, u32[]{:S(2)}) copy-start(bf16[2,256,128]{2,1,0:T(8,128)(2,1)} %copy-done.8) | copy-start | bytes 393220
  91.0 15.9 %copy-start.1 = (bf16[8,256,128]{2,1,0:T(8,128)(2,1)S(1)}, bf16[8,256,128]{2,1,0:T(8,128)(2,1)}, u32[]{:S(2)}) copy-start(bf16[8,256,128]{2,1,0:T(8,128)(2,1)} %copy-done) | copy-start | bytes 1572868
  91.1 15.9 %all-to-all-start.4 = ((bf16[8,128,128]{2,1,0:T(8,128)(2,1)}), bf16[8,128,128]{2,1,0:T(8,128)(2,1)S(1)}, u32[]{:S(2)}, u32[]{:S(2)}) async-start(bf16[8,128,128]{2,1,0:T(8,128)(2,1)} %merge.1), calls=%async_computation.4 | async-start | bytes 524288 | tf_op jit(solution)/shard_map/all_to_all | solution.py:346
  94.6 10.1 %collective-permute-start.2 = (bf16[2,256,128]{2,1,0:T(8,128)(2,1)S(1)}, bf16[2,256,128]{2,1,0:T(8,128)(2,1)S(1)}, u32[]{:S(2)}, u32[]{:S(2)}) collective-permute-start(bf16[2,256,128]{2,1,0:T(8,128)(2,1)S(1)} %copy-done.11), channel_id=1, source_target_pairs={{0,4},{4,8},{8,12},{12,16},{16,20},{20,24},{24,28},{28,32},{32,36}... | collective-permute-start | bytes 393224 | tf_op jit(solution)/shard_map/ppermute | solution.py:289
  97.9 7.8 %collective-permute-start.3 = (bf16[2,256,128]{2,1,0:T(8,128)(2,1)S(1)}, bf16[2,256,128]{2,1,0:T(8,128)(2,1)S(1)}, u32[]{:S(2)}, u32[]{:S(2)}) collective-permute-start(bf16[2,256,128]{2,1,0:T(8,128)(2,1)S(1)} %copy-done.9), channel_id=1, source_target_pairs={{4,0},{8,4},{12,8},{16,12},{20,16},{24,20},{28,24},{32,28},{36,32}... | collective-permute-start | bytes 393224 | tf_op jit(solution)/shard_map/ppermute | solution.py:289

commit v4 on v3

--- a/solution.py
+++ b/solution.py
@@ -25,7 +25,8 @@
 FEATURES = HEADS * HEAD_DIM
 FACTOR = HEAD_DIM ** (-0.5)
 SHUT = -1e30
-LIMIT = 24 << 20
+PHASE = pl.CostEstimate(flops=60_000_000_000, bytes_accessed=200 << 20, transcendentals=0)
+LIMIT = 6 << 20
 F32 = jnp.float32
 BF16 = jnp.bfloat16
 VMEM = pl.BlockSpec(memory_space=pltpu.VMEM)
@@ -179,7 +180,7 @@
 
 def attend_kernel(
     place, held, below, above, level_one, level_two, stats,
-    answer, fine, grad_below, grad_above, part_one, window, ones,
+    result, grad_below, grad_above, part_one, window, ones,
 ):
     near = 3 * BLOCK
     seen = near + GROUP_ROWS
@@ -201,8 +202,8 @@
             slopes = dot_nt(all_v, cot)
             dscore = (chance * (slopes - stats[unit, 2:3]) * FACTOR).astype(BF16)
             chance = chance.astype(BF16)
-            answer[unit, :BLOCK] = dot_tn(chance, all_v).astype(BF16)
-            answer[unit, BLOCK:] = dot_tn(dscore, all_k).astype(BF16)
+            result[unit, :BLOCK] = dot_tn(chance, all_v).astype(BF16)
+            result[unit, BLOCK : 2 * BLOCK] = dot_tn(dscore, all_k).astype(BF16)
             for kind, (left, right) in enumerate(((dscore, query), (chance, cot))):
                 grad = dot_nn(left[:seen], right)
                 window[head, kind, x * BLOCK : (x + 3) * BLOCK] += grad[:near]
@@ -211,8 +212,10 @@
             rows = slice(kind * BLOCK, (kind + 1) * BLOCK)
             grad_below[head, rows] = window[head, kind, :BLOCK].astype(BF16)
             grad_above[head, rows] = window[head, kind, (N_X + 1) * BLOCK :].astype(BF16)
+            fine = slice((2 + kind) * BLOCK, (3 + kind) * BLOCK)
             for x in range(N_X):
-                fine[x * N_HEAD + head, rows] = window[head, kind, (x + 1) * BLOCK : (x + 2) * BLOCK]
+                own = window[head, kind, (x + 1) * BLOCK : (x + 2) * BLOCK]
+                result[x * N_HEAD + head, fine] = own.astype(BF16)
         both = [ones[head, kind].reshape(N_CTX, ONE_ROWS, HEAD_DIM) for kind in range(2)]
         both = jnp.concatenate(both, axis=1)
         for ctx in range(N_CTX):
@@ -239,23 +242,27 @@
             merged[z, rows] = (part_one[z, rows] + carried).astype(BF16)
 
 
-def finish_kernel(answer, fine, from_below, from_above, arrived, result):
+def edge_kernel(result, from_below, from_above, edged):
+    edged[...] = result[...]
+    for head in range(N_HEAD):
+        for kind in range(2):
+            rows = slice(kind * BLOCK, (kind + 1) * BLOCK)
+            fine = slice((2 + kind) * BLOCK, (3 + kind) * BLOCK)
+            for unit, arrived in ((head, from_below), (N_UNIT - N_HEAD + head, from_above)):
+                grad = result[unit, fine].astype(F32) + arrived[head, rows].astype(F32)
+                edged[unit, fine] = grad.astype(BF16)
+
+
+def finish_kernel(edged, arrived, final):
     owned = jnp.sum(arrived[...].astype(F32), axis=0) * 0.25
     for unit in range(N_UNIT):
-        x, head = unit // N_HEAD, unit % N_HEAD
-        result[unit, : 2 * BLOCK] = answer[unit]
+        final[unit, : 2 * BLOCK] = edged[unit, : 2 * BLOCK]
         for kind in range(2):
-            rows = slice(kind * BLOCK, (kind + 1) * BLOCK)
-            total = fine[unit, rows]
-            if x == 0:
-                total = total + from_below[head, rows].astype(F32)
-            if x == N_X - 1:
-                total = total + from_above[head, rows].astype(F32)
+            fine = slice((2 + kind) * BLOCK, (3 + kind) * BLOCK)
             first = (2 * unit + kind) * ONE_ROWS
             carried = owned[first : first + ONE_ROWS].reshape(ONE_ROWS, 1, HEAD_DIM)
-            total = total.reshape(ONE_ROWS, COARSE, HEAD_DIM) + carried
-            out = slice((2 + kind) * BLOCK, (3 + kind) * BLOCK)
-            result[unit, out] = total.reshape(BLOCK, HEAD_DIM).astype(BF16)
+            total = edged[unit, fine].astype(F32).reshape(ONE_ROWS, COARSE, HEAD_DIM) + carried
+            final[unit, fine] = total.reshape(BLOCK, HEAD_DIM).astype(BF16)
 
 
 def unpack_kernel(packed, output, grad_q, grad_k, grad_v):
@@ -268,7 +275,9 @@
     return jax.ShapeDtypeStruct(shape, dtype)
 
 
-def run(kernel, name, out_shape, *args, scratch=(), place=False, cost=None):
+def run(
+    kernel, name, out_shape, *args, scratch=(), place=False, cost=None, limit=LIMIT
+):
     several = isinstance(out_shape, tuple)
     specs = [SMEM if place and i == 0 else VMEM for i in range(len(args))]
     return pl.pallas_call(
@@ -277,7 +286,7 @@
         in_specs=specs,
         out_specs=(VMEM,) * len(out_shape) if several else VMEM,
         scratch_shapes=list(scratch),
-        compiler_params=pltpu.CompilerParams(vmem_limit_bytes=LIMIT),
+        compiler_params=pltpu.CompilerParams(vmem_limit_bytes=limit),
         cost_estimate=cost,
         name=name,
     )(*args)
@@ -298,23 +307,18 @@
     halo = (N_HEAD, 2 * BLOCK, HEAD_DIM)
     tokens = N_UNIT * BLOCK
 
-    packed = run(pack_kernel, "pack", shape_of(wide, BF16), queries, keys, values, cotangent)
+    packed = run(pack_kernel, "pack", shape_of(wide, BF16), queries, keys, values, cotangent, limit=None)
     held = lax.all_to_all(packed, "x", 0, 0, tiled=True)
 
     spread = run(coarsen_one_kernel, "coarsen_one", shape_of(one, BF16), held)
     level_one = lax.all_to_all(spread, "z", 0, 0, tiled=True)
-    below = shifted(held[-N_HEAD:, PAIR], 1)
-    above = shifted(held[:N_HEAD, PAIR], -1)
-
+    below, above = shifted(held[-N_HEAD:, PAIR], 1), shifted(held[:N_HEAD, PAIR], -1)
     spread = run(coarsen_two_kernel, "coarsen_two", shape_of(two, BF16), level_one)
     level_two = lax.all_to_all(spread, GROUP, 0, 0, tiled=True)
 
     stats_shape = shape_of((N_UNIT, 8, HEAD_DIM), F32)
     near = run(
-        near_kernel, "near_stats", stats_shape, place, held, below, above, level_one, place=True,
-        cost=pl.CostEstimate(
-            flops=4 * tokens * 640 * HEAD_DIM, bytes_accessed=2 << 20, transcendentals=640 * tokens
-        ),
+        near_kernel, "near_stats", stats_shape, place, held, below, above, level_one, place=True, cost=PHASE
     )
     stats, part_two = run(
         two_kernel, "level_two", (stats_shape, shape_of(two, BF16)),
@@ -323,16 +327,10 @@
     )
     arrived_two = lax.all_to_all(part_two, GROUP, 0, 0, tiled=True)
 
-    answer, fine, grad_below, grad_above, part_one = run(
+    result, grad_below, grad_above, part_one = run(
         attend_kernel, "attend",
-        (
-            shape_of((N_UNIT, 2 * BLOCK, HEAD_DIM), BF16),
-            shape_of((N_UNIT, 2 * BLOCK, HEAD_DIM), F32),
-            shape_of(halo, BF16),
-            shape_of(halo, BF16),
-            shape_of(one, F32),
-        ),
-        place, held, below, above, level_one, level_two, stats, place=True,
+        (shape_of(wide, BF16), shape_of(halo, BF16), shape_of(halo, BF16), shape_of(one, F32)),
+        place, held, below, above, level_one, level_two, stats, place=True, limit=2 * LIMIT,
         scratch=[
             pltpu.VMEM((N_HEAD, 2, (N_X + 2) * BLOCK, HEAD_DIM), F32),
             pltpu.VMEM((N_HEAD, 2, GROUP_ROWS, HEAD_DIM), F32),
@@ -342,15 +340,14 @@
         ),
     )
     merged = run(merge_kernel, "merge", shape_of(one, BF16), part_one, arrived_two)
-    merged, grad_below, grad_above = lax.optimization_barrier((merged, grad_below, grad_above))
+    from_above = shifted(grad_below, -1)
     arrived_one = lax.all_to_all(merged, "z", 0, 0, tiled=True)
     from_below = shifted(grad_above, 1)
-    from_above = shifted(grad_below, -1)
-    result = run(
-        finish_kernel, "finish", shape_of(wide, BF16), answer, fine, from_below, from_above, arrived_one
-    )
+    edged = run(edge_kernel, "edge", shape_of(wide, BF16), result, from_below, from_above, cost=PHASE)
+    result = run(finish_kernel, "finish", shape_of(wide, BF16), edged, arrived_one)
     arrived = lax.all_to_all(result, "x", 0, 0, tiled=True)
-    return run(unpack_kernel, "unpack", (shape_of((BLOCK, FEATURES), BF16),) * 4, arrived)
+    outs = (shape_of((BLOCK, FEATURES), BF16),) * 4
+    return run(unpack_kernel, "unpack", outs, arrived)
 
 
 def solution(mesh):

time: 126 us -> 119 us (0.944)
  blocking collectives: 55 us -> 31.9 us
  starting transfers between devices: 35.3 us -> 47.7 us
  waiting for transfers between devices: 13.5 us -> 20.2 us
  local copies, waits for them, and re-layouts: 8.2 us -> 2.21 us
  Pallas kernels: 12.5 us -> 15.5 us
    all_to_all x1 -> x0, blocking collectives: 22.9 us -> none  [local(): level_one = lax.all_to_all(spread, 'z', 0, 0, tiled=True)]
    all_to_all x0 -> x1, starting transfers between devices: none -> 14.5 us  [local(): level_one = lax.all_to_all(spread, 'z', 0, 0, tiled=True)]
    all_to_all x1, waiting for transfers between devices: 0.01 us -> 9.77 us  [local(): level_two = lax.all_to_all(spread, GROUP, 0, 0, tiled=True)]
    ppermute x4, waiting for transfers between devices: 8.85 us -> 0.01 us  [shifted(): lax.ppermute(value, LINE, [(s, s + steps) for s in range(first, last)])]
    all_to_all x1, waiting for transfers between devices: 1.23 us -> 10.1 us  [local(): arrived_one = lax.all_to_all(merged, 'z', 0, 0, tiled=True)]
    unnamed x28 -> x4, local copies, waits for them, and re-layouts: 8.18 us -> 2.19 us
    all_to_all x1, starting transfers between devices: 9.08 us -> 3.43 us  [local(): arrived_two = lax.all_to_all(part_two, GROUP, 0, 0, tiled=True)]
    ppermute x4, starting transfers between devices: 12.1 us -> 15.6 us  [shifted(): lax.ppermute(value, LINE, [(s, s + steps) for s in range(first, last)])]
  transfers between devices with their start and end apart: 7 -> 8, of which waited for: 6 -> 3; matrix products, arithmetic and copies ran while one was open for 0% -> 0% of each run, Pallas kernels for 5% -> 7%
where the time goes in v4:
time: 119 us; the launch traced here: 118 us
  starting transfers between devices  47.7 us (40%)
  blocking collectives  31.9 us (27%)
  waiting for transfers between devices  20.2 us (17%)
  Pallas kernels  15.5 us (13%)
  local copies, waits for them, and re-layouts  2.21 us (2%)
    all_to_all x1, blocking collectives, local(): arrived = lax.all_to_all(result, 'x', 0, 0, tiled=True)  17.3 us
    ppermute x4, starting transfers between devices, shifted(): lax.ppermute(value, LINE, [(s, s + steps) for s in range(first, last)])  15.6 us
    pallas_call x10, Pallas kernels, run(): pl.pallas_call(kernel, out_shape=out_shape, in_specs=specs, out_specs=(VM...  15.5 us
    all_to_all x1, blocking collectives, local(): held = lax.all_to_all(packed, 'x', 0, 0, tiled=True)  14.6 us
    all_to_all x1, starting transfers between devices, local(): level_one = lax.all_to_all(spread, 'z', 0, 0, tiled=True)  14.5 us
    all_to_all x1, starting transfers between devices, local(): level_two = lax.all_to_all(spread, GROUP, 0, 0, tiled=True)  10.8 us
    all_to_all x1, waiting for transfers between devices, local(): arrived_one = lax.all_to_all(merged, 'z', 0, 0, tiled=True)  10.1 us
    all_to_all x1, waiting for transfers between devices, local(): level_two = lax.all_to_all(spread, GROUP, 0, 0, tiled=True)  9.77 us
  transfers between devices with their start and end apart: 8, of which 3 were waited for; matrix products, arithmetic and copies ran while one was open for 0% of the time, Pallas kernels for 7%

profile of v4, /device:TPU:1, one launch (start us, length us, event | category | flops | bytes accessed | tf_op | source)
XLA Modules:
  0.0 118.3 jit_solution(15460214723292821753)
XLA Ops:
  0.6 2.4 %pack.1 = bf16[8,512,128]{2,1,0:T(8,128)(2,1)} custom-call(bf16[128,1024]{1,0:T(8,128)(2,1)} %queries.1, bf16[128,1024]{1,0:T(8,128)(2,1)} %keys.1, bf16[128,1024]{1,0:T(8,128)(2,1)} %values.1, bf16[128,1024]{1,0:T(8,128)(2,1)} %cotangent.1), custom_call_target="tpu_custom_call" | custom-call | tf_op jit(solution)/shard_map/pack/pallas_call | solution.py:283
  3.0 14.6 %all_to_all.30.held = bf16[8,512,128]{2,1,0:T(8,128)(2,1)S(1)} all-to-all(bf16[8,512,128]{2,1,0:T(8,128)(2,1)} %pack.1), channel_id=1, replica_groups=mesh['y'=8,'core'=2,'z'=8,'x'=4] {'x'}, dimensions={0} | all-to-all | bytes 2097152 | tf_op jit(solution)/shard_map/all_to_all | solution.py:311
  17.6 0.9 coarsen_one.1
  18.5 14.5 %all-to-all-start.1 = ((bf16[8,128,128]{2,1,0:T(8,128)(2,1)}), bf16[8,128,128]{2,1,0:T(8,128)(2,1)S(1)}, u32[]{:S(2)}, u32[]{:S(2)}) async-start(bf16[8,128,128]{2,1,0:T(8,128)(2,1)} %coarsen_one.1), calls=%async_computation.1 | async-start | bytes 524288 | tf_op jit(solution)/shard_map/all_to_all | solution.py:314
  33.0 6.9 %collective-permute-start.1 = (bf16[2,256,128]{2,1,0:T(8,128)(2,1)S(1)}, bf16[2,256,128]{2,1,0:T(8,128)(2,1)S(1)}, u32[]{:S(2)}, u32[]{:S(2)}) collective-permute-start(bf16[2,256,128]{2,1,0:T(8,128)(2,1)S(1)} %get-tuple-element.16), channel_id=1, source_target_pairs={{4,0},{8,4},{12,8},{16,12},{20,16},{24,20},{28,24},{32,28},{36,32}... | collective-permute-start | bytes 393224 | tf_op jit(solution)/shard_map/ppermute | solution.py:298
  39.9 1.9 %collective-permute-start = (bf16[2,256,128]{2,1,0:T(8,128)(2,1)S(1)}, bf16[2,256,128]{2,1,0:T(8,128)(2,1)S(1)}, u32[]{:S(2)}, u32[]{:S(2)}) collective-permute-start(bf16[2,256,128]{2,1,0:T(8,128)(2,1)S(1)} %get-tuple-element.17), channel_id=1, source_target_pairs={{0,4},{4,8},{8,12},{12,16},{16,20},{20,24},{24,28},{28,32},{32,36}... | collective-permute-start | bytes 393224 | tf_op jit(solution)/shard_map/ppermute | solution.py:298
  41.8 0.1 pad_add_fusion.place
  41.9 0.4 all-to-all-done.1.level_one
  42.3 0.9 coarsen_two.1
  43.2 10.8 %all-to-all-start.2 = ((bf16[16,64,128]{2,1,0:T(8,128)(2,1)}), bf16[16,64,128]{2,1,0:T(8,128)(2,1)S(1)}, u32[]{:S(2)}, u32[]{:S(2)}) async-start(bf16[16,64,128]{2,1,0:T(8,128)(2,1)} %coarsen_two.1), calls=%async_computation.2 | async-start | bytes 524288 | tf_op jit(solution)/shard_map/all_to_all | solution.py:317
  54.0 0.0 collective-permute-done.1.above
  54.0 0.0 collective-permute-done.below
  54.0 1.9 %near_stats.1.near = f32[8,8,128]{2,1,0:T(8,128)S(1)} custom-call(s32[2]{0:T(128)S(1)} %pad_add_fusion.place, bf16[8,512,128]{2,1,0:T(8,128)(2,1)S(1)} %all_to_all.30.held, bf16[2,256,128]{2,1,0:T(8,128)(2,1)S(1)} %collective-permute-done.below, bf16[2,256,128]{2,1,0:T(8,128)(2,1)S(1)} %collective-permute-done.1.above, ...), custom_call_target="tpu_custom_call" | custom-call | flops 60000002048 | bytes 209715200 | tf_op jit(solution)/shard_map/near_stats/pallas_call | solution.py:283
  55.9 9.8 %all-to-all-done.2.level_two = bf16[16,64,128]{2,1,0:T(8,128)(2,1)S(1)} async-done(((bf16[16,64,128]{2,1,0:T(8,128)(2,1)}), bf16[16,64,128]{2,1,0:T(8,128)(2,1)S(1)}, u32[]{:S(2)}, u32[]{:S(2)}) %all-to-all-start.2) | async-done | bytes 262176 | tf_op jit(solution)/shard_map/all_to_all | solution.py:317
  65.7 2.6 %level_two.1 = (f32[8,8,128]{2,1,0:T(8,128)S(1)}, bf16[16,64,128]{2,1,0:T(8,128)(2,1)}) custom-call(s32[2]{0:T(128)S(1)} %pad_add_fusion.place, bf16[8,512,128]{2,1,0:T(8,128)(2,1)S(1)} %all_to_all.30.held, bf16[16,64,128]{2,1,0:T(8,128)(2,1)S(1)} %all-to-all-done.2.level_two, f32[8,8,128]{2,1,0:T(8,128)S(1)} %near_stats.1.near), custom_call_target="tpu_custom_call" | custom-call | tf_op jit(solution)/shard_map/level_two/pallas_call | solution.py:283
  68.3 3.4 %all-to-all-start.3 = ((bf16[16,64,128]{2,1,0:T(8,128)(2,1)}), bf16[16,64,128]{2,1,0:T(8,128)(2,1)S(1)}, u32[]{:S(2)}, u32[]{:S(2)}) async-start(bf16[16,64,128]{2,1,0:T(8,128)(2,1)} %get-tuple-element.15), calls=%async_computation.3 | async-start | bytes 524288 | tf_op jit(solution)/shard_map/all_to_all | solution.py:328
  71.7 4.5 %attend.1 = (bf16[8,512,128]{2,1,0:T(8,128)(2,1)S(1)}, bf16[2,256,128]{2,1,0:T(8,128)(2,1)S(1)}, bf16[2,256,128]{2,1,0:T(8,128)(2,1)S(1)}, f32[8,128,128]{2,1,0:T(8,128)S(1)}) custom-call(s32[2]{0:T(128)S(1)} %pad_add_fusion.place, bf16[8,512,128]{2,1,0:T(8,128)(2,1)S(1)} %all_to_all.30.held, bf16[2,256,128]{2,1,0:T(8,128)(2,1)S(1)} %collective-permute-done.below, ...), custom_call_target="tpu_custom_call" | custom-call | flops 1409286144 | bytes 4194304 | tf_op jit(solution)/shard_map/attend/pallas_call | solution.py:283
  76.2 0.0 copy-start
  76.2 1.0 copy-done
  77.2 3.3 %collective-permute-start.2 = (bf16[2,256,128]{2,1,0:T(8,128)(2,1)S(1)}, bf16[2,256,128]{2,1,0:T(8,128)(2,1)S(1)}, u32[]{:S(2)}, u32[]{:S(2)}) collective-permute-start(bf16[2,256,128]{2,1,0:T(8,128)(2,1)S(1)} %get-tuple-element.12), channel_id=1, source_target_pairs={{0,4},{4,8},{8,12},{12,16},{16,20},{20,24},{24,28},{28,32},{32,36}... | collective-permute-start | bytes 393224 | tf_op jit(solution)/shard_map/ppermute | solution.py:298
  80.5 3.4 %collective-permute-start.3 = (bf16[2,256,128]{2,1,0:T(8,128)(2,1)S(1)}, bf16[2,256,128]{2,1,0:T(8,128)(2,1)S(1)}, u32[]{:S(2)}, u32[]{:S(2)}) collective-permute-start(bf16[2,256,128]{2,1,0:T(8,128)(2,1)S(1)} %get-tuple-element.13), channel_id=1, source_target_pairs={{4,0},{8,4},{12,8},{16,12},{20,16},{24,20},{28,24},{32,28},{36,32}... | collective-permute-start | bytes 393224 | tf_op jit(solution)/shard_map/ppermute | solution.py:298
  84.0 0.0 all-to-all-done.3.arrived
  84.0 0.8 merge.1
  84.8 3.4 %all-to-all-start.4 = ((bf16[8,128,128]{2,1,0:T(8,128)(2,1)}), bf16[8,128,128]{2,1,0:T(8,128)(2,1)S(1)}, u32[]{:S(2)}, u32[]{:S(2)}) async-start(bf16[8,128,128]{2,1,0:T(8,128)(2,1)} %merge.1), calls=%async_computation.4 | async-start | bytes 524288 | tf_op jit(solution)/shard_map/all_to_all | solution.py:344
  88.2 0.0 collective-permute-done.2.from_below
  88.2 0.0 collective-permute-done.3.from_above
  88.2 0.0 copy-start.1
  88.2 1.2 %copy-done.1 = bf16[8,512,128]{2,1,0:T(8,128)(2,1)S(1)} copy-done((bf16[8,512,128]{2,1,0:T(8,128)(2,1)S(1)}, bf16[8,512,128]{2,1,0:T(8,128)(2,1)}, u32[]{:S(2)}) %copy-start.1) | copy-done | bytes 1048600
  89.4 0.1 edge.1.edged
  89.6 10.1 %all-to-all-done.4.arrived = bf16[8,128,128]{2,1,0:T(8,128)(2,1)S(1)} async-done(((bf16[8,128,128]{2,1,0:T(8,128)(2,1)}), bf16[8,128,128]{2,1,0:T(8,128)(2,1)S(1)}, u32[]{:S(2)}, u32[]{:S(2)}) %all-to-all-start.4) | async-done | bytes 262176 | tf_op jit(solution)/shard_map/all_to_all | solution.py:344
  99.6 0.2 finish.1
  99.8 17.3 %all_to_all.31.packed = bf16[8,512,128]{2,1,0:T(8,128)(2,1)S(1)} all-to-all(bf16[8,512,128]{2,1,0:T(8,128)(2,1)S(1)} %finish.1), channel_id=1, replica_groups=mesh['y'=8,'core'=2,'z'=8,'x'=4] {'x'}, dimensions={0} | all-to-all | bytes 2097152 | tf_op jit(solution)/shard_map/all_to_all | solution.py:348
  117.1 1.3 %unpack.1 = (bf16[128,1024]{1,0:T(8,128)(2,1)}, bf16[128,1024]{1,0:T(8,128)(2,1)}, bf16[128,1024]{1,0:T(8,128)(2,1)}, bf16[128,1024]{1,0:T(8,128)(2,1)}) custom-call(bf16[8,512,128]{2,1,0:T(8,128)(2,1)S(1)} %all_to_all.31.packed), custom_call_target="tpu_custom_call" | custom-call | tf_op jit(solution)/shard_map/unpack/pallas_call | solution.py:283
  (1 shorter events, 0.0 us)
Async XLA Ops:
  18.5 23.8 %all-to-all-start.1 = ((bf16[8,128,128]{2,1,0:T(8,128)(2,1)}), bf16[8,128,128]{2,1,0:T(8,128)(2,1)S(1)}, u32[]{:S(2)}, u32[]{:S(2)}) async-start(bf16[8,128,128]{2,1,0:T(8,128)(2,1)} %coarsen_one.1), calls=%async_computation.1 | async-start | bytes 524288 | tf_op jit(solution)/shard_map/all_to_all | solution.py:314
  33.0 21.1 %collective-permute-start.1 = (bf16[2,256,128]{2,1,0:T(8,128)(2,1)S(1)}, bf16[2,256,128]{2,1,0:T(8,128)(2,1)S(1)}, u32[]{:S(2)}, u32[]{:S(2)}) collective-permute-start(bf16[2,256,128]{2,1,0:T(8,128)(2,1)S(1)} %get-tuple-element.16), channel_id=1, source_target_pairs={{4,0},{8,4},{12,8},{16,12},{20,16},{24,20},{28,24},{32,28},{36,32}... | collective-permute-start | bytes 393224 | tf_op jit(solution)/shard_map/ppermute | solution.py:298
  39.9 14.2 %collective-permute-start = (bf16[2,256,128]{2,1,0:T(8,128)(2,1)S(1)}, bf16[2,256,128]{2,1,0:T(8,128)(2,1)S(1)}, u32[]{:S(2)}, u32[]{:S(2)}) collective-permute-start(bf16[2,256,128]{2,1,0:T(8,128)(2,1)S(1)} %get-tuple-element.17), channel_id=1, source_target_pairs={{0,4},{4,8},{8,12},{12,16},{16,20},{20,24},{24,28},{28,32},{32,36}... | collective-permute-start | bytes 393224 | tf_op jit(solution)/shard_map/ppermute | solution.py:298
  43.2 22.5 %all-to-all-start.2 = ((bf16[16,64,128]{2,1,0:T(8,128)(2,1)}), bf16[16,64,128]{2,1,0:T(8,128)(2,1)S(1)}, u32[]{:S(2)}, u32[]{:S(2)}) async-start(bf16[16,64,128]{2,1,0:T(8,128)(2,1)} %coarsen_two.1), calls=%async_computation.2 | async-start | bytes 524288 | tf_op jit(solution)/shard_map/all_to_all | solution.py:317
  68.3 15.7 %all-to-all-start.3 = ((bf16[16,64,128]{2,1,0:T(8,128)(2,1)}), bf16[16,64,128]{2,1,0:T(8,128)(2,1)S(1)}, u32[]{:S(2)}, u32[]{:S(2)}) async-start(bf16[16,64,128]{2,1,0:T(8,128)(2,1)} %get-tuple-element.15), calls=%async_computation.3 | async-start | bytes 524288 | tf_op jit(solution)/shard_map/all_to_all | solution.py:328
  76.2 1.0 copy-start
  77.2 11.0 %collective-permute-start.2 = (bf16[2,256,128]{2,1,0:T(8,128)(2,1)S(1)}, bf16[2,256,128]{2,1,0:T(8,128)(2,1)S(1)}, u32[]{:S(2)}, u32[]{:S(2)}) collective-permute-start(bf16[2,256,128]{2,1,0:T(8,128)(2,1)S(1)} %get-tuple-element.12), channel_id=1, source_target_pairs={{0,4},{4,8},{8,12},{12,16},{16,20},{20,24},{24,28},{28,32},{32,36}... | collective-permute-start | bytes 393224 | tf_op jit(solution)/shard_map/ppermute | solution.py:298
  80.5 7.7 %collective-permute-start.3 = (bf16[2,256,128]{2,1,0:T(8,128)(2,1)S(1)}, bf16[2,256,128]{2,1,0:T(8,128)(2,1)S(1)}, u32[]{:S(2)}, u32[]{:S(2)}) collective-permute-start(bf16[2,256,128]{2,1,0:T(8,128)(2,1)S(1)} %get-tuple-element.13), channel_id=1, source_target_pairs={{4,0},{8,4},{12,8},{16,12},{20,16},{24,20},{28,24},{32,28},{36,32}... | collective-permute-start | bytes 393224 | tf_op jit(solution)/shard_map/ppermute | solution.py:298
  84.8 14.9 %all-to-all-start.4 = ((bf16[8,128,128]{2,1,0:T(8,128)(2,1)}), bf16[8,128,128]{2,1,0:T(8,128)(2,1)S(1)}, u32[]{:S(2)}, u32[]{:S(2)}) async-start(bf16[8,128,128]{2,1,0:T(8,128)(2,1)} %merge.1), calls=%async_computation.4 | async-start | bytes 524288 | tf_op jit(solution)/shard_map/all_to_all | solution.py:344
  88.2 1.2 %copy-start.1 = (bf16[8,512,128]{2,1,0:T(8,128)(2,1)S(1)}, bf16[8,512,128]{2,1,0:T(8,128)(2,1)}, u32[]{:S(2)}) copy-start(bf16[8,512,128]{2,1,0:T(8,128)(2,1)} %copy-done) | copy-start | bytes 3145732

commit v5 on v4

--- a/solution.py
+++ b/solution.py
@@ -180,7 +180,7 @@
 
 def attend_kernel(
     place, held, below, above, level_one, level_two, stats,
-    result, grad_below, grad_above, part_one, window, ones,
+    result, grad_below, grad_above, part_one, window, ones, total,
 ):
     near = 3 * BLOCK
     seen = near + GROUP_ROWS
@@ -202,8 +202,8 @@
             slopes = dot_nt(all_v, cot)
             dscore = (chance * (slopes - stats[unit, 2:3]) * FACTOR).astype(BF16)
             chance = chance.astype(BF16)
-            result[unit, :BLOCK] = dot_tn(chance, all_v).astype(BF16)
-            result[unit, BLOCK : 2 * BLOCK] = dot_tn(dscore, all_k).astype(BF16)
+            total[unit, :BLOCK] = dot_tn(chance, all_v).astype(BF16)
+            total[unit, BLOCK : 2 * BLOCK] = dot_tn(dscore, all_k).astype(BF16)
             for kind, (left, right) in enumerate(((dscore, query), (chance, cot))):
                 grad = dot_nn(left[:seen], right)
                 window[head, kind, x * BLOCK : (x + 3) * BLOCK] += grad[:near]
@@ -215,12 +215,13 @@
             fine = slice((2 + kind) * BLOCK, (3 + kind) * BLOCK)
             for x in range(N_X):
                 own = window[head, kind, (x + 1) * BLOCK : (x + 2) * BLOCK]
-                result[x * N_HEAD + head, fine] = own.astype(BF16)
+                total[x * N_HEAD + head, fine] = own.astype(BF16)
         both = [ones[head, kind].reshape(N_CTX, ONE_ROWS, HEAD_DIM) for kind in range(2)]
         both = jnp.concatenate(both, axis=1)
         for ctx in range(N_CTX):
             first = ((ctx % N_X) * N_HEAD + head) * 2 * ONE_ROWS
             part_one[ctx // N_X, first : first + 2 * ONE_ROWS] = both[ctx]
+    result[...] = total[...]
 
 
 def merge_kernel(part_one, arrived, merged):
@@ -242,26 +243,27 @@
             merged[z, rows] = (part_one[z, rows] + carried).astype(BF16)
 
 
-def edge_kernel(result, from_below, from_above, edged):
-    edged[...] = result[...]
-    for head in range(N_HEAD):
+def edge_kernel(from_below, from_above, edge):
+    edge[0] = from_below[...]
+    edge[1] = from_above[...]
+
+
+def finish_kernel(result, edge, arrived, final):
+    owned = jnp.sum(arrived[...].astype(F32), axis=0) * 0.25
+    for unit in range(N_UNIT):
+        x, head = unit // N_HEAD, unit % N_HEAD
+        final[unit, : 2 * BLOCK] = result[unit, : 2 * BLOCK]
         for kind in range(2):
             rows = slice(kind * BLOCK, (kind + 1) * BLOCK)
             fine = slice((2 + kind) * BLOCK, (3 + kind) * BLOCK)
-            for unit, arrived in ((head, from_below), (N_UNIT - N_HEAD + head, from_above)):
-                grad = result[unit, fine].astype(F32) + arrived[head, rows].astype(F32)
-                edged[unit, fine] = grad.astype(BF16)
-
-
-def finish_kernel(edged, arrived, final):
-    owned = jnp.sum(arrived[...].astype(F32), axis=0) * 0.25
-    for unit in range(N_UNIT):
-        final[unit, : 2 * BLOCK] = edged[unit, : 2 * BLOCK]
-        for kind in range(2):
-            fine = slice((2 + kind) * BLOCK, (3 + kind) * BLOCK)
+            total = result[unit, fine].astype(F32)
+            if x == 0:
+                total = total + edge[0, head, rows].astype(F32)
+            if x == N_X - 1:
+                total = total + edge[1, head, rows].astype(F32)
             first = (2 * unit + kind) * ONE_ROWS
             carried = owned[first : first + ONE_ROWS].reshape(ONE_ROWS, 1, HEAD_DIM)
-            total = edged[unit, fine].astype(F32).reshape(ONE_ROWS, COARSE, HEAD_DIM) + carried
+            total = total.reshape(ONE_ROWS, COARSE, HEAD_DIM) + carried
             final[unit, fine] = total.reshape(BLOCK, HEAD_DIM).astype(BF16)
 
 
@@ -276,7 +278,7 @@
 
 
 def run(
-    kernel, name, out_shape, *args, scratch=(), place=False, cost=None, limit=LIMIT
+    kernel, name, out_shape, *args, scratch=(), place=False, cost=None, limit=LIMIT, aliases={}
 ):
     several = isinstance(out_shape, tuple)
     specs = [SMEM if place and i == 0 else VMEM for i in range(len(args))]
@@ -288,6 +290,7 @@
         scratch_shapes=list(scratch),
         compiler_params=pltpu.CompilerParams(vmem_limit_bytes=limit),
         cost_estimate=cost,
+        input_output_aliases=aliases,
         name=name,
     )(*args)
 
@@ -334,7 +337,9 @@
         scratch=[
             pltpu.VMEM((N_HEAD, 2, (N_X + 2) * BLOCK, HEAD_DIM), F32),
             pltpu.VMEM((N_HEAD, 2, GROUP_ROWS, HEAD_DIM), F32),
+            pltpu.VMEM(wide, BF16),
         ],
+        aliases={1: 0},
         cost=pl.CostEstimate(
             flops=12 * tokens * 896 * HEAD_DIM, bytes_accessed=4 << 20, transcendentals=896 * tokens
         ),
@@ -343,8 +348,8 @@
     from_above = shifted(grad_below, -1)
     arrived_one = lax.all_to_all(merged, "z", 0, 0, tiled=True)
     from_below = shifted(grad_above, 1)
-    edged = run(edge_kernel, "edge", shape_of(wide, BF16), result, from_below, from_above, cost=PHASE)
-    result = run(finish_kernel, "finish", shape_of(wide, BF16), edged, arrived_one)
+    edge = run(edge_kernel, "edge", shape_of((2,) + halo, BF16), from_below, from_above, cost=PHASE)
+    result = run(finish_kernel, "finish", shape_of(wide, BF16), result, edge, arrived_one)
     arrived = lax.all_to_all(result, "x", 0, 0, tiled=True)
     outs = (shape_of((BLOCK, FEATURES), BF16),) * 4
     return run(unpack_kernel, "unpack", outs, arrived)

time: 119 us -> 119 us (level)
  waiting for transfers between devices: 20.2 us -> 22.4 us
  local copies, waits for them, and re-layouts: 2.21 us -> 0.02 us
    all_to_all x1, waiting for transfers between devices: 10.1 us -> 12.3 us  [local(): arrived_one = lax.all_to_all(merged, 'z', 0, 0, tiled=True)]
    unnamed x4 -> x0, local copies, waits for them, and re-layouts: 2.19 us -> none
where the time goes in v5:
time: 119 us
  starting transfers between devices  47.7 us (40%)
  blocking collectives  31.8 us (27%)
  waiting for transfers between devices  22.4 us (19%)
  Pallas kernels  15.7 us (13%)
    all_to_all x1, blocking collectives, local(): arrived = lax.all_to_all(result, 'x', 0, 0, tiled=True)  17.2 us
    pallas_call x10, Pallas kernels, run(): pl.pallas_call(kernel, out_shape=out_shape, in_specs=specs, out_specs=(VM...  15.7 us
    ppermute x4, starting transfers between devices, shifted(): lax.ppermute(value, LINE, [(s, s + steps) for s in range(first, last)])  15.6 us
    all_to_all x1, blocking collectives, local(): held = lax.all_to_all(packed, 'x', 0, 0, tiled=True)  14.6 us
    all_to_all x1, starting transfers between devices, local(): level_one = lax.all_to_all(spread, 'z', 0, 0, tiled=True)  14.5 us
    all_to_all x1, waiting for transfers between devices, local(): arrived_one = lax.all_to_all(merged, 'z', 0, 0, tiled=True)  12.3 us
    all_to_all x1, starting transfers between devices, local(): level_two = lax.all_to_all(spread, GROUP, 0, 0, tiled=True)  10.8 us
    all_to_all x1, waiting for transfers between devices, local(): level_two = lax.all_to_all(spread, GROUP, 0, 0, tiled=True)  9.77 us
  transfers between devices with their start and end apart: 8, of which 3 were waited for; matrix products, arithmetic and copies ran while one was open for 0% of the time, Pallas kernels for 7%

profile of v5, /device:TPU:1, one launch (start us, length us, event | category | flops | bytes accessed | tf_op | source)
XLA Modules:
  0.0 118.5 jit_solution(2450428904773708353)
XLA Ops:
  0.6 2.4 %pack.1 = bf16[8,512,128]{2,1,0:T(8,128)(2,1)} custom-call(bf16[128,1024]{1,0:T(8,128)(2,1)} %queries.1, bf16[128,1024]{1,0:T(8,128)(2,1)} %keys.1, bf16[128,1024]{1,0:T(8,128)(2,1)} %values.1, bf16[128,1024]{1,0:T(8,128)(2,1)} %cotangent.1), custom_call_target="tpu_custom_call" | custom-call | tf_op jit(solution)/shard_map/pack/pallas_call | solution.py:285
  3.0 14.6 %all_to_all.30.held = bf16[8,512,128]{2,1,0:T(8,128)(2,1)S(1)} all-to-all(bf16[8,512,128]{2,1,0:T(8,128)(2,1)} %pack.1), channel_id=1, replica_groups=mesh['y'=8,'core'=2,'z'=8,'x'=4] {'x'}, dimensions={0} | all-to-all | bytes 2097152 | tf_op jit(solution)/shard_map/all_to_all | solution.py:314
  17.6 0.9 coarsen_one.1
  18.5 14.5 %all-to-all-start.1 = ((bf16[8,128,128]{2,1,0:T(8,128)(2,1)}), bf16[8,128,128]{2,1,0:T(8,128)(2,1)S(1)}, u32[]{:S(2)}, u32[]{:S(2)}) async-start(bf16[8,128,128]{2,1,0:T(8,128)(2,1)} %coarsen_one.1), calls=%async_computation.1 | async-start | bytes 524288 | tf_op jit(solution)/shard_map/all_to_all | solution.py:317
  33.0 6.9 %collective-permute-start.1 = (bf16[2,256,128]{2,1,0:T(8,128)(2,1)S(1)}, bf16[2,256,128]{2,1,0:T(8,128)(2,1)S(1)}, u32[]{:S(2)}, u32[]{:S(2)}) collective-permute-start(bf16[2,256,128]{2,1,0:T(8,128)(2,1)S(1)} %get-tuple-element.16), channel_id=1, source_target_pairs={{4,0},{8,4},{12,8},{16,12},{20,16},{24,20},{28,24},{32,28},{36,32}... | collective-permute-start | bytes 393224 | tf_op jit(solution)/shard_map/ppermute | solution.py:301
  39.9 1.9 %collective-permute-start = (bf16[2,256,128]{2,1,0:T(8,128)(2,1)S(1)}, bf16[2,256,128]{2,1,0:T(8,128)(2,1)S(1)}, u32[]{:S(2)}, u32[]{:S(2)}) collective-permute-start(bf16[2,256,128]{2,1,0:T(8,128)(2,1)S(1)} %get-tuple-element.17), channel_id=1, source_target_pairs={{0,4},{4,8},{8,12},{12,16},{16,20},{20,24},{24,28},{28,32},{32,36}... | collective-permute-start | bytes 393224 | tf_op jit(solution)/shard_map/ppermute | solution.py:301
  41.8 0.1 pad_add_fusion.place
  41.9 0.4 all-to-all-done.1.level_one
  42.3 0.9 coarsen_two.1
  43.2 10.8 %all-to-all-start.2 = ((bf16[16,64,128]{2,1,0:T(8,128)(2,1)}), bf16[16,64,128]{2,1,0:T(8,128)(2,1)S(1)}, u32[]{:S(2)}, u32[]{:S(2)}) async-start(bf16[16,64,128]{2,1,0:T(8,128)(2,1)} %coarsen_two.1), calls=%async_computation.2 | async-start | bytes 524288 | tf_op jit(solution)/shard_map/all_to_all | solution.py:320
  54.0 0.0 collective-permute-done.1.above
  54.0 0.0 collective-permute-done.below
  54.0 1.9 %near_stats.1.near = f32[8,8,128]{2,1,0:T(8,128)S(1)} custom-call(s32[2]{0:T(128)S(1)} %pad_add_fusion.place, bf16[8,512,128]{2,1,0:T(8,128)(2,1)S(1)} %all_to_all.30.held, bf16[2,256,128]{2,1,0:T(8,128)(2,1)S(1)} %collective-permute-done.below, bf16[2,256,128]{2,1,0:T(8,128)(2,1)S(1)} %collective-permute-done.1.above, ...), custom_call_target="tpu_custom_call" | custom-call | flops 60000002048 | bytes 209715200 | tf_op jit(solution)/shard_map/near_stats/pallas_call | solution.py:285
  56.0 9.8 %all-to-all-done.2.level_two = bf16[16,64,128]{2,1,0:T(8,128)(2,1)S(1)} async-done(((bf16[16,64,128]{2,1,0:T(8,128)(2,1)}), bf16[16,64,128]{2,1,0:T(8,128)(2,1)S(1)}, u32[]{:S(2)}, u32[]{:S(2)}) %all-to-all-start.2) | async-done | bytes 262176 | tf_op jit(solution)/shard_map/all_to_all | solution.py:320
  65.7 2.6 %level_two.1 = (f32[8,8,128]{2,1,0:T(8,128)S(1)}, bf16[16,64,128]{2,1,0:T(8,128)(2,1)}) custom-call(s32[2]{0:T(128)S(1)} %pad_add_fusion.place, bf16[8,512,128]{2,1,0:T(8,128)(2,1)S(1)} %all_to_all.30.held, bf16[16,64,128]{2,1,0:T(8,128)(2,1)S(1)} %all-to-all-done.2.level_two, f32[8,8,128]{2,1,0:T(8,128)S(1)} %near_stats.1.near), custom_call_target="tpu_custom_call" | custom-call | tf_op jit(solution)/shard_map/level_two/pallas_call | solution.py:285
  68.3 3.4 %all-to-all-start.3 = ((bf16[16,64,128]{2,1,0:T(8,128)(2,1)}), bf16[16,64,128]{2,1,0:T(8,128)(2,1)S(1)}, u32[]{:S(2)}, u32[]{:S(2)}) async-start(bf16[16,64,128]{2,1,0:T(8,128)(2,1)} %get-tuple-element.15), calls=%async_computation.3 | async-start | bytes 524288 | tf_op jit(solution)/shard_map/all_to_all | solution.py:331
  71.7 4.7 %attend.1 = (bf16[8,512,128]{2,1,0:T(8,128)(2,1)S(1)}, bf16[2,256,128]{2,1,0:T(8,128)(2,1)S(1)}, bf16[2,256,128]{2,1,0:T(8,128)(2,1)S(1)}, f32[8,128,128]{2,1,0:T(8,128)S(1)}) custom-call(s32[2]{0:T(128)S(1)} %pad_add_fusion.place, bf16[8,512,128]{2,1,0:T(8,128)(2,1)S(1)} %all_to_all.30.held, ...), custom_call_target="tpu_custom_call", output_to_operand_aliasing={{0}: (1, {})} | custom-call | flops 1409286144 | bytes 4194304 | tf_op jit(solution)/shard_map/attend/pallas_call | solution.py:285
  76.5 3.3 %collective-permute-start.2 = (bf16[2,256,128]{2,1,0:T(8,128)(2,1)S(1)}, bf16[2,256,128]{2,1,0:T(8,128)(2,1)S(1)}, u32[]{:S(2)}, u32[]{:S(2)}) collective-permute-start(bf16[2,256,128]{2,1,0:T(8,128)(2,1)S(1)} %get-tuple-element.12), channel_id=1, source_target_pairs={{0,4},{4,8},{8,12},{12,16},{16,20},{20,24},{24,28},{28,32},{32,36}... | collective-permute-start | bytes 393224 | tf_op jit(solution)/shard_map/ppermute | solution.py:301
  79.8 3.4 %collective-permute-start.3 = (bf16[2,256,128]{2,1,0:T(8,128)(2,1)S(1)}, bf16[2,256,128]{2,1,0:T(8,128)(2,1)S(1)}, u32[]{:S(2)}, u32[]{:S(2)}) collective-permute-start(bf16[2,256,128]{2,1,0:T(8,128)(2,1)S(1)} %get-tuple-element.13), channel_id=1, source_target_pairs={{4,0},{8,4},{12,8},{16,12},{20,16},{24,20},{28,24},{32,28},{36,32}... | collective-permute-start | bytes 393224 | tf_op jit(solution)/shard_map/ppermute | solution.py:301
  83.3 0.0 all-to-all-done.3.arrived
  83.3 0.8 merge.1
  84.1 3.4 %all-to-all-start.4 = ((bf16[8,128,128]{2,1,0:T(8,128)(2,1)}), bf16[8,128,128]{2,1,0:T(8,128)(2,1)S(1)}, u32[]{:S(2)}, u32[]{:S(2)}) async-start(bf16[8,128,128]{2,1,0:T(8,128)(2,1)} %merge.1), calls=%async_computation.4 | async-start | bytes 524288 | tf_op jit(solution)/shard_map/all_to_all | solution.py:349
  87.5 0.0 collective-permute-done.2.from_below
  87.5 0.0 collective-permute-done.3.from_above
  87.5 12.3 %all-to-all-done.4.arrived = bf16[8,128,128]{2,1,0:T(8,128)(2,1)S(1)} async-done(((bf16[8,128,128]{2,1,0:T(8,128)(2,1)}), bf16[8,128,128]{2,1,0:T(8,128)(2,1)S(1)}, u32[]{:S(2)}, u32[]{:S(2)}) %all-to-all-start.4) | async-done | bytes 262176 | tf_op jit(solution)/shard_map/all_to_all | solution.py:349
  99.8 0.2 finish.1
  100.0 17.2 %all_to_all.31.packed = bf16[8,512,128]{2,1,0:T(8,128)(2,1)S(1)} all-to-all(bf16[8,512,128]{2,1,0:T(8,128)(2,1)S(1)} %finish.1), channel_id=1, replica_groups=mesh['y'=8,'core'=2,'z'=8,'x'=4] {'x'}, dimensions={0} | all-to-all | bytes 2097152 | tf_op jit(solution)/shard_map/all_to_all | solution.py:353
  117.3 1.3 %unpack.1 = (bf16[128,1024]{1,0:T(8,128)(2,1)}, bf16[128,1024]{1,0:T(8,128)(2,1)}, bf16[128,1024]{1,0:T(8,128)(2,1)}, bf16[128,1024]{1,0:T(8,128)(2,1)}) custom-call(bf16[8,512,128]{2,1,0:T(8,128)(2,1)S(1)} %all_to_all.31.packed), custom_call_target="tpu_custom_call" | custom-call | tf_op jit(solution)/shard_map/unpack/pallas_call | solution.py:285
  (2 shorter events, 0.0 us)
Async XLA Ops:
  18.5 23.8 %all-to-all-start.1 = ((bf16[8,128,128]{2,1,0:T(8,128)(2,1)}), bf16[8,128,128]{2,1,0:T(8,128)(2,1)S(1)}, u32[]{:S(2)}, u32[]{:S(2)}) async-start(bf16[8,128,128]{2,1,0:T(8,128)(2,1)} %coarsen_one.1), calls=%async_computation.1 | async-start | bytes 524288 | tf_op jit(solution)/shard_map/all_to_all | solution.py:317
  33.0 21.1 %collective-permute-start.1 = (bf16[2,256,128]{2,1,0:T(8,128)(2,1)S(1)}, bf16[2,256,128]{2,1,0:T(8,128)(2,1)S(1)}, u32[]{:S(2)}, u32[]{:S(2)}) collective-permute-start(bf16[2,256,128]{2,1,0:T(8,128)(2,1)S(1)} %get-tuple-element.16), channel_id=1, source_target_pairs={{4,0},{8,4},{12,8},{16,12},{20,16},{24,20},{28,24},{32,28},{36,32}... | collective-permute-start | bytes 393224 | tf_op jit(solution)/shard_map/ppermute | solution.py:301
  39.9 14.2 %collective-permute-start = (bf16[2,256,128]{2,1,0:T(8,128)(2,1)S(1)}, bf16[2,256,128]{2,1,0:T(8,128)(2,1)S(1)}, u32[]{:S(2)}, u32[]{:S(2)}) collective-permute-start(bf16[2,256,128]{2,1,0:T(8,128)(2,1)S(1)} %get-tuple-element.17), channel_id=1, source_target_pairs={{0,4},{4,8},{8,12},{12,16},{16,20},{20,24},{24,28},{28,32},{32,36}... | collective-permute-start | bytes 393224 | tf_op jit(solution)/shard_map/ppermute | solution.py:301
  43.2 22.5 %all-to-all-start.2 = ((bf16[16,64,128]{2,1,0:T(8,128)(2,1)}), bf16[16,64,128]{2,1,0:T(8,128)(2,1)S(1)}, u32[]{:S(2)}, u32[]{:S(2)}) async-start(bf16[16,64,128]{2,1,0:T(8,128)(2,1)} %coarsen_two.1), calls=%async_computation.2 | async-start | bytes 524288 | tf_op jit(solution)/shard_map/all_to_all | solution.py:320
  68.3 15.0 %all-to-all-start.3 = ((bf16[16,64,128]{2,1,0:T(8,128)(2,1)}), bf16[16,64,128]{2,1,0:T(8,128)(2,1)S(1)}, u32[]{:S(2)}, u32[]{:S(2)}) async-start(bf16[16,64,128]{2,1,0:T(8,128)(2,1)} %get-tuple-element.15), calls=%async_computation.3 | async-start | bytes 524288 | tf_op jit(solution)/shard_map/all_to_all | solution.py:331
  76.5 11.0 %collective-permute-start.2 = (bf16[2,256,128]{2,1,0:T(8,128)(2,1)S(1)}, bf16[2,256,128]{2,1,0:T(8,128)(2,1)S(1)}, u32[]{:S(2)}, u32[]{:S(2)}) collective-permute-start(bf16[2,256,128]{2,1,0:T(8,128)(2,1)S(1)} %get-tuple-element.12), channel_id=1, source_target_pairs={{0,4},{4,8},{8,12},{12,16},{16,20},{20,24},{24,28},{28,32},{32,36}... | collective-permute-start | bytes 393224 | tf_op jit(solution)/shard_map/ppermute | solution.py:301
  79.8 7.7 %collective-permute-start.3 = (bf16[2,256,128]{2,1,0:T(8,128)(2,1)S(1)}, bf16[2,256,128]{2,1,0:T(8,128)(2,1)S(1)}, u32[]{:S(2)}, u32[]{:S(2)}) collective-permute-start(bf16[2,256,128]{2,1,0:T(8,128)(2,1)S(1)} %get-tuple-element.13), channel_id=1, source_target_pairs={{4,0},{8,4},{12,8},{16,12},{20,16},{24,20},{28,24},{32,28},{36,32}... | collective-permute-start | bytes 393224 | tf_op jit(solution)/shard_map/ppermute | solution.py:301
  84.1 15.7 %all-to-all-start.4 = ((bf16[8,128,128]{2,1,0:T(8,128)(2,1)}), bf16[8,128,128]{2,1,0:T(8,128)(2,1)S(1)}, u32[]{:S(2)}, u32[]{:S(2)}) async-start(bf16[8,128,128]{2,1,0:T(8,128)(2,1)} %merge.1), calls=%async_computation.4 | async-start | bytes 524288 | tf_op jit(solution)/shard_map/all_to_all | solution.py:349

commit v6 on v5

--- a/solution.py
+++ b/solution.py
@@ -11,7 +11,7 @@
 BLOCK = 128
 COARSE = 16
 ONE_ROWS = BLOCK // COARSE
-N_Y, N_CORE, N_Z, N_X = 8, 2, 8, 4
+N_Y, N_CORE, N_Z, N_X = 8, 2, 4, 8
 AXES = ("y", "core", "z", "x")
 GROUP = ("y", "core")
 LINE = ("y", "core", "z")

time: 119 us -> 113 us (0.950)
  the two profiles are of different devices: /device:TPU:1 before, /device:TPU:24 now
where the time goes in v6:
time: 113 us; the launch traced here: 112 us
  starting transfers between devices  48.3 us (43%)
  waiting for transfers between devices  30.5 us (27%)
  blocking collectives  17.4 us (15%)
  Pallas kernels  15.4 us (14%)
    all_to_all x1, blocking collectives, local(): arrived = lax.all_to_all(result, 'x', 0, 0, tiled=True)  17.4 us
    pallas_call x10, Pallas kernels, run(): pl.pallas_call(kernel, out_shape=out_shape, in_specs=specs, out_specs=(VM...  15.4 us
    ppermute x4, starting transfers between devices, shifted(): lax.ppermute(value, LINE, [(s, s + steps) for s in range(first, last)])  15.3 us
    all_to_all x1, waiting for transfers between devices, local(): held = lax.all_to_all(packed, 'x', 0, 0, tiled=True)  14.8 us
    all_to_all x1, starting transfers between devices, local(): level_one = lax.all_to_all(spread, 'z', 0, 0, tiled=True)  9.4 us
    all_to_all x1, waiting for transfers between devices, local(): arrived_one = lax.all_to_all(merged, 'z', 0, 0, tiled=True)  9.05 us
    all_to_all x1, starting transfers between devices, local(): level_two = lax.all_to_all(spread, GROUP, 0, 0, tiled=True)  7.34 us
    all_to_all x1, starting transfers between devices, local(): held = lax.all_to_all(packed, 'x', 0, 0, tiled=True)  6.11 us
  transfers between devices with their start and end apart: 9, of which 4 were waited for; matrix products, arithmetic and copies ran while one was open for 0% of the time, Pallas kernels for 7%

profile of v6, /device:TPU:24, one launch (start us, length us, event | category | flops | bytes accessed | tf_op | source)
XLA Modules:
  0.0 112.5 jit_solution(14463204610518894111)
XLA Ops:
  0.6 2.4 %pack.1 = bf16[8,512,128]{2,1,0:T(8,128)(2,1)} custom-call(bf16[128,1024]{1,0:T(8,128)(2,1)} %queries.1, bf16[128,1024]{1,0:T(8,128)(2,1)} %keys.1, bf16[128,1024]{1,0:T(8,128)(2,1)} %values.1, bf16[128,1024]{1,0:T(8,128)(2,1)} %cotangent.1), custom_call_target="tpu_custom_call" | custom-call | tf_op jit(solution)/shard_map/pack/pallas_call | solution.py:285
  3.0 6.1 %all-to-all-start = ((bf16[8,512,128]{2,1,0:T(8,128)(2,1)}), bf16[8,512,128]{2,1,0:T(8,128)(2,1)S(1)}, u32[]{:S(2)}, u32[]{:S(2)}) async-start(bf16[8,512,128]{2,1,0:T(8,128)(2,1)} %pack.1), calls=%async_computation | async-start | bytes 2097152 | tf_op jit(solution)/shard_map/all_to_all | solution.py:314
  9.1 14.8 %all-to-all-done.held = bf16[8,512,128]{2,1,0:T(8,128)(2,1)S(1)} async-done(((bf16[8,512,128]{2,1,0:T(8,128)(2,1)}), bf16[8,512,128]{2,1,0:T(8,128)(2,1)S(1)}, u32[]{:S(2)}, u32[]{:S(2)}) %all-to-all-start) | async-done | bytes 1048608 | tf_op jit(solution)/shard_map/all_to_all | solution.py:314
  23.9 0.8 coarsen_one.1
  24.7 9.4 %all-to-all-start.1 = ((bf16[4,128,128]{2,1,0:T(8,128)(2,1)}), bf16[4,128,128]{2,1,0:T(8,128)(2,1)S(1)}, u32[]{:S(2)}, u32[]{:S(2)}) async-start(bf16[4,128,128]{2,1,0:T(8,128)(2,1)} %coarsen_one.1), calls=%async_computation.1 | async-start | bytes 262144 | tf_op jit(solution)/shard_map/all_to_all | solution.py:317
  34.1 4.6 %collective-permute-start.1 = (bf16[1,256,128]{2,1,0:T(8,128)(2,1)S(1)}, bf16[1,256,128]{2,1,0:T(8,128)(2,1)S(1)}, u32[]{:S(2)}, u32[]{:S(2)}) collective-permute-start(bf16[1,256,128]{2,1,0:T(8,128)(2,1)S(1)} %get-tuple-element.16), channel_id=1, source_target_pairs={{8,0},{16,8},{24,16},{32,24},{40,32},{48,40},{56,48},{64,56},{72,6... | collective-permute-start | bytes 196616 | tf_op jit(solution)/shard_map/ppermute | solution.py:301
  38.8 2.1 %collective-permute-start = (bf16[1,256,128]{2,1,0:T(8,128)(2,1)S(1)}, bf16[1,256,128]{2,1,0:T(8,128)(2,1)S(1)}, u32[]{:S(2)}, u32[]{:S(2)}) collective-permute-start(bf16[1,256,128]{2,1,0:T(8,128)(2,1)S(1)} %get-tuple-element.17), channel_id=1, source_target_pairs={{0,8},{8,16},{16,24},{24,32},{32,40},{40,48},{48,56},{56,64},{64,7... | collective-permute-start | bytes 196616 | tf_op jit(solution)/shard_map/ppermute | solution.py:301
  40.9 0.1 pad_add_fusion.place
  41.0 2.2 %all-to-all-done.1.level_one = bf16[4,128,128]{2,1,0:T(8,128)(2,1)S(1)} async-done(((bf16[4,128,128]{2,1,0:T(8,128)(2,1)}), bf16[4,128,128]{2,1,0:T(8,128)(2,1)S(1)}, u32[]{:S(2)}, u32[]{:S(2)}) %all-to-all-start.1) | async-done | bytes 131104 | tf_op jit(solution)/shard_map/all_to_all | solution.py:317
  43.2 0.8 coarsen_two.1
  44.0 7.3 %all-to-all-start.2 = ((bf16[16,32,128]{2,1,0:T(8,128)(2,1)}), bf16[16,32,128]{2,1,0:T(8,128)(2,1)S(1)}, u32[]{:S(2)}, u32[]{:S(2)}) async-start(bf16[16,32,128]{2,1,0:T(8,128)(2,1)} %coarsen_two.1), calls=%async_computation.2 | async-start | bytes 262144 | tf_op jit(solution)/shard_map/all_to_all | solution.py:320
  51.4 0.0 collective-permute-done.1.above
  51.4 0.0 collective-permute-done.below
  51.4 1.9 %near_stats.1.near = f32[8,8,128]{2,1,0:T(8,128)S(1)} custom-call(s32[2]{0:T(128)S(1)} %pad_add_fusion.place, bf16[8,512,128]{2,1,0:T(8,128)(2,1)S(1)} %all-to-all-done.held, bf16[1,256,128]{2,1,0:T(8,128)(2,1)S(1)} %collective-permute-done.below, bf16[1,256,128]{2,1,0:T(8,128)(2,1)S(1)} %collective-permute-done.1.above, ...), custom_call_target="tpu_custom_call" | custom-call | flops 60000002048 | bytes 209715200 | tf_op jit(solution)/shard_map/near_stats/pallas_call | solution.py:285
  53.3 4.4 %all-to-all-done.2.level_two = bf16[16,32,128]{2,1,0:T(8,128)(2,1)S(1)} async-done(((bf16[16,32,128]{2,1,0:T(8,128)(2,1)}), bf16[16,32,128]{2,1,0:T(8,128)(2,1)S(1)}, u32[]{:S(2)}, u32[]{:S(2)}) %all-to-all-start.2) | async-done | bytes 131104 | tf_op jit(solution)/shard_map/all_to_all | solution.py:320
  57.8 2.6 %level_two.1 = (f32[8,8,128]{2,1,0:T(8,128)S(1)}, bf16[16,32,128]{2,1,0:T(8,128)(2,1)}) custom-call(s32[2]{0:T(128)S(1)} %pad_add_fusion.place, bf16[8,512,128]{2,1,0:T(8,128)(2,1)S(1)} %all-to-all-done.held, bf16[16,32,128]{2,1,0:T(8,128)(2,1)S(1)} %all-to-all-done.2.level_two, f32[8,8,128]{2,1,0:T(8,128)S(1)} %near_stats.1.near), custom_call_target="tpu_custom_call" | custom-call | tf_op jit(solution)/shard_map/level_two/pallas_call | solution.py:285
  60.4 5.8 %all-to-all-start.3 = ((bf16[16,32,128]{2,1,0:T(8,128)(2,1)}), bf16[16,32,128]{2,1,0:T(8,128)(2,1)S(1)}, u32[]{:S(2)}, u32[]{:S(2)}) async-start(bf16[16,32,128]{2,1,0:T(8,128)(2,1)} %get-tuple-element.15), calls=%async_computation.3 | async-start | bytes 262144 | tf_op jit(solution)/shard_map/all_to_all | solution.py:331
  66.1 4.8 %attend.1 = (bf16[8,512,128]{2,1,0:T(8,128)(2,1)S(1)}, bf16[1,256,128]{2,1,0:T(8,128)(2,1)S(1)}, bf16[1,256,128]{2,1,0:T(8,128)(2,1)S(1)}, f32[4,128,128]{2,1,0:T(8,128)S(1)}) custom-call(s32[2]{0:T(128)S(1)} %pad_add_fusion.place, bf16[8,512,128]{2,1,0:T(8,128)(2,1)S(1)} %all-to-all-done.held, ...), custom_call_target="tpu_custom_call", output_to_operand_aliasing={{0}: (1, {})} | custom-call | flops 1409286144 | bytes 4194304 | tf_op jit(solution)/shard_map/attend/pallas_call | solution.py:285
  70.9 3.8 %collective-permute-start.2 = (bf16[1,256,128]{2,1,0:T(8,128)(2,1)S(1)}, bf16[1,256,128]{2,1,0:T(8,128)(2,1)S(1)}, u32[]{:S(2)}, u32[]{:S(2)}) collective-permute-start(bf16[1,256,128]{2,1,0:T(8,128)(2,1)S(1)} %get-tuple-element.12), channel_id=1, source_target_pairs={{0,8},{8,16},{16,24},{24,32},{32,40},{40,48},{48,56},{56,64},{64,7... | collective-permute-start | bytes 196616 | tf_op jit(solution)/shard_map/ppermute | solution.py:301
  74.7 4.8 %collective-permute-start.3 = (bf16[1,256,128]{2,1,0:T(8,128)(2,1)S(1)}, bf16[1,256,128]{2,1,0:T(8,128)(2,1)S(1)}, u32[]{:S(2)}, u32[]{:S(2)}) collective-permute-start(bf16[1,256,128]{2,1,0:T(8,128)(2,1)S(1)} %get-tuple-element.13), channel_id=1, source_target_pairs={{8,0},{16,8},{24,16},{32,24},{40,32},{48,40},{56,48},{64,56},{72,6... | collective-permute-start | bytes 196616 | tf_op jit(solution)/shard_map/ppermute | solution.py:301
  79.5 0.0 all-to-all-done.3.arrived
  79.5 0.7 merge.1
  80.2 4.3 %all-to-all-start.4 = ((bf16[4,128,128]{2,1,0:T(8,128)(2,1)}), bf16[4,128,128]{2,1,0:T(8,128)(2,1)S(1)}, u32[]{:S(2)}, u32[]{:S(2)}) async-start(bf16[4,128,128]{2,1,0:T(8,128)(2,1)} %merge.1), calls=%async_computation.4 | async-start | bytes 262144 | tf_op jit(solution)/shard_map/all_to_all | solution.py:349
  84.6 0.0 collective-permute-done.2.from_below
  84.6 0.0 collective-permute-done.3.from_above
  84.6 9.1 %all-to-all-done.4.arrived = bf16[4,128,128]{2,1,0:T(8,128)(2,1)S(1)} async-done(((bf16[4,128,128]{2,1,0:T(8,128)(2,1)}), bf16[4,128,128]{2,1,0:T(8,128)(2,1)S(1)}, u32[]{:S(2)}, u32[]{:S(2)}) %all-to-all-start.4) | async-done | bytes 131104 | tf_op jit(solution)/shard_map/all_to_all | solution.py:349
  93.6 0.2 finish.1
  93.8 17.4 %all_to_all.30.packed = bf16[8,512,128]{2,1,0:T(8,128)(2,1)S(1)} all-to-all(bf16[8,512,128]{2,1,0:T(8,128)(2,1)S(1)} %finish.1), channel_id=1, replica_groups=mesh['y'=8,'core'=2,'z'=4,'x'=8] {'x'}, dimensions={0} | all-to-all | bytes 2097152 | tf_op jit(solution)/shard_map/all_to_all | solution.py:353
  111.2 1.3 %unpack.1 = (bf16[128,1024]{1,0:T(8,128)(2,1)}, bf16[128,1024]{1,0:T(8,128)(2,1)}, bf16[128,1024]{1,0:T(8,128)(2,1)}, bf16[128,1024]{1,0:T(8,128)(2,1)}) custom-call(bf16[8,512,128]{2,1,0:T(8,128)(2,1)S(1)} %all_to_all.30.packed), custom_call_target="tpu_custom_call" | custom-call | tf_op jit(solution)/shard_map/unpack/pallas_call | solution.py:285
  (2 shorter events, 0.0 us)
Async XLA Ops:
  3.0 20.9 %all-to-all-start = ((bf16[8,512,128]{2,1,0:T(8,128)(2,1)}), bf16[8,512,128]{2,1,0:T(8,128)(2,1)S(1)}, u32[]{:S(2)}, u32[]{:S(2)}) async-start(bf16[8,512,128]{2,1,0:T(8,128)(2,1)} %pack.1), calls=%async_computation | async-start | bytes 2097152 | tf_op jit(solution)/shard_map/all_to_all | solution.py:314
  24.7 18.5 %all-to-all-start.1 = ((bf16[4,128,128]{2,1,0:T(8,128)(2,1)}), bf16[4,128,128]{2,1,0:T(8,128)(2,1)S(1)}, u32[]{:S(2)}, u32[]{:S(2)}) async-start(bf16[4,128,128]{2,1,0:T(8,128)(2,1)} %coarsen_one.1), calls=%async_computation.1 | async-start | bytes 262144 | tf_op jit(solution)/shard_map/all_to_all | solution.py:317
  34.1 17.2 %collective-permute-start.1 = (bf16[1,256,128]{2,1,0:T(8,128)(2,1)S(1)}, bf16[1,256,128]{2,1,0:T(8,128)(2,1)S(1)}, u32[]{:S(2)}, u32[]{:S(2)}) collective-permute-start(bf16[1,256,128]{2,1,0:T(8,128)(2,1)S(1)} %get-tuple-element.16), channel_id=1, source_target_pairs={{8,0},{16,8},{24,16},{32,24},{40,32},{48,40},{56,48},{64,56},{72,6... | collective-permute-start | bytes 196616 | tf_op jit(solution)/shard_map/ppermute | solution.py:301
  38.8 12.6 %collective-permute-start = (bf16[1,256,128]{2,1,0:T(8,128)(2,1)S(1)}, bf16[1,256,128]{2,1,0:T(8,128)(2,1)S(1)}, u32[]{:S(2)}, u32[]{:S(2)}) collective-permute-start(bf16[1,256,128]{2,1,0:T(8,128)(2,1)S(1)} %get-tuple-element.17), channel_id=1, source_target_pairs={{0,8},{8,16},{16,24},{24,32},{32,40},{40,48},{48,56},{56,64},{64,7... | collective-permute-start | bytes 196616 | tf_op jit(solution)/shard_map/ppermute | solution.py:301
  44.0 13.7 %all-to-all-start.2 = ((bf16[16,32,128]{2,1,0:T(8,128)(2,1)}), bf16[16,32,128]{2,1,0:T(8,128)(2,1)S(1)}, u32[]{:S(2)}, u32[]{:S(2)}) async-start(bf16[16,32,128]{2,1,0:T(8,128)(2,1)} %coarsen_two.1), calls=%async_computation.2 | async-start | bytes 262144 | tf_op jit(solution)/shard_map/all_to_all | solution.py:320
  60.4 19.1 %all-to-all-start.3 = ((bf16[16,32,128]{2,1,0:T(8,128)(2,1)}), bf16[16,32,128]{2,1,0:T(8,128)(2,1)S(1)}, u32[]{:S(2)}, u32[]{:S(2)}) async-start(bf16[16,32,128]{2,1,0:T(8,128)(2,1)} %get-tuple-element.15), calls=%async_computation.3 | async-start | bytes 262144 | tf_op jit(solution)/shard_map/all_to_all | solution.py:331
  70.9 13.7 %collective-permute-start.2 = (bf16[1,256,128]{2,1,0:T(8,128)(2,1)S(1)}, bf16[1,256,128]{2,1,0:T(8,128)(2,1)S(1)}, u32[]{:S(2)}, u32[]{:S(2)}) collective-permute-start(bf16[1,256,128]{2,1,0:T(8,128)(2,1)S(1)} %get-tuple-element.12), channel_id=1, source_target_pairs={{0,8},{8,16},{16,24},{24,32},{32,40},{40,48},{48,56},{56,64},{64,7... | collective-permute-start | bytes 196616 | tf_op jit(solution)/shard_map/ppermute | solution.py:301
  74.7 9.8 %collective-permute-start.3 = (bf16[1,256,128]{2,1,0:T(8,128)(2,1)S(1)}, bf16[1,256,128]{2,1,0:T(8,128)(2,1)S(1)}, u32[]{:S(2)}, u32[]{:S(2)}) collective-permute-start(bf16[1,256,128]{2,1,0:T(8,128)(2,1)S(1)} %get-tuple-element.13), channel_id=1, source_target_pairs={{8,0},{16,8},{24,16},{32,24},{40,32},{48,40},{56,48},{64,56},{72,6... | collective-permute-start | bytes 196616 | tf_op jit(solution)/shard_map/ppermute | solution.py:301
  80.2 13.4 %all-to-all-start.4 = ((bf16[4,128,128]{2,1,0:T(8,128)(2,1)}), bf16[4,128,128]{2,1,0:T(8,128)(2,1)S(1)}, u32[]{:S(2)}, u32[]{:S(2)}) async-start(bf16[4,128,128]{2,1,0:T(8,128)(2,1)} %merge.1), calls=%async_computation.4 | async-start | bytes 262144 | tf_op jit(solution)/shard_map/all_to_all | solution.py:349

commit v7 on v6

--- a/solution.py
+++ b/solution.py
@@ -178,49 +178,67 @@
         part_two[:, rows] = jnp.concatenate([grad_k, grad_v], axis=1).astype(BF16)
 
 
-def attend_kernel(
-    place, held, below, above, level_one, level_two, stats,
-    result, grad_below, grad_above, part_one, window, ones, total,
+def grads_kernel(
+    place, held, below, above, level_one, stats,
+    fine, grad_below, grad_above, part_one, window, ones,
 ):
     near = 3 * BLOCK
-    seen = near + GROUP_ROWS
-    shut = two_bias(place)
     for head in range(N_HEAD):
         one_k, one_v = split_one(level_one, head)
-        two_k, two_v = split_two(level_two, head)
         window[head] = jnp.zeros_like(window[head])
         for x in range(N_X):
             unit = x * N_HEAD + head
             query, cot = held[unit, QUERY], held[unit, COT]
-            near_k = near_window(held, below, above, x, head, 0)
-            near_v = near_window(held, below, above, x, head, 1)
-            all_k = jnp.concatenate(near_k + [one_k, two_k], axis=0)
-            all_v = jnp.concatenate(near_v + [one_v, two_v], axis=0)
-            bias = jnp.concatenate(near_bias(place, x) + [shut], axis=0)
+            all_k = jnp.concatenate(near_window(held, below, above, x, head, 0) + [one_k], axis=0)
+            all_v = jnp.concatenate(near_window(held, below, above, x, head, 1) + [one_v], axis=0)
+            bias = jnp.concatenate(near_bias(place, x), axis=0)
             scores = dot_nt(all_k, query) * FACTOR + bias
             chance = jnp.exp(scores - stats[unit, 0:1]) * stats[unit, 1:2]
             slopes = dot_nt(all_v, cot)
             dscore = (chance * (slopes - stats[unit, 2:3]) * FACTOR).astype(BF16)
-            chance = chance.astype(BF16)
-            total[unit, :BLOCK] = dot_tn(chance, all_v).astype(BF16)
-            total[unit, BLOCK : 2 * BLOCK] = dot_tn(dscore, all_k).astype(BF16)
-            for kind, (left, right) in enumerate(((dscore, query), (chance, cot))):
-                grad = dot_nn(left[:seen], right)
+            for kind, (left, right) in enumerate(((dscore, query), (chance.astype(BF16), cot))):
+                grad = dot_nn(left, right)
                 window[head, kind, x * BLOCK : (x + 3) * BLOCK] += grad[:near]
                 ones[head, kind] = grad[near:] if x == 0 else ones[head, kind] + grad[near:]
         for kind in range(2):
             rows = slice(kind * BLOCK, (kind + 1) * BLOCK)
             grad_below[head, rows] = window[head, kind, :BLOCK].astype(BF16)
             grad_above[head, rows] = window[head, kind, (N_X + 1) * BLOCK :].astype(BF16)
-            fine = slice((2 + kind) * BLOCK, (3 + kind) * BLOCK)
             for x in range(N_X):
                 own = window[head, kind, (x + 1) * BLOCK : (x + 2) * BLOCK]
-                total[x * N_HEAD + head, fine] = own.astype(BF16)
+                fine[x * N_HEAD + head, rows] = own.astype(BF16)
         both = [ones[head, kind].reshape(N_CTX, ONE_ROWS, HEAD_DIM) for kind in range(2)]
         both = jnp.concatenate(both, axis=1)
         for ctx in range(N_CTX):
             first = ((ctx % N_X) * N_HEAD + head) * 2 * ONE_ROWS
             part_one[ctx // N_X, first : first + 2 * ONE_ROWS] = both[ctx]
+
+
+def answer_kernel(
+    place, held, below, above, level_one, level_two, stats, fine, from_below, from_above,
+    result, total,
+):
+    shut = two_bias(place)
+    for head in range(N_HEAD):
+        one_k, one_v = split_one(level_one, head)
+        two_k, two_v = split_two(level_two, head)
+        for x in range(N_X):
+            unit = x * N_HEAD + head
+            near_k = near_window(held, below, above, x, head, 0)
+            near_v = near_window(held, below, above, x, head, 1)
+            all_k = jnp.concatenate(near_k + [one_k, two_k], axis=0)
+            all_v = jnp.concatenate(near_v + [one_v, two_v], axis=0)
+            bias = jnp.concatenate(near_bias(place, x) + [shut], axis=0)
+            scores = dot_nt(all_k, held[unit, QUERY]) * FACTOR + bias
+            chance = jnp.exp(scores - stats[unit, 0:1]) * stats[unit, 1:2]
+            slopes = dot_nt(all_v, held[unit, COT])
+            dscore = (chance * (slopes - stats[unit, 2:3]) * FACTOR).astype(BF16)
+            total[unit, :BLOCK] = dot_tn(chance.astype(BF16), all_v).astype(BF16)
+            total[unit, BLOCK : 2 * BLOCK] = dot_tn(dscore, all_k).astype(BF16)
+            total[unit, 2 * BLOCK :] = fine[unit]
+        for unit, arrived in ((head, from_below), (N_UNIT - N_HEAD + head, from_above)):
+            edge = fine[unit].astype(F32) + arrived[head].astype(F32)
+            total[unit, 2 * BLOCK :] = edge.astype(BF16)
     result[...] = total[...]
 
 
@@ -243,24 +261,13 @@
             merged[z, rows] = (part_one[z, rows] + carried).astype(BF16)
 
 
-def edge_kernel(from_below, from_above, edge):
-    edge[0] = from_below[...]
-    edge[1] = from_above[...]
-
-
-def finish_kernel(result, edge, arrived, final):
+def finish_kernel(result, arrived, final):
     owned = jnp.sum(arrived[...].astype(F32), axis=0) * 0.25
     for unit in range(N_UNIT):
-        x, head = unit // N_HEAD, unit % N_HEAD
         final[unit, : 2 * BLOCK] = result[unit, : 2 * BLOCK]
         for kind in range(2):
-            rows = slice(kind * BLOCK, (kind + 1) * BLOCK)
             fine = slice((2 + kind) * BLOCK, (3 + kind) * BLOCK)
             total = result[unit, fine].astype(F32)
-            if x == 0:
-                total = total + edge[0, head, rows].astype(F32)
-            if x == N_X - 1:
-                total = total + edge[1, head, rows].astype(F32)
             first = (2 * unit + kind) * ONE_ROWS
             carried = owned[first : first + ONE_ROWS].reshape(ONE_ROWS, 1, HEAD_DIM)
             total = total.reshape(ONE_ROWS, COARSE, HEAD_DIM) + carried
@@ -330,26 +337,27 @@
     )
     arrived_two = lax.all_to_all(part_two, GROUP, 0, 0, tiled=True)
 
-    result, grad_below, grad_above, part_one = run(
-        attend_kernel, "attend",
-        (shape_of(wide, BF16), shape_of(halo, BF16), shape_of(halo, BF16), shape_of(one, F32)),
-        place, held, below, above, level_one, level_two, stats, place=True, limit=2 * LIMIT,
+    pair = shape_of((N_UNIT, 2 * BLOCK, HEAD_DIM), BF16)
+    fine, grad_below, grad_above, part_one = run(
+        grads_kernel, "grads", (pair, shape_of(halo, BF16), shape_of(halo, BF16), shape_of(one, F32)),
+        place, held, below, above, level_one, stats, place=True, limit=2 * LIMIT,
         scratch=[
             pltpu.VMEM((N_HEAD, 2, (N_X + 2) * BLOCK, HEAD_DIM), F32),
             pltpu.VMEM((N_HEAD, 2, GROUP_ROWS, HEAD_DIM), F32),
-            pltpu.VMEM(wide, BF16),
         ],
-        aliases={1: 0},
         cost=pl.CostEstimate(
-            flops=12 * tokens * 896 * HEAD_DIM, bytes_accessed=4 << 20, transcendentals=896 * tokens
+            flops=8 * tokens * 640 * HEAD_DIM, bytes_accessed=4 << 20, transcendentals=640 * tokens
         ),
     )
+    from_above, from_below = shifted(grad_below, -1), shifted(grad_above, 1)
     merged = run(merge_kernel, "merge", shape_of(one, BF16), part_one, arrived_two)
-    from_above = shifted(grad_below, -1)
     arrived_one = lax.all_to_all(merged, "z", 0, 0, tiled=True)
-    from_below = shifted(grad_above, 1)
-    edge = run(edge_kernel, "edge", shape_of((2,) + halo, BF16), from_below, from_above, cost=PHASE)
-    result = run(finish_kernel, "finish", shape_of(wide, BF16), result, edge, arrived_one)
+    result = run(
+        answer_kernel, "answer", shape_of(wide, BF16),
+        place, held, below, above, level_one, level_two, stats, fine, from_below, from_above,
+        place=True, limit=2 * LIMIT, scratch=[pltpu.VMEM(wide, BF16)], aliases={1: 0}, cost=PHASE,
+    )
+    result = run(finish_kernel, "finish", shape_of(wide, BF16), result, arrived_one)
     arrived = lax.all_to_all(result, "x", 0, 0, tiled=True)
     outs = (shape_of((BLOCK, FEATURES), BF16),) * 4
     return run(unpack_kernel, "unpack", outs, arrived)

time: 113 us -> 111 us (0.982)
  waiting for transfers between devices: 30.5 us -> 26.3 us
  Pallas kernels: 15.4 us -> 17.7 us
    all_to_all x1, waiting for transfers between devices: 9.05 us -> 4.85 us  [local(): arrived_one = lax.all_to_all(merged, 'z', 0, 0, tiled=True)]
    pallas_call x10, Pallas kernels: 15.4 us -> 17.7 us  [run(): pl.pallas_call(kernel, out_shape=out_shape, in_specs=specs, out_specs=(VM...]
  transfers between devices with their start and end apart: 9 -> 9, of which waited for: 4 -> 4; matrix products, arithmetic and copies ran while one was open for 0% -> 0% of each run, Pallas kernels for 7% -> 9%
where the time goes in v7:
time: 111 us; the launch traced here: 110 us
  starting transfers between devices  48.3 us (44%)
  waiting for transfers between devices  26.3 us (24%)
  Pallas kernels  17.7 us (16%)
  blocking collectives  17.4 us (16%)
    pallas_call x10, Pallas kernels, run(): pl.pallas_call(kernel, out_shape=out_shape, in_specs=specs, out_specs=(VM...  17.7 us
    all_to_all x1, blocking collectives, local(): arrived = lax.all_to_all(result, 'x', 0, 0, tiled=True)  17.4 us
    ppermute x4, starting transfers between devices, shifted(): lax.ppermute(value, LINE, [(s, s + steps) for s in range(first, last)])  15.3 us
    all_to_all x1, waiting for transfers between devices, local(): held = lax.all_to_all(packed, 'x', 0, 0, tiled=True)  14.8 us
    all_to_all x1, starting transfers between devices, local(): level_one = lax.all_to_all(spread, 'z', 0, 0, tiled=True)  9.4 us
    all_to_all x1, starting transfers between devices, local(): level_two = lax.all_to_all(spread, GROUP, 0, 0, tiled=True)  7.34 us
    all_to_all x1, starting transfers between devices, local(): held = lax.all_to_all(packed, 'x', 0, 0, tiled=True)  6.11 us
    all_to_all x1, starting transfers between devices, local(): arrived_two = lax.all_to_all(part_two, GROUP, 0, 0, tiled=True)  5.79 us
  transfers between devices with their start and end apart: 9, of which 4 were waited for; matrix products, arithmetic and copies ran while one was open for 0% of the time, Pallas kernels for 9%

profile of v7, /device:TPU:24, one launch (start us, length us, event | category | flops | bytes accessed | tf_op | source)
XLA Modules:
  0.0 110.5 jit_solution(17795424494293188014)
XLA Ops:
  0.6 2.4 %pack.1 = bf16[8,512,128]{2,1,0:T(8,128)(2,1)} custom-call(bf16[128,1024]{1,0:T(8,128)(2,1)} %queries.1, bf16[128,1024]{1,0:T(8,128)(2,1)} %keys.1, bf16[128,1024]{1,0:T(8,128)(2,1)} %values.1, bf16[128,1024]{1,0:T(8,128)(2,1)} %cotangent.1), custom_call_target="tpu_custom_call" | custom-call | tf_op jit(solution)/shard_map/pack/pallas_call | solution.py:292
  3.0 6.1 %all-to-all-start = ((bf16[8,512,128]{2,1,0:T(8,128)(2,1)}), bf16[8,512,128]{2,1,0:T(8,128)(2,1)S(1)}, u32[]{:S(2)}, u32[]{:S(2)}) async-start(bf16[8,512,128]{2,1,0:T(8,128)(2,1)} %pack.1), calls=%async_computation | async-start | bytes 2097152 | tf_op jit(solution)/shard_map/all_to_all | solution.py:321
  9.1 14.8 %all-to-all-done.held = bf16[8,512,128]{2,1,0:T(8,128)(2,1)S(1)} async-done(((bf16[8,512,128]{2,1,0:T(8,128)(2,1)}), bf16[8,512,128]{2,1,0:T(8,128)(2,1)S(1)}, u32[]{:S(2)}, u32[]{:S(2)}) %all-to-all-start) | async-done | bytes 1048608 | tf_op jit(solution)/shard_map/all_to_all | solution.py:321
  23.9 0.8 coarsen_one.1
  24.7 9.4 %all-to-all-start.1 = ((bf16[4,128,128]{2,1,0:T(8,128)(2,1)}), bf16[4,128,128]{2,1,0:T(8,128)(2,1)S(1)}, u32[]{:S(2)}, u32[]{:S(2)}) async-start(bf16[4,128,128]{2,1,0:T(8,128)(2,1)} %coarsen_one.1), calls=%async_computation.1 | async-start | bytes 262144 | tf_op jit(solution)/shard_map/all_to_all | solution.py:324
  34.1 4.6 %collective-permute-start.1 = (bf16[1,256,128]{2,1,0:T(8,128)(2,1)S(1)}, bf16[1,256,128]{2,1,0:T(8,128)(2,1)S(1)}, u32[]{:S(2)}, u32[]{:S(2)}) collective-permute-start(bf16[1,256,128]{2,1,0:T(8,128)(2,1)S(1)} %get-tuple-element.16), channel_id=1, source_target_pairs={{8,0},{16,8},{24,16},{32,24},{40,32},{48,40},{56,48},{64,56},{72,6... | collective-permute-start | bytes 196616 | tf_op jit(solution)/shard_map/ppermute | solution.py:308
  38.8 2.1 %collective-permute-start = (bf16[1,256,128]{2,1,0:T(8,128)(2,1)S(1)}, bf16[1,256,128]{2,1,0:T(8,128)(2,1)S(1)}, u32[]{:S(2)}, u32[]{:S(2)}) collective-permute-start(bf16[1,256,128]{2,1,0:T(8,128)(2,1)S(1)} %get-tuple-element.17), channel_id=1, source_target_pairs={{0,8},{8,16},{16,24},{24,32},{32,40},{40,48},{48,56},{56,64},{64,7... | collective-permute-start | bytes 196616 | tf_op jit(solution)/shard_map/ppermute | solution.py:308
  40.9 0.1 pad_add_fusion.place
  41.0 2.2 %all-to-all-done.1.level_one = bf16[4,128,128]{2,1,0:T(8,128)(2,1)S(1)} async-done(((bf16[4,128,128]{2,1,0:T(8,128)(2,1)}), bf16[4,128,128]{2,1,0:T(8,128)(2,1)S(1)}, u32[]{:S(2)}, u32[]{:S(2)}) %all-to-all-start.1) | async-done | bytes 131104 | tf_op jit(solution)/shard_map/all_to_all | solution.py:324
  43.2 0.8 coarsen_two.1
  44.0 7.3 %all-to-all-start.2 = ((bf16[16,32,128]{2,1,0:T(8,128)(2,1)}), bf16[16,32,128]{2,1,0:T(8,128)(2,1)S(1)}, u32[]{:S(2)}, u32[]{:S(2)}) async-start(bf16[16,32,128]{2,1,0:T(8,128)(2,1)} %coarsen_two.1), calls=%async_computation.2 | async-start | bytes 262144 | tf_op jit(solution)/shard_map/all_to_all | solution.py:327
  51.4 0.0 collective-permute-done.1.above
  51.4 0.0 collective-permute-done.below
  51.4 1.9 %near_stats.1.near = f32[8,8,128]{2,1,0:T(8,128)S(1)} custom-call(s32[2]{0:T(128)S(1)} %pad_add_fusion.place, bf16[8,512,128]{2,1,0:T(8,128)(2,1)S(1)} %all-to-all-done.held, bf16[1,256,128]{2,1,0:T(8,128)(2,1)S(1)} %collective-permute-done.below, bf16[1,256,128]{2,1,0:T(8,128)(2,1)S(1)} %collective-permute-done.1.above, ...), custom_call_target="tpu_custom_call" | custom-call | flops 60000002048 | bytes 209715200 | tf_op jit(solution)/shard_map/near_stats/pallas_call | solution.py:292
  53.3 4.4 %all-to-all-done.2.level_two = bf16[16,32,128]{2,1,0:T(8,128)(2,1)S(1)} async-done(((bf16[16,32,128]{2,1,0:T(8,128)(2,1)}), bf16[16,32,128]{2,1,0:T(8,128)(2,1)S(1)}, u32[]{:S(2)}, u32[]{:S(2)}) %all-to-all-start.2) | async-done | bytes 131104 | tf_op jit(solution)/shard_map/all_to_all | solution.py:327
  57.8 2.6 %level_two.1 = (f32[8,8,128]{2,1,0:T(8,128)S(1)}, bf16[16,32,128]{2,1,0:T(8,128)(2,1)}) custom-call(s32[2]{0:T(128)S(1)} %pad_add_fusion.place, bf16[8,512,128]{2,1,0:T(8,128)(2,1)S(1)} %all-to-all-done.held, bf16[16,32,128]{2,1,0:T(8,128)(2,1)S(1)} %all-to-all-done.2.level_two, f32[8,8,128]{2,1,0:T(8,128)S(1)} %near_stats.1.near), custom_call_target="tpu_custom_call" | custom-call | tf_op jit(solution)/shard_map/level_two/pallas_call | solution.py:292
  60.4 5.8 %all-to-all-start.3 = ((bf16[16,32,128]{2,1,0:T(8,128)(2,1)}), bf16[16,32,128]{2,1,0:T(8,128)(2,1)S(1)}, u32[]{:S(2)}, u32[]{:S(2)}) async-start(bf16[16,32,128]{2,1,0:T(8,128)(2,1)} %get-tuple-element.15), calls=%async_computation.3 | async-start | bytes 262144 | tf_op jit(solution)/shard_map/all_to_all | solution.py:338
  66.1 2.8 %grads.1 = (bf16[8,256,128]{2,1,0:T(8,128)(2,1)S(1)}, bf16[1,256,128]{2,1,0:T(8,128)(2,1)S(1)}, bf16[1,256,128]{2,1,0:T(8,128)(2,1)S(1)}, f32[4,128,128]{2,1,0:T(8,128)S(1)}) custom-call(s32[2]{0:T(128)S(1)} %pad_add_fusion.place, bf16[8,512,128]{2,1,0:T(8,128)(2,1)S(1)} %all-to-all-done.held, bf16[1,256,128]{2,1,0:T(8,128)(2,1)S(1)} %collective-permute-done.below, ...), custom_call_target="tpu_custom_call" | custom-call | flops 671088640 | bytes 4194304 | tf_op jit(solution)/shard_map/grads/pallas_call | solution.py:292
  69.0 3.8 %collective-permute-start.2 = (bf16[1,256,128]{2,1,0:T(8,128)(2,1)S(1)}, bf16[1,256,128]{2,1,0:T(8,128)(2,1)S(1)}, u32[]{:S(2)}, u32[]{:S(2)}) collective-permute-start(bf16[1,256,128]{2,1,0:T(8,128)(2,1)S(1)} %get-tuple-element.12), channel_id=1, source_target_pairs={{0,8},{8,16},{16,24},{24,32},{32,40},{40,48},{48,56},{56,64},{64,7... | collective-permute-start | bytes 196616 | tf_op jit(solution)/shard_map/ppermute | solution.py:308
  72.8 4.8 %collective-permute-start.3 = (bf16[1,256,128]{2,1,0:T(8,128)(2,1)S(1)}, bf16[1,256,128]{2,1,0:T(8,128)(2,1)S(1)}, u32[]{:S(2)}, u32[]{:S(2)}) collective-permute-start(bf16[1,256,128]{2,1,0:T(8,128)(2,1)S(1)} %get-tuple-element.13), channel_id=1, source_target_pairs={{8,0},{16,8},{24,16},{32,24},{40,32},{48,40},{56,48},{64,56},{72,6... | collective-permute-start | bytes 196616 | tf_op jit(solution)/shard_map/ppermute | solution.py:308
  77.5 0.0 all-to-all-done.3.arrived
  77.6 0.7 merge.1
  78.3 4.3 %all-to-all-start.4 = ((bf16[4,128,128]{2,1,0:T(8,128)(2,1)}), bf16[4,128,128]{2,1,0:T(8,128)(2,1)S(1)}, u32[]{:S(2)}, u32[]{:S(2)}) async-start(bf16[4,128,128]{2,1,0:T(8,128)(2,1)} %merge.1), calls=%async_computation.4 | async-start | bytes 262144 | tf_op jit(solution)/shard_map/all_to_all | solution.py:354
  82.6 0.0 collective-permute-done.2.from_below
  82.6 0.0 collective-permute-done.3.from_above
  82.6 4.2 %answer.1.result = bf16[8,512,128]{2,1,0:T(8,128)(2,1)S(1)} custom-call(s32[2]{0:T(128)S(1)} %pad_add_fusion.place, bf16[8,512,128]{2,1,0:T(8,128)(2,1)S(1)} %all-to-all-done.held, bf16[1,256,128]{2,1,0:T(8,128)(2,1)S(1)} %collective-permute-done.below, bf16[1,256,128]{2,1,0:T(8,128)(2,1)S(1)} %collective-permute-done.1.above, ...), custom_call_target="tpu_custom_call", output_to_operand_aliasing={{}: (1, {})} | custom-call | flops 60000002048 | bytes 209715200 | tf_op jit(solution)/shard_map/answer/pallas_call | solution.py:292
  86.8 4.8 %all-to-all-done.4.arrived = bf16[4,128,128]{2,1,0:T(8,128)(2,1)S(1)} async-done(((bf16[4,128,128]{2,1,0:T(8,128)(2,1)}), bf16[4,128,128]{2,1,0:T(8,128)(2,1)S(1)}, u32[]{:S(2)}, u32[]{:S(2)}) %all-to-all-start.4) | async-done | bytes 131104 | tf_op jit(solution)/shard_map/all_to_all | solution.py:354
  91.7 0.2 finish.1
  91.8 17.4 %all_to_all.30.packed = bf16[8,512,128]{2,1,0:T(8,128)(2,1)S(1)} all-to-all(bf16[8,512,128]{2,1,0:T(8,128)(2,1)S(1)} %finish.1), channel_id=1, replica_groups=mesh['y'=8,'core'=2,'z'=4,'x'=8] {'x'}, dimensions={0} | all-to-all | bytes 2097152 | tf_op jit(solution)/shard_map/all_to_all | solution.py:361
  109.2 1.3 %unpack.1 = (bf16[128,1024]{1,0:T(8,128)(2,1)}, bf16[128,1024]{1,0:T(8,128)(2,1)}, bf16[128,1024]{1,0:T(8,128)(2,1)}, bf16[128,1024]{1,0:T(8,128)(2,1)}) custom-call(bf16[8,512,128]{2,1,0:T(8,128)(2,1)S(1)} %all_to_all.30.packed), custom_call_target="tpu_custom_call" | custom-call | tf_op jit(solution)/shard_map/unpack/pallas_call | solution.py:292
  (1 shorter events, 0.0 us)
Async XLA Ops:
  3.0 20.9 %all-to-all-start = ((bf16[8,512,128]{2,1,0:T(8,128)(2,1)}), bf16[8,512,128]{2,1,0:T(8,128)(2,1)S(1)}, u32[]{:S(2)}, u32[]{:S(2)}) async-start(bf16[8,512,128]{2,1,0:T(8,128)(2,1)} %pack.1), calls=%async_computation | async-start | bytes 2097152 | tf_op jit(solution)/shard_map/all_to_all | solution.py:321
  24.7 18.5 %all-to-all-start.1 = ((bf16[4,128,128]{2,1,0:T(8,128)(2,1)}), bf16[4,128,128]{2,1,0:T(8,128)(2,1)S(1)}, u32[]{:S(2)}, u32[]{:S(2)}) async-start(bf16[4,128,128]{2,1,0:T(8,128)(2,1)} %coarsen_one.1), calls=%async_computation.1 | async-start | bytes 262144 | tf_op jit(solution)/shard_map/all_to_all | solution.py:324
  34.1 17.2 %collective-permute-start.1 = (bf16[1,256,128]{2,1,0:T(8,128)(2,1)S(1)}, bf16[1,256,128]{2,1,0:T(8,128)(2,1)S(1)}, u32[]{:S(2)}, u32[]{:S(2)}) collective-permute-start(bf16[1,256,128]{2,1,0:T(8,128)(2,1)S(1)} %get-tuple-element.16), channel_id=1, source_target_pairs={{8,0},{16,8},{24,16},{32,24},{40,32},{48,40},{56,48},{64,56},{72,6... | collective-permute-start | bytes 196616 | tf_op jit(solution)/shard_map/ppermute | solution.py:308
  38.8 12.6 %collective-permute-start = (bf16[1,256,128]{2,1,0:T(8,128)(2,1)S(1)}, bf16[1,256,128]{2,1,0:T(8,128)(2,1)S(1)}, u32[]{:S(2)}, u32[]{:S(2)}) collective-permute-start(bf16[1,256,128]{2,1,0:T(8,128)(2,1)S(1)} %get-tuple-element.17), channel_id=1, source_target_pairs={{0,8},{8,16},{16,24},{24,32},{32,40},{40,48},{48,56},{56,64},{64,7... | collective-permute-start | bytes 196616 | tf_op jit(solution)/shard_map/ppermute | solution.py:308
  44.0 13.7 %all-to-all-start.2 = ((bf16[16,32,128]{2,1,0:T(8,128)(2,1)}), bf16[16,32,128]{2,1,0:T(8,128)(2,1)S(1)}, u32[]{:S(2)}, u32[]{:S(2)}) async-start(bf16[16,32,128]{2,1,0:T(8,128)(2,1)} %coarsen_two.1), calls=%async_computation.2 | async-start | bytes 262144 | tf_op jit(solution)/shard_map/all_to_all | solution.py:327
  60.4 17.2 %all-to-all-start.3 = ((bf16[16,32,128]{2,1,0:T(8,128)(2,1)}), bf16[16,32,128]{2,1,0:T(8,128)(2,1)S(1)}, u32[]{:S(2)}, u32[]{:S(2)}) async-start(bf16[16,32,128]{2,1,0:T(8,128)(2,1)} %get-tuple-element.15), calls=%async_computation.3 | async-start | bytes 262144 | tf_op jit(solution)/shard_map/all_to_all | solution.py:338
  69.0 13.6 %collective-permute-start.2 = (bf16[1,256,128]{2,1,0:T(8,128)(2,1)S(1)}, bf16[1,256,128]{2,1,0:T(8,128)(2,1)S(1)}, u32[]{:S(2)}, u32[]{:S(2)}) collective-permute-start(bf16[1,256,128]{2,1,0:T(8,128)(2,1)S(1)} %get-tuple-element.12), channel_id=1, source_target_pairs={{0,8},{8,16},{16,24},{24,32},{32,40},{40,48},{48,56},{56,64},{64,7... | collective-permute-start | bytes 196616 | tf_op jit(solution)/shard_map/ppermute | solution.py:308
  72.8 9.8 %collective-permute-start.3 = (bf16[1,256,128]{2,1,0:T(8,128)(2,1)S(1)}, bf16[1,256,128]{2,1,0:T(8,128)(2,1)S(1)}, u32[]{:S(2)}, u32[]{:S(2)}) collective-permute-start(bf16[1,256,128]{2,1,0:T(8,128)(2,1)S(1)} %get-tuple-element.13), channel_id=1, source_target_pairs={{8,0},{16,8},{24,16},{32,24},{40,32},{48,40},{56,48},{64,56},{72,6... | collective-permute-start | bytes 196616 | tf_op jit(solution)/shard_map/ppermute | solution.py:308
  78.3 13.4 %all-to-all-start.4 = ((bf16[4,128,128]{2,1,0:T(8,128)(2,1)}), bf16[4,128,128]{2,1,0:T(8,128)(2,1)S(1)}, u32[]{:S(2)}, u32[]{:S(2)}) async-start(bf16[4,128,128]{2,1,0:T(8,128)(2,1)} %merge.1), calls=%async_computation.4 | async-start | bytes 262144 | tf_op jit(solution)/shard_map/all_to_all | solution.py:354

commit v8 on v7

--- a/solution.py
+++ b/solution.py
@@ -328,7 +328,7 @@
 
     stats_shape = shape_of((N_UNIT, 8, HEAD_DIM), F32)
     near = run(
-        near_kernel, "near_stats", stats_shape, place, held, below, above, level_one, place=True, cost=PHASE
+        near_kernel, "near_stats", stats_shape, place, held, below, above, level_one, place=True
     )
     stats, part_two = run(
         two_kernel, "level_two", (stats_shape, shape_of(two, BF16)),

time: 111 us -> 119 us (1.072)
  the two profiles are of different devices: /device:TPU:24 before, /device:TPU:8 now
where the time goes in v8:
time: 119 us
  starting transfers between devices  44.1 us (37%)
  blocking collectives  38.3 us (32%)
  waiting for transfers between devices  17.8 us (15%)
  Pallas kernels  17.6 us (15%)
    all_to_all x1, blocking collectives, local(): held = lax.all_to_all(packed, 'x', 0, 0, tiled=True)  21.9 us
    pallas_call x10, Pallas kernels, run(): pl.pallas_call(kernel, out_shape=out_shape, in_specs=specs, out_specs=(VM...  17.6 us
    all_to_all x1, blocking collectives, local(): arrived = lax.all_to_all(result, 'x', 0, 0, tiled=True)  16.4 us
    ppermute x4, starting transfers between devices, shifted(): lax.ppermute(value, LINE, [(s, s + steps) for s in range(first, last)])  15.3 us
    all_to_all x1, starting transfers between devices, local(): level_one = lax.all_to_all(spread, 'z', 0, 0, tiled=True)  9.4 us
    all_to_all x1, waiting for transfers between devices, local(): level_one = lax.all_to_all(spread, 'z', 0, 0, tiled=True)  8.48 us
    all_to_all x1, starting transfers between devices, local(): arrived_two = lax.all_to_all(part_two, GROUP, 0, 0, tiled=True)  8.37 us
    all_to_all x1, starting transfers between devices, local(): level_two = lax.all_to_all(spread, GROUP, 0, 0, tiled=True)  7.56 us
  transfers between devices with their start and end apart: 8, of which 4 were waited for; matrix products, arithmetic and copies ran while one was open for 0% of the time, Pallas kernels for 8%

profile of v8, /device:TPU:8, one launch (start us, length us, event | category | flops | bytes accessed | tf_op | source)
XLA Modules:
  0.0 118.6 jit_solution(5440682603405551078)
XLA Ops:
  0.6 2.4 %pack.1 = bf16[8,512,128]{2,1,0:T(8,128)(2,1)} custom-call(bf16[128,1024]{1,0:T(8,128)(2,1)} %queries.1, bf16[128,1024]{1,0:T(8,128)(2,1)} %keys.1, bf16[128,1024]{1,0:T(8,128)(2,1)} %values.1, bf16[128,1024]{1,0:T(8,128)(2,1)} %cotangent.1), custom_call_target="tpu_custom_call" | custom-call | tf_op jit(solution)/shard_map/pack/pallas_call | solution.py:292
  3.0 21.9 %all_to_all.30.held = bf16[8,512,128]{2,1,0:T(8,128)(2,1)S(1)} all-to-all(bf16[8,512,128]{2,1,0:T(8,128)(2,1)} %pack.1), channel_id=1, replica_groups=mesh['y'=8,'core'=2,'z'=4,'x'=8] {'x'}, dimensions={0} | all-to-all | bytes 2097152 | tf_op jit(solution)/shard_map/all_to_all | solution.py:321
  24.9 0.8 coarsen_one.1
  25.7 9.4 %all-to-all-start.1 = ((bf16[4,128,128]{2,1,0:T(8,128)(2,1)}), bf16[4,128,128]{2,1,0:T(8,128)(2,1)S(1)}, u32[]{:S(2)}, u32[]{:S(2)}) async-start(bf16[4,128,128]{2,1,0:T(8,128)(2,1)} %coarsen_one.1), calls=%async_computation.1 | async-start | bytes 262144 | tf_op jit(solution)/shard_map/all_to_all | solution.py:324
  35.1 8.5 %all-to-all-done.1.level_one = bf16[4,128,128]{2,1,0:T(8,128)(2,1)S(1)} async-done(((bf16[4,128,128]{2,1,0:T(8,128)(2,1)}), bf16[4,128,128]{2,1,0:T(8,128)(2,1)S(1)}, u32[]{:S(2)}, u32[]{:S(2)}) %all-to-all-start.1) | async-done | bytes 131104 | tf_op jit(solution)/shard_map/all_to_all | solution.py:324
  43.6 0.8 coarsen_two.1
  44.4 7.6 %all-to-all-start.2 = ((bf16[16,32,128]{2,1,0:T(8,128)(2,1)}), bf16[16,32,128]{2,1,0:T(8,128)(2,1)S(1)}, u32[]{:S(2)}, u32[]{:S(2)}) async-start(bf16[16,32,128]{2,1,0:T(8,128)(2,1)} %coarsen_two.1), calls=%async_computation.2 | async-start | bytes 262144 | tf_op jit(solution)/shard_map/all_to_all | solution.py:327
  52.0 2.3 %collective-permute-start.1 = (bf16[1,256,128]{2,1,0:T(8,128)(2,1)S(1)}, bf16[1,256,128]{2,1,0:T(8,128)(2,1)S(1)}, u32[]{:S(2)}, u32[]{:S(2)}) collective-permute-start(bf16[1,256,128]{2,1,0:T(8,128)(2,1)S(1)} %get-tuple-element.16), channel_id=1, source_target_pairs={{8,0},{16,8},{24,16},{32,24},{40,32},{48,40},{56,48},{64,56},{72,6... | collective-permute-start | bytes 196616 | tf_op jit(solution)/shard_map/ppermute | solution.py:308
  54.3 4.5 %collective-permute-start = (bf16[1,256,128]{2,1,0:T(8,128)(2,1)S(1)}, bf16[1,256,128]{2,1,0:T(8,128)(2,1)S(1)}, u32[]{:S(2)}, u32[]{:S(2)}) collective-permute-start(bf16[1,256,128]{2,1,0:T(8,128)(2,1)S(1)} %get-tuple-element.17), channel_id=1, source_target_pairs={{0,8},{8,16},{16,24},{24,32},{32,40},{40,48},{48,56},{56,64},{64,7... | collective-permute-start | bytes 196616 | tf_op jit(solution)/shard_map/ppermute | solution.py:308
  58.8 0.1 pad_add_fusion.place
  58.8 1.5 %collective-permute-done.1.above = bf16[1,256,128]{2,1,0:T(8,128)(2,1)S(1)} collective-permute-done((bf16[1,256,128]{2,1,0:T(8,128)(2,1)S(1)}, bf16[1,256,128]{2,1,0:T(8,128)(2,1)S(1)}, u32[]{:S(2)}, u32[]{:S(2)}) %collective-permute-start.1) | collective-permute-done | bytes 65568 | tf_op jit(solution)/shard_map/ppermute | solution.py:308
  60.3 2.9 %collective-permute-done.below = bf16[1,256,128]{2,1,0:T(8,128)(2,1)S(1)} collective-permute-done((bf16[1,256,128]{2,1,0:T(8,128)(2,1)S(1)}, bf16[1,256,128]{2,1,0:T(8,128)(2,1)S(1)}, u32[]{:S(2)}, u32[]{:S(2)}) %collective-permute-start) | collective-permute-done | bytes 65568 | tf_op jit(solution)/shard_map/ppermute | solution.py:308
  63.2 1.9 %near_stats.1.near = f32[8,8,128]{2,1,0:T(8,128)S(1)} custom-call(s32[2]{0:T(128)S(1)} %pad_add_fusion.place, bf16[8,512,128]{2,1,0:T(8,128)(2,1)S(1)} %all_to_all.30.held, bf16[1,256,128]{2,1,0:T(8,128)(2,1)S(1)} %collective-permute-done.below, bf16[1,256,128]{2,1,0:T(8,128)(2,1)S(1)} %collective-permute-done.1.above, ...), custom_call_target="tpu_custom_call" | custom-call | tf_op jit(solution)/shard_map/near_stats/pallas_call | solution.py:292
  65.2 0.0 all-to-all-done.2.level_two
  65.2 2.6 %level_two.1 = (f32[8,8,128]{2,1,0:T(8,128)S(1)}, bf16[16,32,128]{2,1,0:T(8,128)(2,1)}) custom-call(s32[2]{0:T(128)S(1)} %pad_add_fusion.place, bf16[8,512,128]{2,1,0:T(8,128)(2,1)S(1)} %all_to_all.30.held, bf16[16,32,128]{2,1,0:T(8,128)(2,1)S(1)} %all-to-all-done.2.level_two, f32[8,8,128]{2,1,0:T(8,128)S(1)} %near_stats.1.near), custom_call_target="tpu_custom_call" | custom-call | tf_op jit(solution)/shard_map/level_two/pallas_call | solution.py:292
  67.7 8.4 %all-to-all-start.3 = ((bf16[16,32,128]{2,1,0:T(8,128)(2,1)}), bf16[16,32,128]{2,1,0:T(8,128)(2,1)S(1)}, u32[]{:S(2)}, u32[]{:S(2)}) async-start(bf16[16,32,128]{2,1,0:T(8,128)(2,1)} %get-tuple-element.15), calls=%async_computation.3 | async-start | bytes 262144 | tf_op jit(solution)/shard_map/all_to_all | solution.py:338
  76.1 2.8 %grads.1 = (bf16[8,256,128]{2,1,0:T(8,128)(2,1)S(1)}, bf16[1,256,128]{2,1,0:T(8,128)(2,1)S(1)}, bf16[1,256,128]{2,1,0:T(8,128)(2,1)S(1)}, f32[4,128,128]{2,1,0:T(8,128)S(1)}) custom-call(s32[2]{0:T(128)S(1)} %pad_add_fusion.place, bf16[8,512,128]{2,1,0:T(8,128)(2,1)S(1)} %all_to_all.30.held, bf16[1,256,128]{2,1,0:T(8,128)(2,1)S(1)} %collective-permute-done.below, ...), custom_call_target="tpu_custom_call" | custom-call | flops 671088640 | bytes 4194304 | tf_op jit(solution)/shard_map/grads/pallas_call | solution.py:292
  78.9 2.1 %collective-permute-start.2 = (bf16[1,256,128]{2,1,0:T(8,128)(2,1)S(1)}, bf16[1,256,128]{2,1,0:T(8,128)(2,1)S(1)}, u32[]{:S(2)}, u32[]{:S(2)}) collective-permute-start(bf16[1,256,128]{2,1,0:T(8,128)(2,1)S(1)} %get-tuple-element.12), channel_id=1, source_target_pairs={{0,8},{8,16},{16,24},{24,32},{32,40},{40,48},{48,56},{56,64},{64,7... | collective-permute-start | bytes 196616 | tf_op jit(solution)/shard_map/ppermute | solution.py:308
  81.1 6.4 %collective-permute-start.3 = (bf16[1,256,128]{2,1,0:T(8,128)(2,1)S(1)}, bf16[1,256,128]{2,1,0:T(8,128)(2,1)S(1)}, u32[]{:S(2)}, u32[]{:S(2)}) collective-permute-start(bf16[1,256,128]{2,1,0:T(8,128)(2,1)S(1)} %get-tuple-element.13), channel_id=1, source_target_pairs={{8,0},{16,8},{24,16},{32,24},{40,32},{48,40},{56,48},{64,56},{72,6... | collective-permute-start | bytes 196616 | tf_op jit(solution)/shard_map/ppermute | solution.py:308
  87.5 0.0 all-to-all-done.3.arrived
  87.5 0.7 merge.1
  88.2 3.5 %all-to-all-start.4 = ((bf16[4,128,128]{2,1,0:T(8,128)(2,1)}), bf16[4,128,128]{2,1,0:T(8,128)(2,1)S(1)}, u32[]{:S(2)}, u32[]{:S(2)}) async-start(bf16[4,128,128]{2,1,0:T(8,128)(2,1)} %merge.1), calls=%async_computation.4 | async-start | bytes 262144 | tf_op jit(solution)/shard_map/all_to_all | solution.py:354
  91.7 0.0 collective-permute-done.2.from_below
  91.7 0.0 collective-permute-done.3.from_above
  91.7 4.2 %answer.1.result = bf16[8,512,128]{2,1,0:T(8,128)(2,1)S(1)} custom-call(s32[2]{0:T(128)S(1)} %pad_add_fusion.place, bf16[8,512,128]{2,1,0:T(8,128)(2,1)S(1)} %all_to_all.30.held, bf16[1,256,128]{2,1,0:T(8,128)(2,1)S(1)} %collective-permute-done.below, bf16[1,256,128]{2,1,0:T(8,128)(2,1)S(1)} %collective-permute-done.1.above, ...), custom_call_target="tpu_custom_call", output_to_operand_aliasing={{}: (1, {})} | custom-call | flops 60000002048 | bytes 209715200 | tf_op jit(solution)/shard_map/answer/pallas_call | solution.py:292
  95.9 4.9 %all-to-all-done.4.arrived = bf16[4,128,128]{2,1,0:T(8,128)(2,1)S(1)} async-done(((bf16[4,128,128]{2,1,0:T(8,128)(2,1)}), bf16[4,128,128]{2,1,0:T(8,128)(2,1)S(1)}, u32[]{:S(2)}, u32[]{:S(2)}) %all-to-all-start.4) | async-done | bytes 131104 | tf_op jit(solution)/shard_map/all_to_all | solution.py:354
  100.8 0.2 finish.1
  101.0 16.4 %all_to_all.31.packed = bf16[8,512,128]{2,1,0:T(8,128)(2,1)S(1)} all-to-all(bf16[8,512,128]{2,1,0:T(8,128)(2,1)S(1)} %finish.1), channel_id=1, replica_groups=mesh['y'=8,'core'=2,'z'=4,'x'=8] {'x'}, dimensions={0} | all-to-all | bytes 2097152 | tf_op jit(solution)/shard_map/all_to_all | solution.py:361
  117.4 1.3 %unpack.1 = (bf16[128,1024]{1,0:T(8,128)(2,1)}, bf16[128,1024]{1,0:T(8,128)(2,1)}, bf16[128,1024]{1,0:T(8,128)(2,1)}, bf16[128,1024]{1,0:T(8,128)(2,1)}) custom-call(bf16[8,512,128]{2,1,0:T(8,128)(2,1)S(1)} %all_to_all.31.packed), custom_call_target="tpu_custom_call" | custom-call | tf_op jit(solution)/shard_map/unpack/pallas_call | solution.py:292
  (1 shorter events, 0.0 us)
Async XLA Ops:
  25.7 17.9 %all-to-all-start.1 = ((bf16[4,128,128]{2,1,0:T(8,128)(2,1)}), bf16[4,128,128]{2,1,0:T(8,128)(2,1)S(1)}, u32[]{:S(2)}, u32[]{:S(2)}) async-start(bf16[4,128,128]{2,1,0:T(8,128)(2,1)} %coarsen_one.1), calls=%async_computation.1 | async-start | bytes 262144 | tf_op jit(solution)/shard_map/all_to_all | solution.py:324
  44.4 20.7 %all-to-all-start.2 = ((bf16[16,32,128]{2,1,0:T(8,128)(2,1)}), bf16[16,32,128]{2,1,0:T(8,128)(2,1)S(1)}, u32[]{:S(2)}, u32[]{:S(2)}) async-start(bf16[16,32,128]{2,1,0:T(8,128)(2,1)} %coarsen_two.1), calls=%async_computation.2 | async-start | bytes 262144 | tf_op jit(solution)/shard_map/all_to_all | solution.py:327
  52.0 8.3 %collective-permute-start.1 = (bf16[1,256,128]{2,1,0:T(8,128)(2,1)S(1)}, bf16[1,256,128]{2,1,0:T(8,128)(2,1)S(1)}, u32[]{:S(2)}, u32[]{:S(2)}) collective-permute-start(bf16[1,256,128]{2,1,0:T(8,128)(2,1)S(1)} %get-tuple-element.16), channel_id=1, source_target_pairs={{8,0},{16,8},{24,16},{32,24},{40,32},{48,40},{56,48},{64,56},{72,6... | collective-permute-start | bytes 196616 | tf_op jit(solution)/shard_map/ppermute | solution.py:308
  54.3 8.9 %collective-permute-start = (bf16[1,256,128]{2,1,0:T(8,128)(2,1)S(1)}, bf16[1,256,128]{2,1,0:T(8,128)(2,1)S(1)}, u32[]{:S(2)}, u32[]{:S(2)}) collective-permute-start(bf16[1,256,128]{2,1,0:T(8,128)(2,1)S(1)} %get-tuple-element.17), channel_id=1, source_target_pairs={{0,8},{8,16},{16,24},{24,32},{32,40},{40,48},{48,56},{56,64},{64,7... | collective-permute-start | bytes 196616 | tf_op jit(solution)/shard_map/ppermute | solution.py:308
  67.7 19.8 %all-to-all-start.3 = ((bf16[16,32,128]{2,1,0:T(8,128)(2,1)}), bf16[16,32,128]{2,1,0:T(8,128)(2,1)S(1)}, u32[]{:S(2)}, u32[]{:S(2)}) async-start(bf16[16,32,128]{2,1,0:T(8,128)(2,1)} %get-tuple-element.15), calls=%async_computation.3 | async-start | bytes 262144 | tf_op jit(solution)/shard_map/all_to_all | solution.py:338
  78.9 12.8 %collective-permute-start.2 = (bf16[1,256,128]{2,1,0:T(8,128)(2,1)S(1)}, bf16[1,256,128]{2,1,0:T(8,128)(2,1)S(1)}, u32[]{:S(2)}, u32[]{:S(2)}) collective-permute-start(bf16[1,256,128]{2,1,0:T(8,128)(2,1)S(1)} %get-tuple-element.12), channel_id=1, source_target_pairs={{0,8},{8,16},{16,24},{24,32},{32,40},{40,48},{48,56},{56,64},{64,7... | collective-permute-start | bytes 196616 | tf_op jit(solution)/shard_map/ppermute | solution.py:308
  81.1 10.7 %collective-permute-start.3 = (bf16[1,256,128]{2,1,0:T(8,128)(2,1)S(1)}, bf16[1,256,128]{2,1,0:T(8,128)(2,1)S(1)}, u32[]{:S(2)}, u32[]{:S(2)}) collective-permute-start(bf16[1,256,128]{2,1,0:T(8,128)(2,1)S(1)} %get-tuple-element.13), channel_id=1, source_target_pairs={{8,0},{16,8},{24,16},{32,24},{40,32},{48,40},{56,48},{64,56},{72,6... | collective-permute-start | bytes 196616 | tf_op jit(solution)/shard_map/ppermute | solution.py:308
  88.2 12.6 %all-to-all-start.4 = ((bf16[4,128,128]{2,1,0:T(8,128)(2,1)}), bf16[4,128,128]{2,1,0:T(8,128)(2,1)S(1)}, u32[]{:S(2)}, u32[]{:S(2)}) async-start(bf16[4,128,128]{2,1,0:T(8,128)(2,1)} %merge.1), calls=%async_computation.4 | async-start | bytes 262144 | tf_op jit(solution)/shard_map/all_to_all | solution.py:354
